TPU v7x, 32 devices: a whole 2x2x4 slice. The times are simulated.
32 devices in a mesh: tm: 16 (over z, x, core), tok: 2 (over y).
Axes of the slice: x: 2, y: 2, z: 4, core: 2. Of those that a mesh axis runs over, the one named last changes fastest.
Arguments:
- queries: bfloat16 [32, 256, 1024], P('tm', 'tok'), may hold values from -6 to 6
- keys: bfloat16 [32, 256, 1024], P('tm', 'tok'), may hold values from -6 to 6
- values: bfloat16 [32, 256, 1024], P('tm', 'tok'), may hold values from -6 to 6
- epi_dev: int32 [32, 6], replicated, may hold values from 0 to 15, all different within a row; in each aligned block of 2 rows (0 to 1, 2 to 3, ...) at most 2 rows name the same one
- epi_frame: int32 [32, 6], replicated, may hold values from 0 to 1
- epi_block: int32 [32, 6], replicated, may hold values from 0 to 1
- valid: int32 [32, 6], replicated, may hold values 0 or 1
- ref_local: int32 [4], replicated, may hold values from 0 to 7
Outputs:
- attended: bfloat16 [32, 256, 1024], P('tm', 'tok')
Inputs may be any that keep to these rules, and one draw needn't show every extreme that they name: `epi_dev`: the 6 values of one frame differ. Among the frames of one index of tm (aligned blocks of 2 frames), no value is named by more than 2 entries, a bound that some block reaches.
All inputs are finite; a program needn't handle non-finite values.
Results may differ from a plain program's by a relative error of at most 0.0032.
Values may be sent and summed in bfloat16 or wider, within the bound.
No kernel may reach another device: no remote copies, remote signals or barrier semaphores. Data moves between devices by JAX's collectives and lax.ppermute only.
A program may use at most 128 MiB of HBM per device.

v0:
```python
import math

import jax
import jax.numpy as jnp
from jax import lax
from jax.sharding import PartitionSpec as P

HEADS = 16
HEAD_DIM = 64
BLOCK = 128
FRAMES_DEV = 2
ENTRIES = 6
SPAN = 4


def attend_frame(query_slab, key_set, value_set, live_mask, local_heads):
    row_count = query_slab.shape[0]
    block_rows = math.gcd(row_count, 1024)
    query_blocks = query_slab.reshape(row_count // block_rows, block_rows, local_heads, HEAD_DIM)
    key_heads = key_set.reshape(key_set.shape[0], local_heads, HEAD_DIM)
    value_heads = value_set.reshape(value_set.shape[0], local_heads, HEAD_DIM)
    score_scale = HEAD_DIM ** (-0.5)

    def per_block(query_block):
        scores = (
            jnp.einsum("qhd,khd->hqk", query_block, key_heads, preferred_element_type=jnp.float32)
            * score_scale
        )
        scores = jnp.where(live_mask > 0, scores, -1e30)
        row_max = jnp.max(scores, axis=-1, keepdims=True)
        weights = jnp.exp(scores - row_max) * live_mask
        weight_sum = jnp.sum(weights, axis=-1)
        attended = jnp.einsum(
            "hqk,khd->qhd",
            weights.astype(jnp.bfloat16),
            value_heads,
            preferred_element_type=jnp.float32,
        )
        attended = attended / jnp.transpose(weight_sum)[:, :, None]
        return attended.astype(jnp.bfloat16).reshape(block_rows, local_heads * HEAD_DIM)

    return lax.map(per_block, query_blocks).reshape(row_count, local_heads * HEAD_DIM)


def shards(queries, keys, values, epi_dev, epi_frame, epi_block, valid, ref_local):
    local_heads = HEADS // lax.axis_size("tok")
    head_q, head_k, head_v = (
        lax.all_to_all(queries, "tok", split_axis=2, concat_axis=1, tiled=True),
        lax.all_to_all(keys, "tok", split_axis=2, concat_axis=1, tiled=True),
        lax.all_to_all(values, "tok", split_axis=2, concat_axis=1, tiled=True),
    )
    frame_len = head_q.shape[1]
    slab_width = head_q.shape[2]
    my_index = lax.axis_index("tm")
    group_frames = SPAN * FRAMES_DEV
    first_frame = my_index * FRAMES_DEV
    source = epi_dev * FRAMES_DEV + epi_frame
    my_source = lax.dynamic_slice_in_dim(source, first_frame, FRAMES_DEV, 0)
    my_block = lax.dynamic_slice_in_dim(epi_block, first_frame, FRAMES_DEV, 0)
    my_valid = lax.dynamic_slice_in_dim(valid, first_frame, FRAMES_DEV, 0)
    my_group = my_index // SPAN
    ref_frame = my_group * group_frames + lax.dynamic_index_in_dim(
        ref_local, my_group, 0, keepdims=False
    )

    def collect(carry, piece):
        epi_keys, epi_values, ref_keys, ref_values = carry
        piece_keys, piece_values = piece
        piece_len = piece_keys.shape[0]

        def pick_block(frame_index, block_index):
            offset = frame_index
            inside = (offset >= 0) & (offset < piece_len)
            offset = jnp.clip(offset, 0, piece_len - 1)
            corner = (offset, block_index * BLOCK, 0)
            got_keys = lax.dynamic_slice(piece_keys, corner, (1, BLOCK, slab_width))[0]
            got_values = lax.dynamic_slice(piece_values, corner, (1, BLOCK, slab_width))[0]
            return (inside, got_keys, got_values)

        inside, new_keys, new_values = jax.vmap(jax.vmap(pick_block))(my_source, my_block)
        epi_keys = jnp.where(inside[:, :, None, None], new_keys, epi_keys)
        epi_values = jnp.where(inside[:, :, None, None], new_values, epi_values)
        ref_offset = ref_frame
        ref_inside = (ref_offset >= 0) & (ref_offset < piece_len)
        ref_offset = jnp.clip(ref_offset, 0, piece_len - 1)
        ref_keys = jnp.where(
            ref_inside,
            lax.dynamic_index_in_dim(piece_keys, ref_offset, 0, keepdims=False),
            ref_keys,
        )
        ref_values = jnp.where(
            ref_inside,
            lax.dynamic_index_in_dim(piece_values, ref_offset, 0, keepdims=False),
            ref_values,
        )
        return (epi_keys, epi_values, ref_keys, ref_values)

    epi_empty = jnp.zeros((FRAMES_DEV, ENTRIES, BLOCK, slab_width), jnp.bfloat16)
    ref_empty = jnp.zeros((frame_len, slab_width), jnp.bfloat16)
    epi_keys, epi_values, ref_keys, ref_values = collect(
        (epi_empty, epi_empty, ref_empty, ref_empty),
        (
            lax.all_gather(head_k, "tm", axis=0, tiled=True),
            lax.all_gather(head_v, "tm", axis=0, tiled=True),
        ),
    )
    live_epi = my_valid.astype(jnp.float32)

    def one_frame(packed):
        query_slab, key_slab, value_slab, extra_keys, extra_values, extra_live = packed
        key_set = jnp.concatenate(
            [key_slab, ref_keys, extra_keys.reshape(ENTRIES * BLOCK, slab_width)], 0
        )
        value_set = jnp.concatenate(
            [value_slab, ref_values, extra_values.reshape(ENTRIES * BLOCK, slab_width)], 0
        )
        live_mask = jnp.concatenate(
            [jnp.ones((2 * frame_len,), jnp.float32), jnp.repeat(extra_live, BLOCK)]
        )
        return attend_frame(query_slab, key_set, value_set, live_mask, local_heads)

    attended = lax.map(one_frame, (head_q, head_k, head_v, epi_keys, epi_values, live_epi))
    return lax.all_to_all(attended, "tok", split_axis=1, concat_axis=2, tiled=True)


def solution(mesh):
    return jax.shard_map(
        shards,
        mesh=mesh,
        in_specs=(
            P("tm", "tok", None),
            P("tm", "tok", None),
            P("tm", "tok", None),
            P(),
            P(),
            P(),
            P(),
            P(),
        ),
        out_specs=P("tm", "tok", None),
        check_vma=False,
    )
```

profile of v0, /device:TPU:0, one launch (start us, length us, event | category | flops | bytes accessed | tf_op | source)
XLA Modules:
  0.0 261.2 jit_solution(257590890702119702)
XLA Ops:
  6.5 1.4 copy.46
  7.9 12.0 %all_to_all.72 = bf16[2,128,1024]{1,0,2:T(2,128)(2,1)S(1)} all-to-all(bf16[2,128,1024]{1,0,2:T(2,128)(2,1)S(1)} %copy.46), channel_id=1, replica_groups=mesh['tm'=16,'tok'=2] {'tok'}, dimensions={2} | all-to-all | bytes 1048576 | tf_op jit(solution)/shard_map/all_to_all | solution.py:49
  21.6 9.6 %all_to_all.73 = bf16[2,128,1024]{1,0,2:T(2,128)(2,1)S(1)} all-to-all(bf16[2,128,1024]{1,0,2:T(2,128)(2,1)S(1)} %copy.37), channel_id=1, replica_groups=mesh['tm'=16,'tok'=2] {'tok'}, dimensions={2} | all-to-all | bytes 1048576 | tf_op jit(solution)/shard_map/all_to_all | solution.py:50
  33.5 3.5 %all-to-all-start.1 = ((bf16[2,128,1024]{1,0,2:T(2,128)(2,1)}), bf16[2,128,1024]{1,0,2:T(2,128)(2,1)S(1)}, u32[]{:S(2)}, u32[]{:S(2)}) async-start(bf16[2,128,1024]{1,0,2:T(2,128)(2,1)} %copy.44), calls=%async_computation.1 | async-start | bytes 1048576 | tf_op jit(solution)/shard_map/all_to_all | solution.py:48
  38.9 4.7 %all-to-all-done.1 = bf16[2,128,1024]{1,0,2:T(2,128)(2,1)S(1)} async-done(((bf16[2,128,1024]{1,0,2:T(2,128)(2,1)}), bf16[2,128,1024]{1,0,2:T(2,128)(2,1)S(1)}, u32[]{:S(2)}, u32[]{:S(2)}) %all-to-all-start.1) | async-done | bytes 524320 | tf_op jit(solution)/shard_map/all_to_all | solution.py:48
  45.2 51.3 %all-gather.5.cloned.1.call-done = bf16[32,256,512]{2,1,0:T(8,128)(2,1)} async-done(((bf16[2,256,512]{2,1,0:T(8,128)(2,1)}), bf16[32,256,512]{2,1,0:T(8,128)(2,1)}) %all-gather.5.cloned.1.call-update) | async-done | bytes 8388624 | tf_op jit(solution)/shard_map/all_gather | solution.py:103
  96.5 11.4 %copy.48 = bf16[32,256,512]{2,0,1:T(8,128)(2,1)} copy(bf16[32,256,512]{2,1,0:T(8,128)(2,1)} %all-gather.5.cloned.1.call-done) | data formatting | bytes 16777216 | tf_op jit(solution)/shard_map/all_gather | solution.py:103
  107.9 5.9 %gather_fusion.1 = bf16[12,128,512]{2,0,1:T(8,128)(2,1)S(1)} fusion(bf16[32,256,512]{2,0,1:T(8,128)(2,1)} %copy.48, s32[12]{0:T(128)S(1)} %reshape.37), kind=kCustom, calls=%fused_computation.1 | custom fusion | bytes 3145872 | tf_op jit(solution)/shard_map/vmap(vmap())/gather | solution.py:76
  113.8 2.0 copy.49
  117.0 54.9 %all-gather.3.cloned.1.call-done = bf16[32,256,512]{2,1,0:T(8,128)(2,1)} async-done(((bf16[2,256,512]{2,1,0:T(8,128)(2,1)}), bf16[32,256,512]{2,1,0:T(8,128)(2,1)}) %all-gather.3.cloned.1.call-update) | async-done | bytes 8388624 | tf_op jit(solution)/shard_map/all_gather | solution.py:104
  171.9 11.5 %copy.41 = bf16[32,256,512]{2,0,1:T(8,128)(2,1)} copy(bf16[32,256,512]{2,1,0:T(8,128)(2,1)} %all-gather.3.cloned.1.call-done) | data formatting | bytes 16777216 | tf_op jit(solution)/shard_map/all_gather | solution.py:104
  183.4 5.9 %gather_fusion = bf16[12,128,512]{2,0,1:T(8,128)(2,1)S(1)} fusion(bf16[32,256,512]{2,0,1:T(8,128)(2,1)} %copy.41, s32[12]{0:T(128)S(1)} %reshape.37), kind=kCustom, calls=%fused_computation | custom fusion | bytes 3145872 | tf_op jit(solution)/shard_map/vmap(vmap())/gather | solution.py:77
  189.3 2.1 copy.42
  193.2 3.3 %broadcast_select_fusion = (bf16[2,6,128,512]{3,2,1,0:T(8,128)(2,1)S(1)}, bf16[2,6,128,512]{3,2,1,0:T(8,128)(2,1)}) fusion(bf16[2,6,128,512]{3,2,1,0:T(8,128)(2,1)} %bitcast.74, pred[2,6]{1,0:T(4,128)(4,1)S(1)} %copy.39, bf16[2,6,128,512]{3,2,1,0:T(8,128)(2,1)} %bitcast.75), kind=kLoop, calls=%fused_computation.37 | loop fusion | flops 1572864 | bytes 6291468 | tf_op jit(solution)/shard_map/jit(_where)/select_n | solution.py:81
  196.5 43.7 %while.10 = (s32[]{:T(128)}, bf16[2,256,512]{1,2,0:T(8,128)(2,1)}, bf16[2,256,512]{2,1,0:T(8,128)(2,1)}, bf16[256,512]{0,1:T(8,128)(2,1)}, bf16[2,6,128,512]{3,2...) while((s32[]{:T(128)}, bf16[2,256,512]{1,2,0:T(8,128)(2,1)}, ...), condition=%wide.region_3.4_spmd, body=%wide.region_0.3_spmd.sunk | while | flops 694946304 | bytes 48273368 | solution.py:122
  196.6 1.9 constant_dynamic-slice_fusion.10
  201.3 1.3 constant_dynamic-slice_fusion.11
  206.0 7.1 %fusion.55 = (f32[8,256]{1,0:T(8,128)S(1)}, bf16[8,256,1280]{2,1,0:T(8,128)(2,1)}) fusion(f32[1280]{0:T(1024)S(1)} %concatenate.38, pred[1280]{0:T(1024)(128)(4,1)S(1)} %broadcast_compare_fusion.2, bf16[256,8,64]{0,2,1:T(8,128)(2,1)S(1)} %bitcast.70, bf16[768,8,64]{0,2,1:T(8,128)(2,1)S(1)} %concatenate.39, bf16[256,8,64]{0,2,1:T(8,128)(2,1)} %bitcast.80, ...), kind=kOutput, calls=%fused_computation.51.clone.1 | convolution fusion | flops 355206400 | bytes 6830336 | tf_op jit(solution)/shard_map/while/body/eval_jaxpr/while/body/eval_jaxpr/sub | solution.py:31
  213.1 4.4 %fusion.56 = bf16[256,8,64]{0,2,1:T(8,128)(2,1)S(1)} fusion(bf16[8,256,1280]{2,1,0:T(8,128)(2,1)} %get-tuple-element.207, bf16[768,8,64]{0,2,1:T(8,128)(2,1)S(1)} %concatenate.40, bf16[256,8,64]{0,2,1:T(8,128)(2,1)} %bitcast.66, bf16[256,8,64]{0,2,1:T(8,128)(2,1)S(1)} %bitcast.72, f32[256,8]{0,1:T(8,128)S(1)} %bitcast.81), kind=kOutput, calls=%fused_computation.20.clone.1 | convolution fusion | flops 339738624 | bytes 6823936 | tf_op jit(solution)/shard_map/while/body/eval_jaxpr/while/body/eval_jaxpr/hqk,khd->qhd/dot_general | solution.py:33
  218.5 1.9 constant_dynamic-slice_fusion.10
  227.8 7.1 %fusion.55 = (f32[8,256]{1,0:T(8,128)S(1)}, bf16[8,256,1280]{2,1,0:T(8,128)(2,1)}) fusion(f32[1280]{0:T(1024)S(1)} %concatenate.38, pred[1280]{0:T(1024)(128)(4,1)S(1)} %broadcast_compare_fusion.2, bf16[256,8,64]{0,2,1:T(8,128)(2,1)S(1)} %bitcast.70, bf16[768,8,64]{0,2,1:T(8,128)(2,1)S(1)} %concatenate.39, bf16[256,8,64]{0,2,1:T(8,128)(2,1)} %bitcast.80, ...), kind=kOutput, calls=%fused_computation.51.clone.1 | convolution fusion | flops 355206400 | bytes 6830336 | tf_op jit(solution)/shard_map/while/body/eval_jaxpr/while/body/eval_jaxpr/sub | solution.py:31
  234.9 4.4 %fusion.56 = bf16[256,8,64]{0,2,1:T(8,128)(2,1)S(1)} fusion(bf16[8,256,1280]{2,1,0:T(8,128)(2,1)} %get-tuple-element.207, bf16[768,8,64]{0,2,1:T(8,128)(2,1)S(1)} %concatenate.40, bf16[256,8,64]{0,2,1:T(8,128)(2,1)} %bitcast.66, bf16[256,8,64]{0,2,1:T(8,128)(2,1)S(1)} %bitcast.72, f32[256,8]{0,1:T(8,128)S(1)} %bitcast.81), kind=kOutput, calls=%fused_computation.20.clone.1 | convolution fusion | flops 339738624 | bytes 6823936 | tf_op jit(solution)/shard_map/while/body/eval_jaxpr/while/body/eval_jaxpr/hqk,khd->qhd/dot_general | solution.py:33
  240.2 1.3 copy.56
  241.5 11.1 %all_to_all.74 = bf16[2,256,512]{2,0,1:T(2,128)(2,1)S(1)} all-to-all(bf16[2,256,512]{2,0,1:T(2,128)(2,1)S(1)} %copy.56), channel_id=1, replica_groups=mesh['tm'=16,'tok'=2] {'tok'}, dimensions={1} | all-to-all | bytes 1048576 | tf_op jit(solution)/shard_map/all_to_all | solution.py:123
  (101 shorter events, 26.6 us)
Async XLA Ops:
  6.5 14.6 %copy-start.5 = (bf16[2,128,1024]{2,1,0:T(8,128)(2,1)S(1)}, bf16[2,128,1024]{2,1,0:T(8,128)(2,1)}, u32[]{:S(2)}) copy-start(bf16[2,128,1024]{2,1,0:T(8,128)(2,1)} %param.12) | copy-start | bytes 1572868
  6.5 90.0 %all-gather.5.cloned.1.call-start = ((), (), s32[]{:S(2)}) async-start(), calls=%async_computation.5 | async-start | bytes 8912896 | tf_op jit(solution)/shard_map/all_gather | solution.py:103
  19.9 12.4 %copy-start.6 = (bf16[2,128,1024]{2,1,0:T(8,128)(2,1)S(1)}, bf16[2,128,1024]{2,1,0:T(8,128)(2,1)}, u32[]{:S(2)}) copy-start(bf16[2,128,1024]{2,1,0:T(8,128)(2,1)} %param.10) | copy-start | bytes 1572868
  21.1 150.8 %all-gather.3.cloned.1.call-start = ((), (), s32[]{:S(2)}) async-start(), calls=%async_computation.4 | async-start | bytes 8912896 | tf_op jit(solution)/shard_map/all_gather | solution.py:104
  21.6 15.4 %copy-start.11 = (s32[32,6]{0,1:T(8,128)S(1)}, s32[32,6]{0,1:T(8,128)}, u32[]{:S(2)}) copy-start(s32[32,6]{0,1:T(8,128)} %param.14) | copy-start | bytes 2308
  21.6 15.4 %copy-start.12 = (s32[32,6]{0,1:T(8,128)S(1)}, s32[32,6]{0,1:T(8,128)}, u32[]{:S(2)}) copy-start(s32[32,6]{0,1:T(8,128)} %param.13) | copy-start | bytes 2308
  21.6 15.4 %copy-start.15 = (s32[4]{0:T(128)S(1)}, s32[4]{0:T(128)}, u32[]{:S(2)}) copy-start(s32[4]{0:T(128)} %param.17) | copy-start | bytes 52
  21.6 16.9 %copy-start.13 = (s32[32,6]{0,1:T(8,128)S(1)}, s32[32,6]{0,1:T(8,128)}, u32[]{:S(2)}) copy-start(s32[32,6]{0,1:T(8,128)} %param.15) | copy-start | bytes 2308
  21.6 16.9 %copy-start.14 = (s32[32,6]{0,1:T(8,128)S(1)}, s32[32,6]{0,1:T(8,128)}, u32[]{:S(2)}) copy-start(s32[32,6]{0,1:T(8,128)} %param.16) | copy-start | bytes 2308
  33.5 10.1 %all-to-all-start.1 = ((bf16[2,128,1024]{1,0,2:T(2,128)(2,1)}), bf16[2,128,1024]{1,0,2:T(2,128)(2,1)S(1)}, u32[]{:S(2)}, u32[]{:S(2)}) async-start(bf16[2,128,1024]{1,0,2:T(2,128)(2,1)} %copy.44), calls=%async_computation.1 | async-start | bytes 1048576 | tf_op jit(solution)/shard_map/all_to_all | solution.py:48
  196.5 6.0 %copy-start = (bf16[2,6,128,512]{3,2,1,0:T(8,128)(2,1)}, bf16[2,6,128,512]{3,2,1,0:T(8,128)(2,1)S(1)}, u32[]{:S(2)}) copy-start(bf16[2,6,128,512]{3,2,1,0:T(8,128)(2,1)S(1)} %get-tuple-element.244) | copy-start | bytes 4718596 | tf_op jit(solution)/shard_map/while
  196.5 6.1 %copy-start.9 = (bf16[256,512]{0,1:T(8,128)(2,1)}, bf16[256,512]{0,1:T(8,128)(2,1)S(1)}, u32[]{:S(2)}) copy-start(bf16[256,512]{0,1:T(8,128)(2,1)S(1)} %get-tuple-element.243) | copy-start | bytes 786436 | tf_op jit(solution)/shard_map/while
  204.3 1.7 copy-start.2
  204.3 1.7 copy-start.4
  206.0 7.1 %copy-start.3 = (bf16[1,256,512]{1,2,0:T(8,128)(2,1)S(1)}, bf16[1,256,512]{1,2,0:T(8,128)(2,1)}, u32[]{:S(2)}) copy-start(bf16[1,256,512]{1,2,0:T(8,128)(2,1)} %copy.70) | copy-start | bytes 786436 | tf_op jit(solution)/shard_map/while
  213.1 4.4 %copy-start.7 = (bf16[2,256,512]{1,2,0:T(8,128)(2,1)S(1)}, bf16[2,256,512]{1,2,0:T(8,128)(2,1)}, u32[]{:S(2)}) copy-start(bf16[2,256,512]{1,2,0:T(8,128)(2,1)} %get-tuple-element.224) | copy-start | bytes 1572868 | tf_op jit(solution)/shard_map/while
  213.1 5.3 %copy-start.1 = (bf16[2,6,128,512]{3,2,1,0:T(8,128)(2,1)S(1)}, bf16[2,6,128,512]{3,2,1,0:T(8,128)(2,1)}, u32[]{:S(2)}) copy-start(bf16[2,6,128,512]{3,2,1,0:T(8,128)(2,1)} %copy-done) | copy-start | bytes 4718596 | tf_op jit(solution)/shard_map/while
  213.1 5.3 %copy-start.10 = (bf16[256,512]{0,1:T(8,128)(2,1)S(1)}, bf16[256,512]{0,1:T(8,128)(2,1)}, u32[]{:S(2)}) copy-start(bf16[256,512]{0,1:T(8,128)(2,1)} %copy-done.9) | copy-start | bytes 786436 | tf_op jit(solution)/shard_map/while
  218.4 6.0 %copy-start = (bf16[2,6,128,512]{3,2,1,0:T(8,128)(2,1)}, bf16[2,6,128,512]{3,2,1,0:T(8,128)(2,1)S(1)}, u32[]{:S(2)}) copy-start(bf16[2,6,128,512]{3,2,1,0:T(8,128)(2,1)S(1)} %get-tuple-element.244) | copy-start | bytes 4718596 | tf_op jit(solution)/shard_map/while
  218.4 6.1 %copy-start.9 = (bf16[256,512]{0,1:T(8,128)(2,1)}, bf16[256,512]{0,1:T(8,128)(2,1)S(1)}, u32[]{:S(2)}) copy-start(bf16[256,512]{0,1:T(8,128)(2,1)S(1)} %get-tuple-element.243) | copy-start | bytes 786436 | tf_op jit(solution)/shard_map/while
  227.8 7.1 %copy-start.3 = (bf16[1,256,512]{1,2,0:T(8,128)(2,1)S(1)}, bf16[1,256,512]{1,2,0:T(8,128)(2,1)}, u32[]{:S(2)}) copy-start(bf16[1,256,512]{1,2,0:T(8,128)(2,1)} %copy.70) | copy-start | bytes 786436 | tf_op jit(solution)/shard_map/while
  234.9 4.4 %copy-start.7 = (bf16[2,256,512]{1,2,0:T(8,128)(2,1)S(1)}, bf16[2,256,512]{1,2,0:T(8,128)(2,1)}, u32[]{:S(2)}) copy-start(bf16[2,256,512]{1,2,0:T(8,128)(2,1)} %get-tuple-element.224) | copy-start | bytes 1572868 | tf_op jit(solution)/shard_map/while
  234.9 5.3 %copy-start.1 = (bf16[2,6,128,512]{3,2,1,0:T(8,128)(2,1)S(1)}, bf16[2,6,128,512]{3,2,1,0:T(8,128)(2,1)}, u32[]{:S(2)}) copy-start(bf16[2,6,128,512]{3,2,1,0:T(8,128)(2,1)} %copy-done) | copy-start | bytes 4718596 | tf_op jit(solution)/shard_map/while
  234.9 5.3 %copy-start.10 = (bf16[256,512]{0,1:T(8,128)(2,1)S(1)}, bf16[256,512]{0,1:T(8,128)(2,1)}, u32[]{:S(2)}) copy-start(bf16[256,512]{0,1:T(8,128)(2,1)} %copy-done.9) | copy-start | bytes 786436 | tf_op jit(solution)/shard_map/while
  (4 other events, 5.0 us)
Sparse Core Ops, SparseCore 0:
  21.2 75.2 all-gather.4
  98.7 73.1 all-gather.2
where the time goes:
time: 262 us; the launch traced here: 261 us
  waiting for transfers between devices  111 us (42%)
  local copies, waits for them, and re-layouts  71 us (27%)
  blocking collectives  32.7 us (12%)
  matrix products  23 us (9%)
  between operations  14.2 us (5%)
  other arithmetic  5.45 us (2%)
  starting transfers between devices  3.53 us (1%)
    all_gather x1, waiting for transfers between devices, shards(): lax.all_gather(head_v, 'tm', axis=0, tiled=True)  54.9 us
    all_gather x1, waiting for transfers between devices, shards(): lax.all_gather(head_k, 'tm', axis=0, tiled=True)  51.3 us
    dynamic_slice x14, local copies, waits for them, and re-layouts, shards(): lax.map(one_frame, (head_q, head_k, head_v, epi_keys, epi_values, live_epi))  14.9 us
    sub x2, matrix products, per_block(): weights = jnp.exp(scores - row_max) * live_mask  14.2 us
    all_to_all x1, blocking collectives, shards(): lax.all_to_all(keys, 'tok', split_axis=2, concat_axis=1, tiled=True)  12 us
    all_gather x1, local copies, waits for them, and re-layouts, shards(): lax.all_gather(head_v, 'tm', axis=0, tiled=True)  11.5 us
    all_gather x1, local copies, waits for them, and re-layouts, shards(): lax.all_gather(head_k, 'tm', axis=0, tiled=True)  11.4 us
    all_to_all x1, blocking collectives, shards(): lax.all_to_all(attended, 'tok', split_axis=1, concat_axis=2, tiled=True)  11.1 us
  transfers between devices with their start and end apart: 3, of which 3 were waited for; matrix products, arithmetic and copies ran while one was open for 9% of the time, Pallas kernels for 0%

commit v1 on v0

v1 whole, which is shorter than its diff:
```python
import functools
import math

import jax
import jax.numpy as jnp
from jax import lax
from jax.experimental import pallas as pl
from jax.experimental.pallas import tpu as pltpu
from jax.sharding import PartitionSpec as P

HEADS = 16
HEAD_DIM = 64
BLOCK = 128
FRAMES_DEV = 2
ENTRIES = 6
SPAN = 4


def attend_kernel(
    table_ref, q_ref, pool_ref, out_ref, key_set, value_set, sems, *, inner, n_tok, n_frames
):
    step = pl.program_id(0)
    count = pl.num_programs(0)
    entry_len = n_frames * ENTRIES
    n_blocks = 2 * n_tok + ENTRIES
    outer_index = table_ref[4 * entry_len + n_frames // (SPAN * FRAMES_DEV)]

    def block_place(frame, block):
        ref_block = block - n_tok
        entry = frame * ENTRIES + jnp.maximum(block - 2 * n_tok, 0)
        group = frame // (SPAN * FRAMES_DEV)
        ref_frame = group * (SPAN * FRAMES_DEV) + table_ref[4 * entry_len + group]
        is_own, is_ref = block < n_tok, block < 2 * n_tok
        dev = jnp.where(
            is_own,
            frame // FRAMES_DEV,
            jnp.where(is_ref, ref_frame // FRAMES_DEV, table_ref[entry]),
        )
        place = jnp.where(
            is_own,
            frame % FRAMES_DEV,
            jnp.where(is_ref, ref_frame % FRAMES_DEV, table_ref[entry_len + entry]),
        )
        token_block = jnp.where(
            is_own, block, jnp.where(is_ref, ref_block, table_ref[2 * entry_len + entry])
        )
        return dev // inner, (dev % inner) * n_tok + token_block, place

    def copies(slot, block, source):
        outer, row, place = source
        return (
            pltpu.make_async_copy(
                pool_ref.at[outer, row, place, 0],
                key_set.at[slot, pl.ds(block * BLOCK, BLOCK)],
                sems.at[slot, block, 0],
            ),
            pltpu.make_async_copy(
                pool_ref.at[outer, row, place, 1],
                value_set.at[slot, pl.ds(block * BLOCK, BLOCK)],
                sems.at[slot, block, 1],
            ),
        )

    def fetch(local, slot):
        frame = outer_index * (inner * FRAMES_DEV) + local

        @pl.loop(0, n_blocks)
        def _(block):
            for copy in copies(slot, block, block_place(frame, block)):
                copy.start()

    slot = lax.rem(step, 2)

    @pl.when(step == 0)
    def _():
        fetch(step, slot)

    @pl.when(step + 1 < count)
    def _():
        fetch(step + 1, 1 - slot)

    @pl.loop(0, n_blocks)
    def _(block):
        for copy in copies(slot, block, (0, 0, 0)):
            copy.wait()

    width = q_ref.shape[-1]
    rows = n_tok * BLOCK
    n_keys = n_blocks * BLOCK
    frame = outer_index * (inner * FRAMES_DEV) + step
    position = lax.broadcasted_iota(jnp.int32, (1, n_keys), 1)
    bias = jnp.zeros((1, n_keys), jnp.float32)
    for entry in range(ENTRIES):
        live = table_ref[3 * entry_len + frame * ENTRIES + entry]
        low = 2 * rows + entry * BLOCK
        dead = (position >= low) & (position < low + BLOCK) & (live == 0)
        bias = jnp.where(dead, -1e30, bias)
    block_rows = math.gcd(rows, 256)
    lane_head = lax.broadcasted_iota(jnp.int32, (1, width), 1) // HEAD_DIM
    keys = key_set.at[slot]
    values = value_set.at[slot]
    for first in range(0, n_tok, block_rows // BLOCK):
        query = q_ref[0, first : first + block_rows // BLOCK, 0].reshape(block_rows, width)
        query = query * jnp.asarray(HEAD_DIM**-0.5, query.dtype)
        result = jnp.zeros((block_rows, width), jnp.float32)
        for head in range(width // HEAD_DIM):
            mine = lane_head == head
            head_query = jnp.where(mine, query, jnp.zeros_like(query))
            scores = lax.dot_general(
                head_query, keys[...], (((1,), (1,)), ((), ())), preferred_element_type=jnp.float32
            )
            scores = scores + bias
            weights = jnp.exp(scores - jnp.max(scores, axis=-1, keepdims=True))
            weight_sum = jnp.sum(weights, axis=-1, keepdims=True)
            attended = jnp.dot(
                weights.astype(jnp.bfloat16), values[...], preferred_element_type=jnp.float32
            )
            result = jnp.where(mine, attended / weight_sum, result)
        out_ref[0, first : first + block_rows // BLOCK, 0] = result.astype(out_ref.dtype).reshape(
            block_rows // BLOCK, BLOCK, width
        )


def attend(table, query, pool, inner, n_tok, n_frames):
    n_local = inner * FRAMES_DEV
    width = query.shape[-1]
    n_blocks = 2 * n_tok + ENTRIES
    frame_spec = pl.BlockSpec(
        (1, n_tok, 1, BLOCK, width), lambda g, t: (g // FRAMES_DEV, 0, g % FRAMES_DEV, 0, 0)
    )
    key_rows = n_blocks * BLOCK
    flops = 4 * n_local * n_tok * BLOCK * key_rows * width
    return pl.pallas_call(
        functools.partial(attend_kernel, inner=inner, n_tok=n_tok, n_frames=n_frames),
        out_shape=jax.ShapeDtypeStruct(query.shape, query.dtype),
        grid_spec=pltpu.PrefetchScalarGridSpec(
            num_scalar_prefetch=1,
            grid=(n_local,),
            in_specs=[frame_spec, pl.BlockSpec(memory_space=pl.ANY)],
            out_specs=frame_spec,
            scratch_shapes=[
                pltpu.VMEM((2, key_rows, width), query.dtype),
                pltpu.VMEM((2, key_rows, width), query.dtype),
                pltpu.SemaphoreType.DMA((2, n_blocks, 2)),
            ],
        ),
        compiler_params=pltpu.CompilerParams(vmem_limit_bytes=48 * 1024 * 1024),
        cost_estimate=pl.CostEstimate(
            flops=flops,
            bytes_accessed=4 * n_local * key_rows * width + 4 * query.size,
            transcendentals=flops // (4 * HEAD_DIM),
        ),
    )(table, query, pool)


def shards(queries, keys, values, epi_dev, epi_frame, epi_block, valid, ref_local, *, n_tm, n_tok):
    inner = math.gcd(SPAN, max(1, HEADS // n_tok))
    n_outer = n_tm // inner
    n_ranks = inner * n_tok
    width = keys.shape[2] // n_ranks
    n_frames = epi_dev.shape[0]
    plane_groups = [
        [(o * inner + i) * n_tok + t for i in range(inner) for t in range(n_tok)]
        for o in range(n_outer)
    ]
    outer_groups = [[o * inner + i for o in range(n_outer)] for i in range(inner)]

    def to_heads(x):
        return lax.all_to_all(
            x, ("tm", "tok"), 0, 0, axis_index_groups=plane_groups, tiled=True
        )

    my_outer = lax.axis_index("tm") // inner
    table = jnp.concatenate(
        [a.reshape(-1) for a in (epi_dev, epi_frame, epi_block, valid, ref_local)]
        + [my_outer.reshape(1).astype(jnp.int32)]
    )
    pair = jnp.stack([keys, values]).reshape(2, FRAMES_DEV, BLOCK, n_ranks, width)
    own = to_heads(pair.transpose(3, 1, 0, 2, 4))
    pool = lax.all_gather(own, "tm", axis=0, axis_index_groups=outer_groups)
    query = to_heads(queries.reshape(FRAMES_DEV, BLOCK, n_ranks, width).transpose(2, 0, 1, 3))
    query = query.reshape(inner, n_tok, FRAMES_DEV, BLOCK, width)
    attended = attend(table, query, pool, inner, n_tok, n_frames)
    attended = to_heads(attended.reshape(n_ranks, FRAMES_DEV, BLOCK, width))
    return attended.transpose(1, 2, 0, 3).reshape(queries.shape)


def solution(mesh):
    return jax.shard_map(
        functools.partial(shards, n_tm=mesh.shape["tm"], n_tok=mesh.shape["tok"]),
        mesh=mesh,
        in_specs=(P("tm", "tok", None),) * 3 + (P(),) * 5,
        out_specs=P("tm", "tok", None),
        check_vma=False,
    )
```

time: 262 us -> 157 us (0.60)
  local copies, waits for them, and re-layouts: 71 us -> 8.97 us
  waiting for transfers between devices: 111 us -> 75.8 us
  matrix products: 23 us -> 0 us
  Pallas kernels: 0 us -> 22.7 us
  other arithmetic: 5.45 us -> 0.1 us
    all_gather x2 -> x1, waiting for transfers between devices: 106 us -> 68 us  [shards(): pool = lax.all_gather(own, 'tm', axis=0, axis_index_groups=outer_groups)]
    all_gather x2 -> x0, local copies, waits for them, and re-layouts: 22.9 us -> none  [the longest x1 11.5 us: shards(): lax.all_gather(head_v, 'tm', axis=0, tiled=True)]
    pallas_call x0 -> x1, Pallas kernels: none -> 22.7 us  [attend(): pl.pallas_call(functools.partial(attend_kernel, inner=inner, n_tok=n_tok,...]
    gather x4 -> x0, local copies, waits for them, and re-layouts: 16 us -> none  [the longest x2 8 us: pick_block(): lax.dynamic_slice(piece_values, corner, (1, BLOCK, slab_width))[0]]
    dynamic_slice x15 -> x0, local copies, waits for them, and re-layouts: 15.5 us -> none  [the longest x14 14.9 us: shards(): lax.map(one_frame, (head_q, head_k, head_v, epi_keys, epi_values, live_epi))]
    sub x2 -> x0, matrix products: 14.2 us -> none  [per_block(): weights = jnp.exp(scores - row_max) * live_mask]
    dot_general x2 -> x0, matrix products: 8.82 us -> none  [per_block(): jnp.einsum('hqk,khd->qhd', weights.astype(jnp.bfloat16), value_heads, pre...]
    select_n x3 -> x0, other arithmetic: 5.26 us -> none  [the longest x1 3.32 us: collect(): epi_keys = jnp.where(inside[:, :, None, None], new_keys, epi_keys)]
  transfers between devices with their start and end apart: 3 -> 2, of which waited for: 3 -> 2; matrix products, arithmetic and copies ran while one was open for 9% -> 1% of each run, Pallas kernels for 0% -> 0%
where the time goes in v1:
time: 157 us
  waiting for transfers between devices  75.8 us (48%)
  blocking collectives  31.9 us (20%)
  Pallas kernels  22.7 us (14%)
  between operations  13.6 us (9%)
  local copies, waits for them, and re-layouts  8.97 us (6%)
  starting transfers between devices  3.5 us (2%)
    all_gather x1, waiting for transfers between devices, shards(): pool = lax.all_gather(own, 'tm', axis=0, axis_index_groups=outer_groups)  68 us
    all_to_all x2, blocking collectives, to_heads(): lax.all_to_all(x, ('tm', 'tok'), 0, 0, axis_index_groups=plane_groups, ti...  31.9 us
    pallas_call x1, Pallas kernels, attend(): pl.pallas_call(functools.partial(attend_kernel, inner=inner, n_tok=n_tok,...  22.7 us
    all_to_all x1, waiting for transfers between devices, to_heads(): lax.all_to_all(x, ('tm', 'tok'), 0, 0, axis_index_groups=plane_groups, ti...  7.84 us
    unnamed x20, local copies, waits for them, and re-layouts  5.26 us
    all_to_all x1, starting transfers between devices, to_heads(): lax.all_to_all(x, ('tm', 'tok'), 0, 0, axis_index_groups=plane_groups, ti...  3.49 us
  transfers between devices with their start and end apart: 2, of which 2 were waited for; matrix products, arithmetic and copies ran while one was open for 1% of the time, Pallas kernels for 0%

profile of v1, /device:TPU:0, one launch (start us, length us, event | category | flops | bytes accessed | tf_op | source)
XLA Modules:
  0.0 156.5 jit_solution(17967382414434627515)
XLA Ops:
  6.5 1.4 copy.41
  7.9 1.3 copy.42
  9.2 0.1 maximum_bitcast_fusion
  9.3 0.1 copy.43
  9.5 19.6 %all_to_all.15 = bf16[8,2,2,128,128]{3,4,1,2,0:T(8,128)(2,1)S(1)} all-to-all(bf16[8,2,2,128,128]{3,4,1,2,0:T(8,128)(2,1)S(1)} %copy.43), channel_id=1, replica_groups={{0,1,2,3,4,5,6,7},{8,9,10,11,12,13,14,15},{16,17,18,19,20,21,22,23},{24..., dimensions={0} | all-to-all | bytes 2097152 | tf_op jit(solution)/shard_map/all_to_all | solution.py:169
  29.1 1.3 copy.44
  30.4 0.0 all-gather.3.cloned.1.call-update
  30.4 0.9 bitcast_bitcast_fusion
  31.3 3.5 %all-to-all-start = ((bf16[8,2,128,128]{3,2,1,0:T(8,128)(2,1)}), bf16[8,2,128,128]{3,2,1,0:T(8,128)(2,1)S(1)}, u32[]{:S(2)}, u32[]{:S(2)}) async-start(bf16[8,2,128,128]{3,2,1,0:T(8,128)(2,1)} %bitcast_bitcast_fusion), calls=%async_computation | async-start | bytes 1048576 | tf_op jit(solution)/shard_map/all_to_all | solution.py:169
  34.9 0.1 copy.36
  35.0 0.1 reshape.32
  35.1 0.1 copy.37
  35.2 0.1 reshape.33
  35.3 0.1 copy.38
  35.4 0.1 reshape.34
  35.5 0.1 copy.39
  35.6 0.1 reshape.35
  35.7 0.1 concatenate.4.table_ref
  35.8 7.8 %all-to-all-done = bf16[8,2,128,128]{3,2,1,0:T(8,128)(2,1)S(1)} async-done(((bf16[8,2,128,128]{3,2,1,0:T(8,128)(2,1)}), bf16[8,2,128,128]{3,2,1,0:T(8,128)(2,1)S(1)}, u32[]{:S(2)}, u32[]{:S(2)}) %all-to-all-start) | async-done | bytes 524320 | tf_op jit(solution)/shard_map/all_to_all | solution.py:169
  43.6 68.0 %all-gather.3.cloned.1.call-done = bf16[32,2,2,128,128]{4,3,2,1,0:T(8,128)(2,1)} async-done(((bf16[8,2,2,128,128]{4,3,2,1,0:T(8,128)(2,1)}), bf16[32,2,2,128,128]{4,3,2,1,0:T(8,128)(2,1)}) %all-gather.3.cloned.1.call-update) | async-done | bytes 4194320 | tf_op jit(solution)/shard_map/all_gather | solution.py:180
  111.6 2.2 %copy-done.1 = bf16[32,2,2,128,128]{4,3,2,1,0:T(8,128)(2,1)S(1)} copy-done((bf16[32,2,2,128,128]{4,3,2,1,0:T(8,128)(2,1)S(1)}, bf16[32,2,2,128,128]{4,3,2,1,0:T(8,128)(2,1)}, u32[]{:S(2)}) %copy-start.1) | copy-done | bytes 4194328
  113.8 22.7 %shard_map.82 = bf16[4,2,2,128,128]{4,3,2,1,0:T(8,128)(2,1)S(1)} custom-call(s32[773]{0:T(1024)S(1)} %concatenate.4.table_ref, bf16[4,2,2,128,128]{4,3,2,1,0:T(8,128)(2,1)S(1)} %bitcast.21, bf16[4,8,2,2,128,128]{5,4,3,2,1,0:T(8,128)(2,1)S(1)} %bitcast.23), custom_call_target="tpu_custom_call" | custom-call | flops 1342177280 | bytes 6291456 | tf_op jit(solution)/shard_map/pallas_call | solution.py:133
  136.5 12.3 %all_to_all.16 = bf16[8,2,128,128]{3,2,1,0:T(8,128)(2,1)S(1)} all-to-all(bf16[8,2,128,128]{3,2,1,0:T(8,128)(2,1)S(1)} %bitcast.22), channel_id=1, replica_groups={{0,1,2,3,4,5,6,7},{8,9,10,11,12,13,14,15},{16,17,18,19,20,21,22,23},{24..., dimensions={0} | all-to-all | bytes 1048576 | tf_op jit(solution)/shard_map/all_to_all | solution.py:169
  148.8 0.9 copy_bitcast_fusion
  (14 shorter events, 0.0 us)
Async XLA Ops:
  6.5 23.9 %copy-start = (bf16[2,128,1024]{2,1,0:T(8,128)(2,1)S(1)}, bf16[2,128,1024]{2,1,0:T(8,128)(2,1)}, u32[]{:S(2)}) copy-start(bf16[2,128,1024]{2,1,0:T(8,128)(2,1)} %param.8) | copy-start | bytes 1572868
  6.5 105.1 %all-gather.3.cloned.1.call-start = ((), (), s32[]{:S(2)}) async-start(), calls=%async_computation.3 | async-start | bytes 5242880 | tf_op jit(solution)/shard_map/all_gather | solution.py:180
  9.5 25.4 %copy-start.2 = (s32[32,6]{0,1:T(8,128)S(1)}, s32[32,6]{0,1:T(8,128)}, u32[]{:S(2)}) copy-start(s32[32,6]{0,1:T(8,128)} %param.11) | copy-start | bytes 2308
  9.5 25.6 %copy-start.3 = (s32[32,6]{0,1:T(8,128)S(1)}, s32[32,6]{0,1:T(8,128)}, u32[]{:S(2)}) copy-start(s32[32,6]{0,1:T(8,128)} %param.12) | copy-start | bytes 2308
  9.5 25.8 %copy-start.4 = (s32[32,6]{0,1:T(8,128)S(1)}, s32[32,6]{0,1:T(8,128)}, u32[]{:S(2)}) copy-start(s32[32,6]{0,1:T(8,128)} %param.13) | copy-start | bytes 2308
  9.5 26.0 %copy-start.5 = (s32[32,6]{0,1:T(8,128)S(1)}, s32[32,6]{0,1:T(8,128)}, u32[]{:S(2)}) copy-start(s32[32,6]{0,1:T(8,128)} %param.14) | copy-start | bytes 2308
  9.5 26.2 %copy-start.6 = (s32[4]{0:T(128)S(1)}, s32[4]{0:T(128)}, u32[]{:S(2)}) copy-start(s32[4]{0:T(128)} %param.15) | copy-start | bytes 52
  31.3 12.3 %all-to-all-start = ((bf16[8,2,128,128]{3,2,1,0:T(8,128)(2,1)}), bf16[8,2,128,128]{3,2,1,0:T(8,128)(2,1)S(1)}, u32[]{:S(2)}, u32[]{:S(2)}) async-start(bf16[8,2,128,128]{3,2,1,0:T(8,128)(2,1)} %bitcast_bitcast_fusion), calls=%async_computation | async-start | bytes 1048576 | tf_op jit(solution)/shard_map/all_to_all | solution.py:169
  111.6 2.2 %copy-start.1 = (bf16[32,2,2,128,128]{4,3,2,1,0:T(8,128)(2,1)S(1)}, bf16[32,2,2,128,128]{4,3,2,1,0:T(8,128)(2,1)}, u32[]{:S(2)}) copy-start(bf16[32,2,2,128,128]{4,3,2,1,0:T(8,128)(2,1)} %all-gather.3.cloned.1.call-done) | copy-start | bytes 12582916
Sparse Core Ops, SparseCore 0:
  30.5 81.0 all-gather.2

commit v2 on v1

--- a/solution.py
+++ b/solution.py
@@ -17,10 +17,13 @@
 
 
 def attend_kernel(
-    table_ref, q_ref, pool_ref, out_ref, key_set, value_set, sems, *, inner, n_tok, n_frames
+    table_ref, plan_ref, q_ref, *refs, inner, n_tok, n_frames, spot_row
 ):
+    buffers, (out_ref, key_set, value_set, sems) = refs[:-4], refs[-4:]
+    key_buffers, value_buffers = buffers[::2], buffers[1::2]
     step = pl.program_id(0)
     count = pl.num_programs(0)
+    units = inner * n_tok * FRAMES_DEV
     entry_len = n_frames * ENTRIES
     n_blocks = 2 * n_tok + ENTRIES
     outer_index = table_ref[4 * entry_len + n_frames // (SPAN * FRAMES_DEV)]
@@ -44,20 +47,18 @@
         token_block = jnp.where(
             is_own, block, jnp.where(is_ref, ref_block, table_ref[2 * entry_len + entry])
         )
-        return dev // inner, (dev % inner) * n_tok + token_block, place
-
-    def copies(slot, block, source):
-        outer, row, place = source
+        unit = ((dev % inner) * n_tok + token_block) * FRAMES_DEV + place
+        outer = dev // inner
+        return jnp.where(outer == outer_index, unit, plan_ref[spot_row, outer * units + unit])
+
+    def copies(slot, block, index, spot):
+        rows = pl.ds(block * BLOCK, BLOCK)
         return (
             pltpu.make_async_copy(
-                pool_ref.at[outer, row, place, 0],
-                key_set.at[slot, pl.ds(block * BLOCK, BLOCK)],
-                sems.at[slot, block, 0],
+                key_buffers[index].at[spot], key_set.at[slot, rows], sems.at[slot, block, 0]
             ),
             pltpu.make_async_copy(
-                pool_ref.at[outer, row, place, 1],
-                value_set.at[slot, pl.ds(block * BLOCK, BLOCK)],
-                sems.at[slot, block, 1],
+                value_buffers[index].at[spot], value_set.at[slot, rows], sems.at[slot, block, 1]
             ),
         )
 
@@ -66,8 +67,13 @@
 
         @pl.loop(0, n_blocks)
         def _(block):
-            for copy in copies(slot, block, block_place(frame, block)):
-                copy.start()
+            code = block_place(frame, block)
+            for index in range(len(key_buffers)):
+
+                @pl.when(code // 1024 == index)
+                def _():
+                    for copy in copies(slot, block, index, code % 1024):
+                        copy.start()
 
     slot = lax.rem(step, 2)
 
@@ -81,7 +87,7 @@
 
     @pl.loop(0, n_blocks)
     def _(block):
-        for copy in copies(slot, block, (0, 0, 0)):
+        for copy in copies(slot, block, 0, 0):
             copy.wait()
 
     width = q_ref.shape[-1]
@@ -121,22 +127,24 @@
         )
 
 
-def attend(table, query, pool, inner, n_tok, n_frames):
+def attend(table, plan, query, buffers, inner, n_tok, n_frames, spot_row):
     n_local = inner * FRAMES_DEV
     width = query.shape[-1]
     n_blocks = 2 * n_tok + ENTRIES
     frame_spec = pl.BlockSpec(
-        (1, n_tok, 1, BLOCK, width), lambda g, t: (g // FRAMES_DEV, 0, g % FRAMES_DEV, 0, 0)
+        (1, n_tok, 1, BLOCK, width), lambda g, *_: (g // FRAMES_DEV, 0, g % FRAMES_DEV, 0, 0)
     )
     key_rows = n_blocks * BLOCK
     flops = 4 * n_local * n_tok * BLOCK * key_rows * width
     return pl.pallas_call(
-        functools.partial(attend_kernel, inner=inner, n_tok=n_tok, n_frames=n_frames),
+        functools.partial(
+            attend_kernel, inner=inner, n_tok=n_tok, n_frames=n_frames, spot_row=spot_row
+        ),
         out_shape=jax.ShapeDtypeStruct(query.shape, query.dtype),
         grid_spec=pltpu.PrefetchScalarGridSpec(
-            num_scalar_prefetch=1,
+            num_scalar_prefetch=2,
             grid=(n_local,),
-            in_specs=[frame_spec, pl.BlockSpec(memory_space=pl.ANY)],
+            in_specs=[frame_spec] + [pl.BlockSpec(memory_space=pl.ANY)] * len(buffers),
             out_specs=frame_spec,
             scratch_shapes=[
                 pltpu.VMEM((2, key_rows, width), query.dtype),
@@ -150,39 +158,239 @@
             bytes_accessed=4 * n_local * key_rows * width + 4 * query.size,
             transcendentals=flops // (4 * HEAD_DIM),
         ),
-    )(table, query, pool)
+    )(table, plan, query, *buffers)
+
+
+def plan_kernel(
+    me_ref, ref_ref, dev_ref, place_ref, block_ref, valid_ref, out_ref, *, inner, n_tok, rounds, room
+):
+    n_frames = dev_ref.shape[0]
+    units = inner * n_tok * FRAMES_DEV
+    plane_frames = inner * FRAMES_DEV
+    n_outer = n_frames // plane_frames
+    lanes = out_ref.shape[1]
+    f32 = jnp.float32
+    me = me_ref[0].astype(f32)
+    dev, place = dev_ref[...], place_ref[...]
+    ids = (dev // inner) * units + ((dev % inner) * n_tok + block_ref[...]) * FRAMES_DEV + place
+    used = valid_ref[...] > 0
+    frame_lane = lax.broadcasted_iota(jnp.int32, (n_frames, lanes), 1)
+    hit = jnp.zeros((n_frames, lanes), f32)
+    for entry in range(ENTRIES):
+        here = (ids[:, entry : entry + 1] == frame_lane) & used[:, entry : entry + 1]
+        hit = jnp.where(here, 1.0, hit)
+    lane = lax.broadcasted_iota(jnp.int32, (1, lanes), 1)
+    unit = lane % units
+    origin = (lane // units).astype(f32)
+    need = []
+    for plane in range(n_outer):
+        rows = lax.slice_in_dim(hit, plane * plane_frames, (plane + 1) * plane_frames)
+        wanted = jnp.max(rows, axis=0, keepdims=True) > 0
+        if inner % SPAN:
+            group = plane * inner // SPAN
+            ref_frame = group * (SPAN * FRAMES_DEV) + ref_ref[group]
+            ref_dev = ref_frame // FRAMES_DEV
+            wanted = wanted | (
+                (lane // (n_tok * FRAMES_DEV) == ref_dev)
+                & (lane % FRAMES_DEV == ref_frame % FRAMES_DEV)
+            )
+        need.append(wanted)
+
+    square_row = lax.broadcasted_iota(jnp.int32, (lanes, lanes), 0)
+    square_lane = lax.broadcasted_iota(jnp.int32, (lanes, lanes), 1)
+    diagonal = square_row == square_lane
+    earlier = square_row < square_lane
+
+    def column(row):
+        return jnp.sum(jnp.where(diagonal, row, 0.0), axis=1, keepdims=True)
+
+    def count(mask, axis):
+        return jnp.sum(jnp.where(mask, 1.0, 0.0), axis=axis, keepdims=True)
+
+    def one_way(start, reach, here):
+        start_col, reach_col = column(start), column(reach)
+        ahead = (reach_col > reach) | ((reach_col == reach) & earlier)
+        rank = count((start_col == start) & (reach_col > 0) & ahead, 0)
+        depart = jnp.zeros_like(start)
+        for plane in range(n_outer - 1, 0, -1):
+            total = jnp.zeros((1, 1), f32)
+            turn = jnp.ones_like(start)
+            for step in range(1, rounds + 1):
+                if plane < n_outer - 1:
+                    passing = (
+                        (start > plane)
+                        & (start - reach <= plane - 1)
+                        & (depart + (start - plane) == step)
+                        & (reach > 0)
+                    )
+                    total = total + (room - count(passing, 1))
+                else:
+                    total = total + room
+                turn = turn + jnp.where(total <= rank, 1.0, 0.0)
+            depart = jnp.where((start == plane) & (reach > 0), turn, depart)
+        last = jnp.max(jnp.where(reach > 0, depart + reach - 1.0, 0.0), axis=1, keepdims=True)
+
+        def on_link(link):
+            crosses = (reach > 0) & (start > link) & (start - reach <= link)
+            step = jnp.where(crosses, depart + (start - 1.0 - link), -1.0)
+            slot = count((column(step) == step) & earlier, 0)
+            return crosses, step, slot
+
+        arrives, in_step, in_slot = on_link(here)
+        leaves, out_step, out_slot = on_link(here - 1.0)
+        source = jnp.where(start == here, unit.astype(f32), units + in_slot)
+        key = column(jnp.where(leaves, (out_step - 1.0) * room + out_slot, -1.0))
+        sent = jnp.sum(
+            jnp.where(key == square_lane.astype(f32), column(source), 0.0), axis=0, keepdims=True
+        )
+        return arrives, in_step, in_slot, sent, last
+
+    lowest, highest = origin, origin
+    for plane in range(n_outer):
+        highest = jnp.where(need[plane] & (origin < plane), float(plane), highest)
+        other = n_outer - 1 - plane
+        lowest = jnp.where(need[other] & (origin > other), float(other), lowest)
+    top = n_outer - 1.0
+    down = one_way(origin, origin - lowest, me)
+    up = one_way(top - origin, highest - origin, top - me)
+    unit_f = unit.astype(f32)
+    spots = unit_f
+    for way, (arrives, in_step, in_slot, _, _) in enumerate((down, up)):
+        spots = jnp.where(arrives, (in_step + way * rounds) * 1024 + in_slot, spots)
+    distance = origin - me
+    full = jnp.where(distance > 0, distance, jnp.where(distance < 0, n_outer - 1 - distance, 0))
+    last = jnp.maximum(down[4], up[4]) + jnp.zeros_like(origin)
+    rows = [spots, down[3], up[3], full * 1024 + unit_f, last]
+    for index, row in enumerate(rows):
+        out_ref[index : index + 1, :] = row.astype(jnp.int32)
+
+
+def make_plan(epi_dev, epi_frame, epi_block, valid, ref_local, my_outer, inner, n_tok, rounds, room):
+    n_blocks = epi_dev.shape[0] * n_tok
+    lanes = -(-n_blocks // 128) * 128
+    smem, vmem = pl.BlockSpec(memory_space=pltpu.SMEM), pl.BlockSpec(memory_space=pltpu.VMEM)
+    return pl.pallas_call(
+        functools.partial(plan_kernel, inner=inner, n_tok=n_tok, rounds=rounds, room=room),
+        out_shape=jax.ShapeDtypeStruct((8, lanes), jnp.int32),
+        in_specs=[smem, smem, vmem, vmem, vmem, vmem],
+        out_specs=vmem,
+        compiler_params=pltpu.CompilerParams(vmem_limit_bytes=32 * 1024 * 1024),
+    )(my_outer.reshape(1), ref_local, epi_dev, epi_frame, epi_block, valid)
+
+
+def pack_kernel(plan_ref, *refs, step, room, units):
+    sources, targets = refs[:-2], refs[-2:]
+    own = sources[0]
+    for way, target in enumerate(targets):
+        for slot in range(room):
+            code = plan_ref[1 + way, (step - 1) * room + slot]
+            if step == 1:
+                target[slot] = own[code]
+            else:
+
+                @pl.when(code < units)
+                def _():
+                    target[slot] = own[code]
+
+                @pl.when(code >= units)
+                def _():
+                    target[slot] = sources[1 + way][code - units]
+
+
+def pack(plan, own, previous, step, room):
+    out = jax.ShapeDtypeStruct((room,) + own.shape[1:], own.dtype)
+    whole = pl.BlockSpec(memory_space=pltpu.VMEM)
+    return pl.pallas_call(
+        functools.partial(pack_kernel, step=step, room=room, units=own.shape[0]),
+        out_shape=(out, out),
+        grid_spec=pltpu.PrefetchScalarGridSpec(
+            num_scalar_prefetch=1,
+            grid=(),
+            in_specs=[whole] * (1 + len(previous)),
+            out_specs=(whole, whole),
+        ),
+        compiler_params=pltpu.CompilerParams(vmem_limit_bytes=16 * 1024 * 1024),
+        cost_estimate=pl.CostEstimate(
+            flops=0, bytes_accessed=8 * math.prod(out.shape), transcendentals=0
+        ),
+    )(plan, own, *previous)
 
 
 def shards(queries, keys, values, epi_dev, epi_frame, epi_block, valid, ref_local, *, n_tm, n_tok):
     inner = math.gcd(SPAN, max(1, HEADS // n_tok))
     n_outer = n_tm // inner
     n_ranks = inner * n_tok
+    units = n_ranks * FRAMES_DEV
     width = keys.shape[2] // n_ranks
     n_frames = epi_dev.shape[0]
+    rounds, room = n_outer - 1, -(-units * 5 // 8)
     plane_groups = [
         [(o * inner + i) * n_tok + t for i in range(inner) for t in range(n_tok)]
         for o in range(n_outer)
     ]
-    outer_groups = [[o * inner + i for o in range(n_outer)] for i in range(inner)]
-
-    def to_heads(x):
+
+    def exchange(x):
         return lax.all_to_all(
             x, ("tm", "tok"), 0, 0, axis_index_groups=plane_groups, tiled=True
         )
 
-    my_outer = lax.axis_index("tm") // inner
+    def to_heads(x):
+        return exchange(
+            x.reshape(FRAMES_DEV, BLOCK, n_ranks, width).transpose(2, 0, 1, 3)
+        )
+
+    def shift(x, way):
+        pairs = [
+            (o * inner + i, (o + way) * inner + i)
+            for o in range(n_outer)
+            for i in range(inner)
+            if 0 <= o + way < n_outer
+        ]
+        return lax.ppermute(x, "tm", pairs)
+
+    my_outer = (lax.axis_index("tm") // inner).astype(jnp.int32)
     table = jnp.concatenate(
         [a.reshape(-1) for a in (epi_dev, epi_frame, epi_block, valid, ref_local)]
-        + [my_outer.reshape(1).astype(jnp.int32)]
+        + [my_outer.reshape(1)]
     )
-    pair = jnp.stack([keys, values]).reshape(2, FRAMES_DEV, BLOCK, n_ranks, width)
-    own = to_heads(pair.transpose(3, 1, 0, 2, 4))
-    pool = lax.all_gather(own, "tm", axis=0, axis_index_groups=outer_groups)
-    query = to_heads(queries.reshape(FRAMES_DEV, BLOCK, n_ranks, width).transpose(2, 0, 1, 3))
-    query = query.reshape(inner, n_tok, FRAMES_DEV, BLOCK, width)
-    attended = attend(table, query, pool, inner, n_tok, n_frames)
-    attended = to_heads(attended.reshape(n_ranks, FRAMES_DEV, BLOCK, width))
-    return attended.transpose(1, 2, 0, 3).reshape(queries.shape)
+    plan = make_plan(
+        epi_dev, epi_frame, epi_block, valid, ref_local, my_outer, inner, n_tok, rounds, room
+    )
+    own_keys = to_heads(keys).reshape(units, BLOCK, width)
+    own_values = to_heads(values).reshape(units, BLOCK, width)
+    query = to_heads(queries).reshape(inner, n_tok, FRAMES_DEV, BLOCK, width)
+
+    def finish(query, own, down, up, spot_row):
+        buffers = [own] + down + up
+        flat = [array for pair in buffers for array in pair]
+        attended = attend(table, plan, query, flat, inner, n_tok, n_frames, spot_row)
+        attended = exchange(attended.reshape(n_ranks, FRAMES_DEV, BLOCK, width))
+        return attended.transpose(1, 2, 0, 3).reshape(queries.shape)
+
+    def listed(query, own_keys, own_values):
+        got = {}
+        for step in range(1, rounds + 1):
+            for kind, own in enumerate((own_keys, own_values)):
+                previous = [got[kind, way, step - 1] for way in (0, 1)] if step > 1 else []
+                sent = pack(plan, own, previous, step, room)
+                for way in (0, 1):
+                    got[kind, way, step] = shift(sent[way], 2 * way - 1)
+        received = [
+            [(got[0, way, step], got[1, way, step]) for step in range(1, rounds + 1)]
+            for way in (0, 1)
+        ]
+        return finish(query, (own_keys, own_values), *received, 0)
+
+    def gathered(query, own_keys, own_values):
+        received = ([], [])
+        for way in (0, 1):
+            pair = (own_keys, own_values)
+            for _ in range(n_outer - 1):
+                pair = tuple(shift(array, 2 * way - 1) for array in pair)
+                received[way].append(pair)
+        return finish(query, (own_keys, own_values), *received, 3)
+
+    return lax.cond(plan[4, 0] <= rounds, listed, gathered, query, own_keys, own_values)
 
 
 def solution(mesh):

time: 157 us -> 129 us (0.82)
  waiting for transfers between devices: 75.8 us -> 25.4 us
  starting transfers between devices: 3.5 us -> 48.4 us
  blocking collectives: 31.9 us -> 11.3 us
  between operations: 13.6 us -> 0.8 us
  Pallas kernels: 22.7 us -> 32.6 us
    all_gather x1 -> x0, waiting for transfers between devices: 68 us -> none  [shards(): pool = lax.all_gather(own, 'tm', axis=0, axis_index_groups=outer_groups)]
    ppermute x0 -> x12, starting transfers between devices: none -> 36.1 us  [shift(): return lax.ppermute(x, 'tm', pairs)]
    all_to_all x2 -> x1, blocking collectives: 31.9 us -> 11.3 us  [exchange(): lax.all_to_all(x, ('tm', 'tok'), 0, 0, axis_index_groups=plane_groups, ti...]
    all_to_all x1 -> x3, waiting for transfers between devices: 7.84 us -> 17.9 us  [exchange(): lax.all_to_all(x, ('tm', 'tok'), 0, 0, axis_index_groups=plane_groups, ti...]
    all_to_all x1 -> x3, starting transfers between devices: 3.49 us -> 12.3 us  [exchange(): lax.all_to_all(x, ('tm', 'tok'), 0, 0, axis_index_groups=plane_groups, ti...]
    ppermute x0 -> x12, waiting for transfers between devices: none -> 7.43 us  [shift(): return lax.ppermute(x, 'tm', pairs)]
    pallas_call x0 -> x7, Pallas kernels: none -> 6.09 us  [the longest x6 4.78 us: pack(): pl.pallas_call(functools.partial(pack_kernel, step=step, room=room, units...]
    pallas_call x1, Pallas kernels: 22.7 us -> 26.5 us  [attend(): pl.pallas_call(functools.partial(attend_kernel, inner=inner, n_tok=n_tok,...]
  transfers between devices with their start and end apart: 2 -> 15, of which waited for: 2 -> 9; matrix products, arithmetic and copies ran while one was open for 1% -> 3% of each run, Pallas kernels for 0% -> 4%
where the time goes in v2:
time: 129 us; the launch traced here: 128 us
  starting transfers between devices  48.4 us (38%)
  Pallas kernels  32.6 us (25%)
  waiting for transfers between devices  25.4 us (20%)
  blocking collectives  11.3 us (9%)
  local copies, waits for them, and re-layouts  9.22 us (7%)
    ppermute x12, starting transfers between devices, shift(): return lax.ppermute(x, 'tm', pairs)  36.1 us
    pallas_call x1, Pallas kernels, attend(): pl.pallas_call(functools.partial(attend_kernel, inner=inner, n_tok=n_tok,...  26.5 us
    all_to_all x3, waiting for transfers between devices, exchange(): lax.all_to_all(x, ('tm', 'tok'), 0, 0, axis_index_groups=plane_groups, ti...  17.9 us
    all_to_all x3, starting transfers between devices, exchange(): lax.all_to_all(x, ('tm', 'tok'), 0, 0, axis_index_groups=plane_groups, ti...  12.3 us
    all_to_all x1, blocking collectives, exchange(): lax.all_to_all(x, ('tm', 'tok'), 0, 0, axis_index_groups=plane_groups, ti...  11.3 us
    ppermute x12, waiting for transfers between devices, shift(): return lax.ppermute(x, 'tm', pairs)  7.43 us
    unnamed x22, local copies, waits for them, and re-layouts  5.26 us
    pallas_call x6, Pallas kernels, pack(): pl.pallas_call(functools.partial(pack_kernel, step=step, room=room, units...  4.78 us
  transfers between devices with their start and end apart: 15, of which 9 were waited for; matrix products, arithmetic and copies ran while one was open for 3% of the time, Pallas kernels for 4%

profile of v2, /device:TPU:0, one launch (start us, length us, event | category | flops | bytes accessed | tf_op | source)
XLA Modules:
  0.0 128.0 jit_solution(8374397860300022761)
XLA Ops:
  2.0 5.3 %all-to-all-start.4 = ((bf16[8,2,128,128]{3,2,1,0:T(8,128)(2,1)}), bf16[8,2,128,128]{3,2,1,0:T(8,128)(2,1)S(1)}, u32[]{:S(2)}, u32[]{:S(2)}) async-start(bf16[8,2,128,128]{3,2,1,0:T(8,128)(2,1)} %bitcast_bitcast_fusion), calls=%async_computation.4 | async-start | bytes 1048576 | tf_op jit(solution)/shard_map/all_to_all | solution.py:333
  8.2 7.9 %all-to-all-done.4 = bf16[8,2,128,128]{3,2,1,0:T(8,128)(2,1)S(1)} async-done(((bf16[8,2,128,128]{3,2,1,0:T(8,128)(2,1)}), bf16[8,2,128,128]{3,2,1,0:T(8,128)(2,1)S(1)}, u32[]{:S(2)}, u32[]{:S(2)}) %all-to-all-start.4) | async-done | bytes 524320 | tf_op jit(solution)/shard_map/all_to_all | solution.py:333
  16.1 3.5 %all-to-all-start.2 = ((bf16[8,2,128,128]{3,2,1,0:T(8,128)(2,1)}), bf16[8,2,128,128]{3,2,1,0:T(8,128)(2,1)S(1)}, u32[]{:S(2)}, u32[]{:S(2)}) async-start(bf16[8,2,128,128]{3,2,1,0:T(8,128)(2,1)} %bitcast_bitcast_fusion.2), calls=%async_computation.2 | async-start | bytes 1048576 | tf_op jit(solution)/shard_map/all_to_all | solution.py:333
  20.6 7.8 %all-to-all-done.2 = bf16[8,2,128,128]{3,2,1,0:T(8,128)(2,1)S(1)} async-done(((bf16[8,2,128,128]{3,2,1,0:T(8,128)(2,1)}), bf16[8,2,128,128]{3,2,1,0:T(8,128)(2,1)S(1)}, u32[]{:S(2)}, u32[]{:S(2)}) %all-to-all-start.2) | async-done | bytes 524320 | tf_op jit(solution)/shard_map/all_to_all | solution.py:333
  28.4 3.5 %all-to-all-start.3 = ((bf16[8,2,128,128]{3,2,1,0:T(8,128)(2,1)}), bf16[8,2,128,128]{3,2,1,0:T(8,128)(2,1)S(1)}, u32[]{:S(2)}, u32[]{:S(2)}) async-start(bf16[8,2,128,128]{3,2,1,0:T(8,128)(2,1)} %bitcast_bitcast_fusion.1), calls=%async_computation.3 | async-start | bytes 1048576 | tf_op jit(solution)/shard_map/all_to_all | solution.py:333
  35.8 1.3 %shard_map.84 = s32[8,128]{1,0:T(8,128)S(1)} custom-call(s32[1]{0:T(128)} %bitcast.4.me_ref, s32[4]{0:T(128)S(1)} %copy-done.1, s32[32,6]{1,0:T(8,128)S(1)} %copy.22.dev_ref, s32[32,6]{1,0:T(8,128)S(1)} %copy.23.place_ref, s32[32,6]{1,0:T(8,128)S(1)} %copy.24.block_ref, s32[32,6]{1,0:T(8,128)S(1)} %copy.25.valid_ref), custom_call_target="tpu_custom_call" | custom-call | tf_op jit(solution)/shard_map/pallas_call | solution.py:272
  38.5 2.2 %all-to-all-done.3 = bf16[8,2,128,128]{3,2,1,0:T(8,128)(2,1)S(1)} async-done(((bf16[8,2,128,128]{3,2,1,0:T(8,128)(2,1)}), bf16[8,2,128,128]{3,2,1,0:T(8,128)(2,1)S(1)}, u32[]{:S(2)}, u32[]{:S(2)}) %all-to-all-start.3) | async-done | bytes 524320 | tf_op jit(solution)/shard_map/all_to_all | solution.py:333
  40.7 86.5 %conditional.1 = (bf16[2,128,1024]{2,1,0:T(8,128)(2,1)S(1)}) conditional(s32[]{:T(128)} %bitcast.5, (bf16[16,128,128]{2,1,0:T(8,128)(2,1)S(1)}, bf16[16,128,128]{2,1,0:T(8,128)(2,1)S(1)}, s32[773]{0:T(1024)S(1)}, s32[8,128]{1,0:T(8,128)S(1)}, bf16[4,2,2,128,128]{4,3,2,1,0:T(8,128)(2,1)S(1)}) %tuple.21, (s32[8,128]{1,0:T(8,128)S(1)}, ...), branch_computations={%region_0.1_spmd, %region_1.2_spmd} | conditional | flops 1342177280 | bytes 37749280 | solution.py:393
  41.3 1.3 %collective-permute-start.12 = (bf16[10,128,128]{2,1,0:T(8,128)(2,1)S(1)}, bf16[10,128,128]{2,1,0:T(8,128)(2,1)S(1)}, u32[]{:S(2)}, u32[]{:S(2)}) collective-permute-start(bf16[10,128,128]{2,1,0:T(8,128)(2,1)S(1)} %get-tuple-element.38), channel_id=1, source_target_pairs={{8,0},{10,2},{12,4},{14,6},{16,8},{18,10},{20,12},{22,14},{24,16},... | collective-permute-start | bytes 983048 | tf_op jit(solution)/shard_map/cond/branch_1_fun/ppermute | solution.py:349
  42.6 4.6 %collective-permute-start.14 = (bf16[10,128,128]{2,1,0:T(8,128)(2,1)S(1)}, bf16[10,128,128]{2,1,0:T(8,128)(2,1)S(1)}, u32[]{:S(2)}, u32[]{:S(2)}) collective-permute-start(bf16[10,128,128]{2,1,0:T(8,128)(2,1)S(1)} %get-tuple-element.40), channel_id=1, source_target_pairs={{0,8},{2,10},{4,12},{6,14},{8,16},{10,18},{12,20},{14,22},{16,24},... | collective-permute-start | bytes 983048 | tf_op jit(solution)/shard_map/cond/branch_1_fun/ppermute | solution.py:349
  47.9 1.3 %collective-permute-start.13 = (bf16[10,128,128]{2,1,0:T(8,128)(2,1)S(1)}, bf16[10,128,128]{2,1,0:T(8,128)(2,1)S(1)}, u32[]{:S(2)}, u32[]{:S(2)}) collective-permute-start(bf16[10,128,128]{2,1,0:T(8,128)(2,1)S(1)} %get-tuple-element.39), channel_id=1, source_target_pairs={{8,0},{10,2},{12,4},{14,6},{16,8},{18,10},{20,12},{22,14},{24,16},... | collective-permute-start | bytes 983048 | tf_op jit(solution)/shard_map/cond/branch_1_fun/ppermute | solution.py:349
  49.2 4.6 %collective-permute-start.16 = (bf16[10,128,128]{2,1,0:T(8,128)(2,1)S(1)}, bf16[10,128,128]{2,1,0:T(8,128)(2,1)S(1)}, u32[]{:S(2)}, u32[]{:S(2)}) collective-permute-start(bf16[10,128,128]{2,1,0:T(8,128)(2,1)S(1)} %get-tuple-element.42), channel_id=1, source_target_pairs={{0,8},{2,10},{4,12},{6,14},{8,16},{10,18},{12,20},{14,22},{16,24},... | collective-permute-start | bytes 983048 | tf_op jit(solution)/shard_map/cond/branch_1_fun/ppermute | solution.py:349
  53.8 1.3 %collective-permute-done.14.refs_2_.refs_8_ = bf16[10,128,128]{2,1,0:T(8,128)(2,1)S(1)} collective-permute-done((bf16[10,128,128]{2,1,0:T(8,128)(2,1)S(1)}, bf16[10,128,128]{2,1,0:T(8,128)(2,1)S(1)}, u32[]{:S(2)}, u32[]{:S(2)}) %collective-permute-start.14) | collective-permute-done | bytes 327712 | tf_op jit(solution)/shard_map/cond/branch_1_fun/ppermute | solution.py:349
  56.0 1.3 %collective-permute-start.15 = (bf16[10,128,128]{2,1,0:T(8,128)(2,1)S(1)}, bf16[10,128,128]{2,1,0:T(8,128)(2,1)S(1)}, u32[]{:S(2)}, u32[]{:S(2)}) collective-permute-start(bf16[10,128,128]{2,1,0:T(8,128)(2,1)S(1)} %get-tuple-element.41), channel_id=1, source_target_pairs={{8,0},{10,2},{12,4},{14,6},{16,8},{18,10},{20,12},{22,14},{24,16},... | collective-permute-start | bytes 983048 | tf_op jit(solution)/shard_map/cond/branch_1_fun/ppermute | solution.py:349
  57.3 5.0 %collective-permute-start.18 = (bf16[10,128,128]{2,1,0:T(8,128)(2,1)S(1)}, bf16[10,128,128]{2,1,0:T(8,128)(2,1)S(1)}, u32[]{:S(2)}, u32[]{:S(2)}) collective-permute-start(bf16[10,128,128]{2,1,0:T(8,128)(2,1)S(1)} %get-tuple-element.44), channel_id=1, source_target_pairs={{0,8},{2,10},{4,12},{6,14},{8,16},{10,18},{12,20},{14,22},{16,24},... | collective-permute-start | bytes 983048 | tf_op jit(solution)/shard_map/cond/branch_1_fun/ppermute | solution.py:349
  63.2 1.3 %collective-permute-start.17 = (bf16[10,128,128]{2,1,0:T(8,128)(2,1)S(1)}, bf16[10,128,128]{2,1,0:T(8,128)(2,1)S(1)}, u32[]{:S(2)}, u32[]{:S(2)}) collective-permute-start(bf16[10,128,128]{2,1,0:T(8,128)(2,1)S(1)} %get-tuple-element.43), channel_id=1, source_target_pairs={{8,0},{10,2},{12,4},{14,6},{16,8},{18,10},{20,12},{22,14},{24,16},... | collective-permute-start | bytes 983048 | tf_op jit(solution)/shard_map/cond/branch_1_fun/ppermute | solution.py:349
  64.5 4.6 %collective-permute-start.20 = (bf16[10,128,128]{2,1,0:T(8,128)(2,1)S(1)}, bf16[10,128,128]{2,1,0:T(8,128)(2,1)S(1)}, u32[]{:S(2)}, u32[]{:S(2)}) collective-permute-start(bf16[10,128,128]{2,1,0:T(8,128)(2,1)S(1)} %get-tuple-element.46), channel_id=1, source_target_pairs={{0,8},{2,10},{4,12},{6,14},{8,16},{10,18},{12,20},{14,22},{16,24},... | collective-permute-start | bytes 983048 | tf_op jit(solution)/shard_map/cond/branch_1_fun/ppermute | solution.py:349
  70.0 1.3 %collective-permute-start.19 = (bf16[10,128,128]{2,1,0:T(8,128)(2,1)S(1)}, bf16[10,128,128]{2,1,0:T(8,128)(2,1)S(1)}, u32[]{:S(2)}, u32[]{:S(2)}) collective-permute-start(bf16[10,128,128]{2,1,0:T(8,128)(2,1)S(1)} %get-tuple-element.45), channel_id=1, source_target_pairs={{8,0},{10,2},{12,4},{14,6},{16,8},{18,10},{20,12},{22,14},{24,16},... | collective-permute-start | bytes 983048 | tf_op jit(solution)/shard_map/cond/branch_1_fun/ppermute | solution.py:349
  71.3 4.6 %collective-permute-start.22 = (bf16[10,128,128]{2,1,0:T(8,128)(2,1)S(1)}, bf16[10,128,128]{2,1,0:T(8,128)(2,1)S(1)}, u32[]{:S(2)}, u32[]{:S(2)}) collective-permute-start(bf16[10,128,128]{2,1,0:T(8,128)(2,1)S(1)} %get-tuple-element.48), channel_id=1, source_target_pairs={{0,8},{2,10},{4,12},{6,14},{8,16},{10,18},{12,20},{14,22},{16,24},... | collective-permute-start | bytes 983048 | tf_op jit(solution)/shard_map/cond/branch_1_fun/ppermute | solution.py:349
  77.4 1.3 %collective-permute-start.21 = (bf16[10,128,128]{2,1,0:T(8,128)(2,1)S(1)}, bf16[10,128,128]{2,1,0:T(8,128)(2,1)S(1)}, u32[]{:S(2)}, u32[]{:S(2)}) collective-permute-start(bf16[10,128,128]{2,1,0:T(8,128)(2,1)S(1)} %get-tuple-element.47), channel_id=1, source_target_pairs={{8,0},{10,2},{12,4},{14,6},{16,8},{18,10},{20,12},{22,14},{24,16},... | collective-permute-start | bytes 983048 | tf_op jit(solution)/shard_map/cond/branch_1_fun/ppermute | solution.py:349
  78.7 5.0 %collective-permute-start.23 = (bf16[10,128,128]{2,1,0:T(8,128)(2,1)S(1)}, bf16[10,128,128]{2,1,0:T(8,128)(2,1)S(1)}, u32[]{:S(2)}, u32[]{:S(2)}) collective-permute-start(bf16[10,128,128]{2,1,0:T(8,128)(2,1)S(1)} %get-tuple-element.49), channel_id=1, source_target_pairs={{0,8},{2,10},{4,12},{6,14},{8,16},{10,18},{12,20},{14,22},{16,24},... | collective-permute-start | bytes 983048 | tf_op jit(solution)/shard_map/cond/branch_1_fun/ppermute | solution.py:349
  83.8 4.2 %collective-permute-done.21.refs_7_ = bf16[10,128,128]{2,1,0:T(8,128)(2,1)S(1)} collective-permute-done((bf16[10,128,128]{2,1,0:T(8,128)(2,1)S(1)}, bf16[10,128,128]{2,1,0:T(8,128)(2,1)S(1)}, u32[]{:S(2)}, u32[]{:S(2)}) %collective-permute-start.21) | collective-permute-done | bytes 327712 | tf_op jit(solution)/shard_map/cond/branch_1_fun/ppermute | solution.py:349
  89.2 26.5 %branch_1_fun.13 = bf16[4,2,2,128,128]{4,3,2,1,0:T(8,128)(2,1)S(1)} custom-call(s32[773]{0:T(1024)S(1)} %get-tuple-element.33.table_ref, s32[8,128]{1,0:T(8,128)S(1)} %get-tuple-element.34.plan_ref, bf16[4,2,2,128,128]{4,3,2,1,0:T(8,128)(2,1)S(1)} %get-tuple-element.35.q_ref, bf16[16,128,128]{2,1,0:T(8,128)(2,1)S(1)} %get-tuple-element.36.refs_0_, ...), custom_call_target="tpu_custom_call" | custom-call | flops 1342177280 | bytes 6291456 | tf_op jit(solution)/shard_map/cond/branch_1_fun/pallas_call | solution.py:139
  115.8 11.3 %all_to_all.24 = bf16[8,2,128,128]{3,2,1,0:T(8,128)(2,1)S(1)} all-to-all(bf16[8,2,128,128]{3,2,1,0:T(8,128)(2,1)S(1)} %bitcast.41), channel_id=1, replica_groups={{0,1,2,3,4,5,6,7},{8,9,10,11,12,13,14,15},{16,17,18,19,20,21,22,23},{24..., dimensions={0} | all-to-all | bytes 1048576 | tf_op jit(solution)/shard_map/cond/branch_1_fun/all_to_all | solution.py:333
  (48 shorter events, 15.9 us)
Async XLA Ops:
  0.0 1.0 copy-start
  2.0 5.3 %copy-start.2 = (bf16[2,128,1024]{2,1,0:T(8,128)(2,1)S(1)}, bf16[2,128,1024]{2,1,0:T(8,128)(2,1)}, u32[]{:S(2)}) copy-start(bf16[2,128,1024]{2,1,0:T(8,128)(2,1)} %param.11) | copy-start | bytes 1572868
  2.0 14.2 %all-to-all-start.4 = ((bf16[8,2,128,128]{3,2,1,0:T(8,128)(2,1)}), bf16[8,2,128,128]{3,2,1,0:T(8,128)(2,1)S(1)}, u32[]{:S(2)}, u32[]{:S(2)}) async-start(bf16[8,2,128,128]{3,2,1,0:T(8,128)(2,1)} %bitcast_bitcast_fusion), calls=%async_computation.4 | async-start | bytes 1048576 | tf_op jit(solution)/shard_map/all_to_all | solution.py:333
  8.2 11.4 %copy-start.3 = (bf16[2,128,1024]{2,1,0:T(8,128)(2,1)S(1)}, bf16[2,128,1024]{2,1,0:T(8,128)(2,1)}, u32[]{:S(2)}) copy-start(bf16[2,128,1024]{2,1,0:T(8,128)(2,1)} %param.12) | copy-start | bytes 1572868
  16.1 12.3 %all-to-all-start.2 = ((bf16[8,2,128,128]{3,2,1,0:T(8,128)(2,1)}), bf16[8,2,128,128]{3,2,1,0:T(8,128)(2,1)S(1)}, u32[]{:S(2)}, u32[]{:S(2)}) async-start(bf16[8,2,128,128]{3,2,1,0:T(8,128)(2,1)} %bitcast_bitcast_fusion.2), calls=%async_computation.2 | async-start | bytes 1048576 | tf_op jit(solution)/shard_map/all_to_all | solution.py:333
  28.4 12.3 %all-to-all-start.3 = ((bf16[8,2,128,128]{3,2,1,0:T(8,128)(2,1)}), bf16[8,2,128,128]{3,2,1,0:T(8,128)(2,1)S(1)}, u32[]{:S(2)}, u32[]{:S(2)}) async-start(bf16[8,2,128,128]{3,2,1,0:T(8,128)(2,1)} %bitcast_bitcast_fusion.1), calls=%async_computation.3 | async-start | bytes 1048576 | tf_op jit(solution)/shard_map/all_to_all | solution.py:333
  31.9 0.7 copy-start.5
  32.7 0.7 copy-start.6
  33.5 0.7 copy-start.7
  34.2 0.7 copy-start.8
  35.1 0.7 copy-start.1
  41.3 12.5 %collective-permute-start.12 = (bf16[10,128,128]{2,1,0:T(8,128)(2,1)S(1)}, bf16[10,128,128]{2,1,0:T(8,128)(2,1)S(1)}, u32[]{:S(2)}, u32[]{:S(2)}) collective-permute-start(bf16[10,128,128]{2,1,0:T(8,128)(2,1)S(1)} %get-tuple-element.38), channel_id=1, source_target_pairs={{8,0},{10,2},{12,4},{14,6},{16,8},{18,10},{20,12},{22,14},{24,16},... | collective-permute-start | bytes 983048 | tf_op jit(solution)/shard_map/cond/branch_1_fun/ppermute | solution.py:349
  42.6 12.5 %collective-permute-start.14 = (bf16[10,128,128]{2,1,0:T(8,128)(2,1)S(1)}, bf16[10,128,128]{2,1,0:T(8,128)(2,1)S(1)}, u32[]{:S(2)}, u32[]{:S(2)}) collective-permute-start(bf16[10,128,128]{2,1,0:T(8,128)(2,1)S(1)} %get-tuple-element.40), channel_id=1, source_target_pairs={{0,8},{2,10},{4,12},{6,14},{8,16},{10,18},{12,20},{14,22},{16,24},... | collective-permute-start | bytes 983048 | tf_op jit(solution)/shard_map/cond/branch_1_fun/ppermute | solution.py:349
  47.9 14.4 %collective-permute-start.13 = (bf16[10,128,128]{2,1,0:T(8,128)(2,1)S(1)}, bf16[10,128,128]{2,1,0:T(8,128)(2,1)S(1)}, u32[]{:S(2)}, u32[]{:S(2)}) collective-permute-start(bf16[10,128,128]{2,1,0:T(8,128)(2,1)S(1)} %get-tuple-element.39), channel_id=1, source_target_pairs={{8,0},{10,2},{12,4},{14,6},{16,8},{18,10},{20,12},{22,14},{24,16},... | collective-permute-start | bytes 983048 | tf_op jit(solution)/shard_map/cond/branch_1_fun/ppermute | solution.py:349
  49.2 13.2 %collective-permute-start.16 = (bf16[10,128,128]{2,1,0:T(8,128)(2,1)S(1)}, bf16[10,128,128]{2,1,0:T(8,128)(2,1)S(1)}, u32[]{:S(2)}, u32[]{:S(2)}) collective-permute-start(bf16[10,128,128]{2,1,0:T(8,128)(2,1)S(1)} %get-tuple-element.42), channel_id=1, source_target_pairs={{0,8},{2,10},{4,12},{6,14},{8,16},{10,18},{12,20},{14,22},{16,24},... | collective-permute-start | bytes 983048 | tf_op jit(solution)/shard_map/cond/branch_1_fun/ppermute | solution.py:349
  56.0 13.1 %collective-permute-start.15 = (bf16[10,128,128]{2,1,0:T(8,128)(2,1)S(1)}, bf16[10,128,128]{2,1,0:T(8,128)(2,1)S(1)}, u32[]{:S(2)}, u32[]{:S(2)}) collective-permute-start(bf16[10,128,128]{2,1,0:T(8,128)(2,1)S(1)} %get-tuple-element.41), channel_id=1, source_target_pairs={{8,0},{10,2},{12,4},{14,6},{16,8},{18,10},{20,12},{22,14},{24,16},... | collective-permute-start | bytes 983048 | tf_op jit(solution)/shard_map/cond/branch_1_fun/ppermute | solution.py:349
  57.3 11.8 %collective-permute-start.18 = (bf16[10,128,128]{2,1,0:T(8,128)(2,1)S(1)}, bf16[10,128,128]{2,1,0:T(8,128)(2,1)S(1)}, u32[]{:S(2)}, u32[]{:S(2)}) collective-permute-start(bf16[10,128,128]{2,1,0:T(8,128)(2,1)S(1)} %get-tuple-element.44), channel_id=1, source_target_pairs={{0,8},{2,10},{4,12},{6,14},{8,16},{10,18},{12,20},{14,22},{16,24},... | collective-permute-start | bytes 983048 | tf_op jit(solution)/shard_map/cond/branch_1_fun/ppermute | solution.py:349
  63.2 12.7 %collective-permute-start.17 = (bf16[10,128,128]{2,1,0:T(8,128)(2,1)S(1)}, bf16[10,128,128]{2,1,0:T(8,128)(2,1)S(1)}, u32[]{:S(2)}, u32[]{:S(2)}) collective-permute-start(bf16[10,128,128]{2,1,0:T(8,128)(2,1)S(1)} %get-tuple-element.43), channel_id=1, source_target_pairs={{8,0},{10,2},{12,4},{14,6},{16,8},{18,10},{20,12},{22,14},{24,16},... | collective-permute-start | bytes 983048 | tf_op jit(solution)/shard_map/cond/branch_1_fun/ppermute | solution.py:349
  64.5 12.0 %collective-permute-start.20 = (bf16[10,128,128]{2,1,0:T(8,128)(2,1)S(1)}, bf16[10,128,128]{2,1,0:T(8,128)(2,1)S(1)}, u32[]{:S(2)}, u32[]{:S(2)}) collective-permute-start(bf16[10,128,128]{2,1,0:T(8,128)(2,1)S(1)} %get-tuple-element.46), channel_id=1, source_target_pairs={{0,8},{2,10},{4,12},{6,14},{8,16},{10,18},{12,20},{14,22},{16,24},... | collective-permute-start | bytes 983048 | tf_op jit(solution)/shard_map/cond/branch_1_fun/ppermute | solution.py:349
  70.0 13.7 %collective-permute-start.19 = (bf16[10,128,128]{2,1,0:T(8,128)(2,1)S(1)}, bf16[10,128,128]{2,1,0:T(8,128)(2,1)S(1)}, u32[]{:S(2)}, u32[]{:S(2)}) collective-permute-start(bf16[10,128,128]{2,1,0:T(8,128)(2,1)S(1)} %get-tuple-element.45), channel_id=1, source_target_pairs={{8,0},{10,2},{12,4},{14,6},{16,8},{18,10},{20,12},{22,14},{24,16},... | collective-permute-start | bytes 983048 | tf_op jit(solution)/shard_map/cond/branch_1_fun/ppermute | solution.py:349
  71.3 12.5 %collective-permute-start.22 = (bf16[10,128,128]{2,1,0:T(8,128)(2,1)S(1)}, bf16[10,128,128]{2,1,0:T(8,128)(2,1)S(1)}, u32[]{:S(2)}, u32[]{:S(2)}) collective-permute-start(bf16[10,128,128]{2,1,0:T(8,128)(2,1)S(1)} %get-tuple-element.48), channel_id=1, source_target_pairs={{0,8},{2,10},{4,12},{6,14},{8,16},{10,18},{12,20},{14,22},{16,24},... | collective-permute-start | bytes 983048 | tf_op jit(solution)/shard_map/cond/branch_1_fun/ppermute | solution.py:349
  77.4 10.7 %collective-permute-start.21 = (bf16[10,128,128]{2,1,0:T(8,128)(2,1)S(1)}, bf16[10,128,128]{2,1,0:T(8,128)(2,1)S(1)}, u32[]{:S(2)}, u32[]{:S(2)}) collective-permute-start(bf16[10,128,128]{2,1,0:T(8,128)(2,1)S(1)} %get-tuple-element.47), channel_id=1, source_target_pairs={{8,0},{10,2},{12,4},{14,6},{16,8},{18,10},{20,12},{22,14},{24,16},... | collective-permute-start | bytes 983048 | tf_op jit(solution)/shard_map/cond/branch_1_fun/ppermute | solution.py:349
  78.7 10.5 %collective-permute-start.23 = (bf16[10,128,128]{2,1,0:T(8,128)(2,1)S(1)}, bf16[10,128,128]{2,1,0:T(8,128)(2,1)S(1)}, u32[]{:S(2)}, u32[]{:S(2)}) collective-permute-start(bf16[10,128,128]{2,1,0:T(8,128)(2,1)S(1)} %get-tuple-element.49), channel_id=1, source_target_pairs={{0,8},{2,10},{4,12},{6,14},{8,16},{10,18},{12,20},{14,22},{16,24},... | collective-permute-start | bytes 983048 | tf_op jit(solution)/shard_map/cond/branch_1_fun/ppermute | solution.py:349
  127.2 0.8 copy-start.4

commit v3 on v2

v3 whole, which is shorter than its diff:
```python
import functools
import math

import jax
import jax.numpy as jnp
from jax import lax
from jax.experimental import pallas as pl
from jax.experimental.pallas import tpu as pltpu
from jax.sharding import PartitionSpec as P

HEADS = 16
HEAD_DIM = 64
BLOCK = 128
FRAMES_DEV = 2
ENTRIES = 6
SPAN = 4


def plan_kernel(
    me_ref, ref_ref, dev_hbm, place_hbm, block_hbm, valid_hbm, out_ref, entries, sems,
    *, inner, n_tok, rounds, room,
):
    copies = [
        pltpu.make_async_copy(array, entries.at[index], sems.at[index])
        for index, array in enumerate((dev_hbm, place_hbm, block_hbm, valid_hbm))
    ]
    for copy in copies:
        copy.start()
    for copy in copies:
        copy.wait()
    n_frames = dev_hbm.shape[0]
    units = inner * n_tok * FRAMES_DEV
    plane_frames = inner * FRAMES_DEV
    n_outer = n_frames // plane_frames
    lanes = out_ref.shape[1]
    f32 = jnp.float32
    me = me_ref[0].astype(f32)
    dev, place = entries[0], entries[1]
    ids = (dev // inner) * units + ((dev % inner) * n_tok + entries[2]) * FRAMES_DEV + place
    used = entries[3] > 0
    frame_lane = lax.broadcasted_iota(jnp.int32, (n_frames, lanes), 1)
    hit = jnp.zeros((n_frames, lanes), f32)
    for entry in range(ENTRIES):
        here = (ids[:, entry : entry + 1] == frame_lane) & used[:, entry : entry + 1]
        hit = jnp.where(here, 1.0, hit)
    lane = lax.broadcasted_iota(jnp.int32, (1, lanes), 1)
    unit = lane % units
    origin = (lane // units).astype(f32)
    need = []
    for plane in range(n_outer):
        rows = lax.slice_in_dim(hit, plane * plane_frames, (plane + 1) * plane_frames)
        wanted = jnp.max(rows, axis=0, keepdims=True) > 0
        if inner % SPAN:
            group = plane * inner // SPAN
            ref_frame = group * (SPAN * FRAMES_DEV) + ref_ref[group]
            ref_dev = ref_frame // FRAMES_DEV
            wanted = wanted | (
                (lane // (n_tok * FRAMES_DEV) == ref_dev)
                & (lane % FRAMES_DEV == ref_frame % FRAMES_DEV)
            )
        need.append(wanted)

    square_row = lax.broadcasted_iota(jnp.int32, (lanes, lanes), 0)
    square_lane = lax.broadcasted_iota(jnp.int32, (lanes, lanes), 1)
    diagonal = square_row == square_lane
    earlier = square_row < square_lane

    def column(row):
        return jnp.sum(jnp.where(diagonal, row, 0.0), axis=1, keepdims=True)

    def count(mask, axis):
        return jnp.sum(jnp.where(mask, 1.0, 0.0), axis=axis, keepdims=True)

    def one_way(start, reach, here):
        start_col, reach_col = column(start), column(reach)
        ahead = (reach_col > reach) | ((reach_col == reach) & earlier)
        rank = count((start_col == start) & (reach_col > 0) & ahead, 0)
        depart = jnp.zeros_like(start)
        for plane in range(n_outer - 1, 0, -1):
            total = jnp.zeros((1, 1), f32)
            turn = jnp.ones_like(start)
            for step in range(1, rounds + 1):
                if plane < n_outer - 1:
                    passing = (
                        (start > plane)
                        & (start - reach <= plane - 1)
                        & (depart + (start - plane) == step)
                        & (reach > 0)
                    )
                    total = total + (room - count(passing, 1))
                else:
                    total = total + room
                turn = turn + jnp.where(total <= rank, 1.0, 0.0)
            depart = jnp.where((start == plane) & (reach > 0), turn, depart)
        last = jnp.max(jnp.where(reach > 0, depart + reach - 1.0, 0.0), axis=1, keepdims=True)

        def on_link(link):
            crosses = (reach > 0) & (start > link) & (start - reach <= link)
            step = jnp.where(crosses, depart + (start - 1.0 - link), -1.0)
            slot = count((column(step) == step) & earlier, 0)
            return crosses, step, slot

        arrives, in_step, in_slot = on_link(here)
        leaves, out_step, out_slot = on_link(here - 1.0)
        source = jnp.where(start == here, unit.astype(f32), units + in_slot)
        key = column(jnp.where(leaves, (out_step - 1.0) * room + out_slot, -1.0))
        sent = jnp.sum(
            jnp.where(key == square_lane.astype(f32), column(source), 0.0), axis=0, keepdims=True
        )
        return arrives, in_step, in_slot, sent, last

    lowest, highest = origin, origin
    for plane in range(n_outer):
        highest = jnp.where(need[plane] & (origin < plane), float(plane), highest)
        other = n_outer - 1 - plane
        lowest = jnp.where(need[other] & (origin > other), float(other), lowest)
    top = n_outer - 1.0
    down = one_way(origin, origin - lowest, me)
    up = one_way(top - origin, highest - origin, top - me)
    unit_f = unit.astype(f32)
    spots = unit_f
    for way, (arrives, in_step, in_slot, _, _) in enumerate((down, up)):
        spots = jnp.where(arrives, (in_step + way * rounds) * 1024 + in_slot, spots)
    distance = origin - me
    full = jnp.where(distance > 0, distance, jnp.where(distance < 0, n_outer - 1 - distance, 0))
    last = jnp.maximum(down[4], up[4]) + jnp.zeros_like(origin)
    full = full * 1024 + unit_f
    first = me * plane_frames
    row_frame = lax.broadcasted_iota(jnp.int32, (n_frames, lanes), 0).astype(f32)
    wide_lane = frame_lane.astype(f32)
    group = me_ref[0] * inner // SPAN
    ref_frame = group * (SPAN * FRAMES_DEV) + ref_ref[group]
    ref_dev = ref_frame // FRAMES_DEV

    def places(table):
        listed = jnp.zeros((1, lanes), f32)
        for entry in range(ENTRIES):
            mine, live = ids[:, entry : entry + 1], used[:, entry : entry + 1]
            found = jnp.sum(jnp.where(mine == frame_lane, table, 0.0), axis=1, keepdims=True)
            found = jnp.where(live, found, 65536.0)
            target = (row_frame - first) * 8 + entry
            listed += jnp.sum(jnp.where(target == wide_lane, found, 0.0), axis=0, keepdims=True)
        listed = jnp.where(lane % 8 < ENTRIES, listed, 65536.0)
        refs = jnp.zeros((1, lanes), f32)
        for block in range(n_tok):
            which = (ref_dev * n_tok + block) * FRAMES_DEV + ref_frame % FRAMES_DEV
            found = jnp.sum(jnp.where(lane == which, table, 0.0), axis=1, keepdims=True)
            refs = jnp.where(lane == block, found, refs)
        return [listed, refs]

    last = jnp.maximum(down[4], up[4]) + jnp.zeros_like(origin)
    rows = [down[3], up[3], last] + places(spots) + places(full)
    for index, row in enumerate(rows):
        out_ref[index : index + 1, :] = row.astype(jnp.int32)


def make_plan(epi_dev, epi_frame, epi_block, valid, ref_local, my_outer, inner, n_tok, rounds, room):
    n_blocks = epi_dev.shape[0] * n_tok
    lanes = -(-n_blocks // 128) * 128
    smem, anywhere = pl.BlockSpec(memory_space=pltpu.SMEM), pl.BlockSpec(memory_space=pl.ANY)
    return pl.pallas_call(
        functools.partial(plan_kernel, inner=inner, n_tok=n_tok, rounds=rounds, room=room),
        out_shape=jax.ShapeDtypeStruct((8, lanes), jnp.int32),
        in_specs=[smem, smem] + [anywhere] * 4,
        out_specs=pl.BlockSpec(memory_space=pltpu.VMEM),
        scratch_shapes=[
            pltpu.VMEM((4,) + epi_dev.shape, jnp.int32),
            pltpu.SemaphoreType.DMA((4,)),
        ],
        compiler_params=pltpu.CompilerParams(vmem_limit_bytes=32 * 1024 * 1024),
    )(my_outer.reshape(1), ref_local, epi_dev, epi_frame, epi_block, valid)


def pack_kernel(plan_ref, *refs, step, room, units):
    sources, targets = refs[:-2], refs[-2:]
    own = sources[0]
    for way, target in enumerate(targets):
        for slot in range(room):
            code = plan_ref[way, (step - 1) * room + slot]
            if step == 1:
                target[slot] = own[code, 1:3]
            else:

                @pl.when(code < units)
                def _():
                    target[slot] = own[code, 1:3]

                @pl.when(code >= units)
                def _():
                    target[slot] = sources[1 + way][code - units]


def pack(plan, own, previous, step, room):
    out = jax.ShapeDtypeStruct((room, 2) + own.shape[2:], own.dtype)
    whole = pl.BlockSpec(memory_space=pltpu.VMEM)
    return pl.pallas_call(
        functools.partial(pack_kernel, step=step, room=room, units=own.shape[0]),
        out_shape=(out, out),
        grid_spec=pltpu.PrefetchScalarGridSpec(
            num_scalar_prefetch=1,
            grid=(),
            in_specs=[whole] * (1 + len(previous)),
            out_specs=(whole, whole),
        ),
        compiler_params=pltpu.CompilerParams(vmem_limit_bytes=24 * 1024 * 1024),
        cost_estimate=pl.CostEstimate(
            flops=0, bytes_accessed=8 * math.prod(out.shape), transcendentals=0
        ),
    )(plan, own, *previous)


def fold(keys, values, query, acc, stat, fresh):
    width, tile = acc.shape
    scores = jnp.dot(keys, query, preferred_element_type=jnp.float32)
    top = jnp.max(scores, axis=0, keepdims=True)
    if not fresh:
        old_top = stat[0:1]
        top = jnp.maximum(old_top, top)
    weights = jnp.exp(scores - top)
    total = jnp.sum(weights, axis=0, keepdims=True)
    weights = weights.astype(jnp.bfloat16)
    if not fresh:
        keep = jnp.exp(old_top - top)
        total = stat[1:2] * keep + total
    stat[0:1] = top
    stat[1:2] = total
    channels = values.T
    for head in range(width // HEAD_DIM):
        rows, lanes = pl.ds(head * HEAD_DIM, HEAD_DIM), slice(head * tile, (head + 1) * tile)
        attended = jnp.dot(
            channels[head * HEAD_DIM : (head + 1) * HEAD_DIM],
            weights[:, lanes],
            preferred_element_type=jnp.float32,
        )
        acc[rows] = attended if fresh else acc[rows] * keep[:, lanes] + attended


def listed_items(plan_ref, sources, block_set, query_ref, acc_ref, stat_ref, spot_row, n_refs):
    n_local, n_tiles = acc_ref.shape[:2]

    def item(local, code):
        spot, origin = code & 1023, code >> 10
        for number, (source, first) in sources.items():

            @pl.when(origin == number)
            def _():
                block_set[...] = source[spot, first : first + 2]

        hit = functools.reduce(jnp.logical_or, [origin == number for number in sources])

        @pl.when(hit)
        def _():
            for tile in range(n_tiles):
                fold(
                    block_set[0], block_set[1], query_ref[local, tile], acc_ref.at[local, tile],
                    stat_ref.at[local, tile], False,
                )

    @pl.loop(0, n_local * 8)
    def _(index):
        item(index >> 3, plan_ref[spot_row, index])

    if n_refs:

        @pl.loop(0, n_local * n_refs)
        def _(index):
            item(lax.div(index, n_refs), plan_ref[spot_row + 1, lax.rem(index, n_refs)])


def near_kernel(plan_ref, own_ref, query_ref, acc_ref, stat_ref, block_set, *, n_tok, spot_row, ref_near):
    n_local, n_tiles, width, tile = acc_ref.shape
    heads = width // HEAD_DIM
    row_head = lax.broadcasted_iota(jnp.int32, (width, 1), 0) // HEAD_DIM

    @pl.loop(0, n_local, unroll=2)
    def _(local):
        base = (local // FRAMES_DEV) * (n_tok * FRAMES_DEV) + local % FRAMES_DEV
        spots = [base + block * FRAMES_DEV for block in range(n_tok)]
        blocks = [own_ref.at[spot] for spot in spots]
        if ref_near:
            blocks += [own_ref.at[plan_ref[spot_row + 1, block]] for block in range(n_tok)]
        keys = jnp.concatenate([block[1] for block in blocks], 0)
        values = jnp.concatenate([block[2] for block in blocks], 0)
        for index in range(n_tiles):
            first = index * tile // BLOCK
            turned = jnp.concatenate(
                [own_ref[spot, 0].T for spot in spots[first : first + tile // BLOCK]], 1
            )
            turned = turned * jnp.asarray(HEAD_DIM**-0.5, turned.dtype)
            query = jnp.concatenate(
                [jnp.where(row_head == head, turned, jnp.zeros_like(turned)) for head in range(heads)],
                1,
            )
            query_ref[local, index] = query
            fold(keys, values, query, acc_ref.at[local, index], stat_ref.at[local, index], True)

    listed_items(
        plan_ref, {0: (own_ref, 1)}, block_set, query_ref, acc_ref, stat_ref, spot_row,
        0 if ref_near else n_tok,
    )


def near(plan, own, n_local, n_tok, spot_row, ref_near):
    width = own.shape[-1]
    rows = n_tok * BLOCK
    tile = math.gcd(rows, 256)
    lanes = tile * (width // HEAD_DIM)
    whole = pl.BlockSpec(memory_space=pltpu.VMEM)
    pairs = n_local * rows * (1 + ref_near) * rows
    return pl.pallas_call(
        functools.partial(near_kernel, n_tok=n_tok, spot_row=spot_row, ref_near=ref_near),
        out_shape=(
            jax.ShapeDtypeStruct((n_local, rows // tile, width, lanes), own.dtype),
            jax.ShapeDtypeStruct((n_local, rows // tile, width, tile), jnp.float32),
            jax.ShapeDtypeStruct((n_local, rows // tile, 2, lanes), jnp.float32),
        ),
        grid_spec=pltpu.PrefetchScalarGridSpec(
            num_scalar_prefetch=1,
            grid=(),
            in_specs=[whole],
            out_specs=(whole, whole, whole),
            scratch_shapes=[pltpu.VMEM((2, BLOCK, width), own.dtype)],
        ),
        compiler_params=pltpu.CompilerParams(vmem_limit_bytes=40 * 1024 * 1024),
        cost_estimate=pl.CostEstimate(
            flops=4 * pairs * width,
            bytes_accessed=16 * n_local * rows * width,
            transcendentals=pairs * width // HEAD_DIM,
        ),
    )(plan, own)


def stage_kernel(
    plan_ref, down_ref, up_ref, query_ref, acc_in, stat_in, acc_ref, *refs, numbers, spot_row, n_refs, final
):
    stat_ref, block_set = refs[-2:]
    if final:
        out_ref, acc_ref = acc_ref, refs[0]
    sources = {numbers[0]: (down_ref, 0), numbers[1]: (up_ref, 0)}
    listed_items(plan_ref, sources, block_set, query_ref, acc_ref, stat_ref, spot_row, n_refs)
    if not final:
        return
    n_local, n_tiles, width, tile = acc_ref.shape
    n_tok = n_tiles * tile // BLOCK
    row_head = lax.broadcasted_iota(jnp.int32, (width, 1), 0) // HEAD_DIM

    @pl.loop(0, n_local, unroll=2)
    def _(local):
        for index in range(n_tiles):
            total = stat_ref[local, index][1:2]
            share = 1.0 / total[:, :tile]
            for head in range(1, width // HEAD_DIM):
                other = 1.0 / total[:, head * tile : (head + 1) * tile]
                share = jnp.where(row_head == head, other, share)
            result = (acc_ref[local, index] * share).T.astype(out_ref.dtype)
            for block in range(tile // BLOCK):
                rank = (local // FRAMES_DEV) * n_tok + index * (tile // BLOCK) + block
                out_ref[rank, local % FRAMES_DEV] = result[block * BLOCK : (block + 1) * BLOCK]


def stage(plan, received, query, acc, stat, numbers, n_ranks, spot_row, n_refs, final):
    width = acc.shape[2]
    whole = pl.BlockSpec(memory_space=pltpu.VMEM)
    out_shape = [jax.ShapeDtypeStruct(x.shape, x.dtype) for x in (acc, stat)]
    if final:
        out_shape = [
            jax.ShapeDtypeStruct((n_ranks, FRAMES_DEV, BLOCK, width), query.dtype)
        ] + out_shape
    pairs = 2 * acc.size // width * BLOCK
    return pl.pallas_call(
        functools.partial(
            stage_kernel, numbers=numbers, spot_row=spot_row, n_refs=n_refs, final=final
        ),
        out_shape=out_shape,
        grid_spec=pltpu.PrefetchScalarGridSpec(
            num_scalar_prefetch=1,
            grid=(),
            in_specs=[whole] * 5,
            out_specs=[whole] * len(out_shape),
            scratch_shapes=[pltpu.VMEM((2, BLOCK, width), query.dtype)],
        ),
        input_output_aliases={4: len(out_shape) - 2, 5: len(out_shape) - 1},
        compiler_params=pltpu.CompilerParams(vmem_limit_bytes=40 * 1024 * 1024),
        cost_estimate=pl.CostEstimate(
            flops=4 * pairs * width,
            bytes_accessed=8 * acc.size,
            transcendentals=pairs * width // HEAD_DIM,
        ),
    )(plan, *received, query, acc, stat)


def shards(queries, keys, values, epi_dev, epi_frame, epi_block, valid, ref_local, *, n_tm, n_tok):
    inner = math.gcd(SPAN, max(1, HEADS // n_tok))
    n_outer = n_tm // inner
    n_ranks = inner * n_tok
    units = n_ranks * FRAMES_DEV
    width = keys.shape[2] // n_ranks
    rounds, room = n_outer - 1, -(-units * 5 // 8)
    ref_near = inner % SPAN == 0
    plane_groups = [
        [(o * inner + i) * n_tok + t for i in range(inner) for t in range(n_tok)]
        for o in range(n_outer)
    ]

    def exchange(x):
        return lax.all_to_all(
            x, ("tm", "tok"), 0, 0, axis_index_groups=plane_groups, tiled=True
        )

    def shift(x, way):
        pairs = [
            (o * inner + i, (o + way) * inner + i)
            for o in range(n_outer)
            for i in range(inner)
            if 0 <= o + way < n_outer
        ]
        return lax.ppermute(x, "tm", pairs)

    my_outer = (lax.axis_index("tm") // inner).astype(jnp.int32)
    plan = make_plan(
        epi_dev, epi_frame, epi_block, valid, ref_local, my_outer, inner, n_tok, rounds, room
    )
    three = jnp.stack([queries, keys, values]).reshape(3, FRAMES_DEV, BLOCK, n_ranks, width)
    own = exchange(three.transpose(3, 1, 0, 2, 4)).reshape(units, 3, BLOCK, width)
    n_local = inner * FRAMES_DEV
    n_refs = 0 if ref_near else n_tok

    def passed(own, spot_row, send):
        received = None
        for step in range(1, rounds + 1):
            arriving = [shift(sent, 2 * way - 1) for way, sent in enumerate(send(own, received, step))]
            if step == 1:
                query, acc, stat = near(plan, own, n_local, n_tok, spot_row, ref_near)
            else:
                numbers = (step - 1, rounds + step - 1)
                acc, stat = stage(
                    plan, received, query, acc, stat, numbers, n_ranks, spot_row, n_refs, False
                )
            own, acc = lax.optimization_barrier((own, acc))
            received = arriving
        numbers = (rounds, 2 * rounds)
        return stage(plan, received, query, acc, stat, numbers, n_ranks, spot_row, n_refs, True)[0]

    def listed(own):
        return passed(own, 3, lambda own, got, step: pack(plan, own, got or [], step, room))

    def gathered(own):
        return passed(own, 5, lambda own, got, step: got or [own[:, 1:3]] * 2)

    attended = exchange(lax.cond(plan[2, 0] <= rounds, listed, gathered, own))
    return attended.transpose(1, 2, 0, 3).reshape(queries.shape)


def solution(mesh):
    return jax.shard_map(
        functools.partial(shards, n_tm=mesh.shape["tm"], n_tok=mesh.shape["tok"]),
        mesh=mesh,
        in_specs=(P("tm", "tok", None),) * 3 + (P(),) * 5,
        out_specs=P("tm", "tok", None),
        check_vma=False,
    )
```

time: 129 us -> 109 us (0.84); the launches traced: 128 us -> 107 us
  starting transfers between devices: 48.4 us -> 23.9 us
  waiting for transfers between devices: 25.4 us -> 32.3 us
  local copies, waits for them, and re-layouts: 9.22 us -> 4.14 us
  other arithmetic: 0 us -> 1.35 us
    ppermute x12 -> x6, starting transfers between devices: 36.1 us -> 18.6 us  [shift(): return lax.ppermute(x, 'tm', pairs)]
    ppermute x12 -> x6, waiting for transfers between devices: 7.43 us -> 15.5 us  [shift(): return lax.ppermute(x, 'tm', pairs)]
    all_to_all x3 -> x1, starting transfers between devices: 12.3 us -> 5.31 us  [exchange(): lax.all_to_all(x, ('tm', 'tok'), 0, 0, axis_index_groups=plane_groups, ti...]
    transpose x3 -> x0, local copies, waits for them, and re-layouts: 2.82 us -> none  [to_heads(): x.reshape(FRAMES_DEV, BLOCK, n_ranks, width).transpose(2, 0, 1, 3)]
    unnamed x22 -> x21, local copies, waits for them, and re-layouts: 5.26 us -> 2.47 us
    pallas_call x6 -> x3, Pallas kernels: 4.78 us -> 2.51 us  [pack(): pl.pallas_call(functools.partial(pack_kernel, step=step, room=room, units...]
    pallas_call x1 -> x4, Pallas kernels: 26.5 us -> 28.3 us  [the longest x3 17.7 us: stage(): pl.pallas_call(functools.partial(stage_kernel, numbers=numbers, spot_row=...]
    transpose x0 -> x1, other arithmetic: none -> 1.35 us  [shards(): three.transpose(3, 1, 0, 2, 4)]
  transfers between devices with their start and end apart: 15 -> 7, of which waited for: 9 -> 7; matrix products, arithmetic and copies ran while one was open for 3% -> 1% of each run, Pallas kernels for 4% -> 24%
where the time goes in v3:
time: 109 us; the launch traced here: 107 us
  Pallas kernels  32.5 us (30%)
  waiting for transfers between devices  32.3 us (30%)
  starting transfers between devices  23.9 us (22%)
  blocking collectives  11.5 us (11%)
  local copies, waits for them, and re-layouts  4.14 us (4%)
  other arithmetic  1.35 us (1%)
    ppermute x6, starting transfers between devices, shift(): return lax.ppermute(x, 'tm', pairs)  18.6 us
    pallas_call x3, Pallas kernels, stage(): pl.pallas_call(functools.partial(stage_kernel, numbers=numbers, spot_row=...  17.7 us
    all_to_all x1, waiting for transfers between devices, exchange(): lax.all_to_all(x, ('tm', 'tok'), 0, 0, axis_index_groups=plane_groups, ti...  16.9 us
    ppermute x6, waiting for transfers between devices, shift(): return lax.ppermute(x, 'tm', pairs)  15.5 us
    all_to_all x1, blocking collectives, exchange(): lax.all_to_all(x, ('tm', 'tok'), 0, 0, axis_index_groups=plane_groups, ti...  11.5 us
    pallas_call x1, Pallas kernels, near(): pl.pallas_call(functools.partial(near_kernel, n_tok=n_tok, spot_row=spot_...  10.6 us
    all_to_all x1, starting transfers between devices, exchange(): lax.all_to_all(x, ('tm', 'tok'), 0, 0, axis_index_groups=plane_groups, ti...  5.31 us
    pallas_call x3, Pallas kernels, pack(): pl.pallas_call(functools.partial(pack_kernel, step=step, room=room, units...  2.51 us
  transfers between devices with their start and end apart: 7, of which 7 were waited for; matrix products, arithmetic and copies ran while one was open for 1% of the time, Pallas kernels for 24%

profile of v3, /device:TPU:0, one launch (start us, length us, event | category | flops | bytes accessed | tf_op | source)
XLA Modules:
  0.0 106.7 jit_solution(5979392930716228903)
XLA Ops:
  0.0 1.2 %copy.30 = bf16[32,8,8,128]{3,2,1,0:T(8,128)(2,1)S(1)} copy(bf16[32,8,8,128]{3,1,2,0:T(8,128)(2,1)} %bitcast.28) | data formatting | bytes 1048576
  2.5 1.3 %maximum_bitcast_fusion = bf16[8,2,3,128,128]{4,3,2,1,0:T(8,128)(2,1)} fusion(bf16[1,2,128,8,128]{4,2,0,1,3:T(8,128)(2,1)S(1)} %copy.27, bf16[1,2,128,8,128]{4,2,0,1,3:T(8,128)(2,1)S(1)} %copy.26, bf16[1,2,128,8,128]{4,2,0,1,3:T(8,128)(2,1)S(1)} %copy.25), kind=kLoop, calls=%fused_computation | loop fusion | flops 1572864 | bytes 3145728 | tf_op jit(solution)/shard_map/transpose | solution.py:424
  3.8 5.3 %all-to-all-start = ((bf16[8,2,3,128,128]{4,3,2,1,0:T(8,128)(2,1)}), bf16[8,2,3,128,128]{4,3,2,1,0:T(8,128)(2,1)S(1)}, u32[]{:S(2)}, u32[]{:S(2)}) async-start(bf16[8,2,3,128,128]{4,3,2,1,0:T(8,128)(2,1)} %maximum_bitcast_fusion), calls=%async_computation | async-start | bytes 3145728 | tf_op jit(solution)/shard_map/all_to_all | solution.py:406
  9.5 1.8 %shard_map.82 = s32[8,128]{1,0:T(8,128)S(1)} custom-call(s32[1]{0:T(128)} %bitcast.me_ref, s32[4]{0:T(128)S(1)} %copy-done, s32[32,6]{1,0:T(8,128)S(1)} %copy.21.dev_hbm, s32[32,6]{1,0:T(8,128)S(1)} %copy.22.place_hbm, s32[32,6]{1,0:T(8,128)S(1)} %copy.23.block_hbm, s32[32,6]{1,0:T(8,128)S(1)} %copy.24.valid_hbm), custom_call_target="tpu_custom_call" | custom-call | tf_op jit(solution)/shard_map/pallas_call | solution.py:161
  12.4 16.9 %all-to-all-done = bf16[8,2,3,128,128]{4,3,2,1,0:T(8,128)(2,1)S(1)} async-done(((bf16[8,2,3,128,128]{4,3,2,1,0:T(8,128)(2,1)}), bf16[8,2,3,128,128]{4,3,2,1,0:T(8,128)(2,1)S(1)}, u32[]{:S(2)}, u32[]{:S(2)}) %all-to-all-start) | async-done | bytes 1572896 | tf_op jit(solution)/shard_map/all_to_all | solution.py:406
  29.3 64.9 %conditional.1 = (bf16[8,2,128,128]{3,2,1,0:T(8,128)(2,1)S(1)}) conditional(s32[]{:T(128)} %bitcast.1, (bf16[16,3,128,128]{3,2,1,0:T(8,128)(2,1)S(1)}, s32[8,128]{1,0:T(8,128)S(1)}) %tuple.21, (s32[8,128]{1,0:T(8,128)S(1)}, bf16[16,3,128,128]{3,2,1,0:T(8,128)(2,1)S(1)}) %tuple.22), branch_computations={%region_0.1_spmd, %region_1.2_spmd} | conditional | flops 1342177280 | bytes 37748984 | solution.py:450
  30.0 1.3 %collective-permute-start.6 = (bf16[10,2,128,128]{3,2,1,0:T(8,128)(2,1)S(1)}, bf16[10,2,128,128]{3,2,1,0:T(8,128)(2,1)S(1)}, u32[]{:S(2)}, u32[]{:S(2)}) collective-permute-start(bf16[10,2,128,128]{3,2,1,0:T(8,128)(2,1)S(1)} %get-tuple-element.31), channel_id=1, source_target_pairs={{8,0},{10,2},{12,4},{14,6},{16,8},{18,10},{20,12},{22,14},{24,16},... | collective-permute-start | bytes 1966088 | tf_op jit(solution)/shard_map/cond/branch_1_fun/ppermute | solution.py:417
  31.3 4.6 %collective-permute-start.7 = (bf16[10,2,128,128]{3,2,1,0:T(8,128)(2,1)S(1)}, bf16[10,2,128,128]{3,2,1,0:T(8,128)(2,1)S(1)}, u32[]{:S(2)}, u32[]{:S(2)}) collective-permute-start(bf16[10,2,128,128]{3,2,1,0:T(8,128)(2,1)S(1)} %get-tuple-element.32), channel_id=1, source_target_pairs={{0,8},{2,10},{4,12},{6,14},{8,16},{10,18},{12,20},{14,22},{16,24},... | collective-permute-start | bytes 1966088 | tf_op jit(solution)/shard_map/cond/branch_1_fun/ppermute | solution.py:417
  35.9 10.6 %branch_1_fun.7 = (bf16[8,1,128,512]{3,2,1,0:T(8,128)(2,1)S(1)}, f32[8,1,128,256]{3,2,1,0:T(8,128)S(1)}, f32[8,1,2,512]{3,2,1,0:T(2,128)S(1)}) custom-call(s32[8,128]{1,0:T(8,128)S(1)} %get-tuple-element.27.plan_ref, bf16[16,3,128,128]{3,2,1,0:T(8,128)(2,1)S(1)} %get-tuple-element.37.own_ref.refs_0_), custom_call_target="tpu_custom_call" | custom-call | flops 536870912 | bytes 4194304 | tf_op jit(solution)/shard_map/cond/branch_1_fun/pallas_call | solution.py:310
  46.5 2.1 %collective-permute-done.6.down_ref.refs_1_ = bf16[10,2,128,128]{3,2,1,0:T(8,128)(2,1)S(1)} collective-permute-done((bf16[10,2,128,128]{3,2,1,0:T(8,128)(2,1)S(1)}, bf16[10,2,128,128]{3,2,1,0:T(8,128)(2,1)S(1)}, u32[]{:S(2)}, u32[]{:S(2)}) %collective-permute-start.6) | collective-permute-done | bytes 655392 | tf_op jit(solution)/shard_map/cond/branch_1_fun/ppermute | solution.py:417
  48.6 1.2 %collective-permute-done.7.up_ref.refs_2_ = bf16[10,2,128,128]{3,2,1,0:T(8,128)(2,1)S(1)} collective-permute-done((bf16[10,2,128,128]{3,2,1,0:T(8,128)(2,1)S(1)}, bf16[10,2,128,128]{3,2,1,0:T(8,128)(2,1)S(1)}, u32[]{:S(2)}, u32[]{:S(2)}) %collective-permute-start.7) | collective-permute-done | bytes 655392 | tf_op jit(solution)/shard_map/cond/branch_1_fun/ppermute | solution.py:417
  49.7 0.9 branch_1_fun.10
  50.7 1.3 %collective-permute-start.8 = (bf16[10,2,128,128]{3,2,1,0:T(8,128)(2,1)S(1)}, bf16[10,2,128,128]{3,2,1,0:T(8,128)(2,1)S(1)}, u32[]{:S(2)}, u32[]{:S(2)}) collective-permute-start(bf16[10,2,128,128]{3,2,1,0:T(8,128)(2,1)S(1)} %get-tuple-element.38), channel_id=1, source_target_pairs={{8,0},{10,2},{12,4},{14,6},{16,8},{18,10},{20,12},{22,14},{24,16},... | collective-permute-start | bytes 1966088 | tf_op jit(solution)/shard_map/cond/branch_1_fun/ppermute | solution.py:417
  52.0 5.1 %collective-permute-start.9 = (bf16[10,2,128,128]{3,2,1,0:T(8,128)(2,1)S(1)}, bf16[10,2,128,128]{3,2,1,0:T(8,128)(2,1)S(1)}, u32[]{:S(2)}, u32[]{:S(2)}) collective-permute-start(bf16[10,2,128,128]{3,2,1,0:T(8,128)(2,1)S(1)} %get-tuple-element.39), channel_id=1, source_target_pairs={{0,8},{2,10},{4,12},{6,14},{8,16},{10,18},{12,20},{14,22},{16,24},... | collective-permute-start | bytes 1966088 | tf_op jit(solution)/shard_map/cond/branch_1_fun/ppermute | solution.py:417
  57.0 5.9 %branch_1_fun.9 = (f32[8,1,128,256]{3,2,1,0:T(8,128)S(1)}, f32[8,1,2,512]{3,2,1,0:T(2,128)S(1)}) custom-call(s32[8,128]{1,0:T(8,128)S(1)} %get-tuple-element.27.plan_ref, bf16[10,2,128,128]{3,2,1,0:T(8,128)(2,1)S(1)} %collective-permute-done.6.down_ref.refs_1_, ...), custom_call_target="tpu_custom_call", output_to_operand_aliasing={{0}: (4, {}), {1}: (5, {})} | custom-call | flops 268435456 | bytes 2097152 | tf_op jit(solution)/shard_map/cond/branch_1_fun/pallas_call | solution.py:370
  62.9 5.9 %collective-permute-done.8.refs_1_.down_ref = bf16[10,2,128,128]{3,2,1,0:T(8,128)(2,1)S(1)} collective-permute-done((bf16[10,2,128,128]{3,2,1,0:T(8,128)(2,1)S(1)}, bf16[10,2,128,128]{3,2,1,0:T(8,128)(2,1)S(1)}, u32[]{:S(2)}, u32[]{:S(2)}) %collective-permute-start.8) | collective-permute-done | bytes 655392 | tf_op jit(solution)/shard_map/cond/branch_1_fun/ppermute | solution.py:417
  68.8 1.2 %collective-permute-done.9.refs_2_.up_ref = bf16[10,2,128,128]{3,2,1,0:T(8,128)(2,1)S(1)} collective-permute-done((bf16[10,2,128,128]{3,2,1,0:T(8,128)(2,1)S(1)}, bf16[10,2,128,128]{3,2,1,0:T(8,128)(2,1)S(1)}, u32[]{:S(2)}, u32[]{:S(2)}) %collective-permute-start.9) | collective-permute-done | bytes 655392 | tf_op jit(solution)/shard_map/cond/branch_1_fun/ppermute | solution.py:417
  70.9 1.3 %collective-permute-start.10 = (bf16[10,2,128,128]{3,2,1,0:T(8,128)(2,1)S(1)}, bf16[10,2,128,128]{3,2,1,0:T(8,128)(2,1)S(1)}, u32[]{:S(2)}, u32[]{:S(2)}) collective-permute-start(bf16[10,2,128,128]{3,2,1,0:T(8,128)(2,1)S(1)} %get-tuple-element.40), channel_id=1, source_target_pairs={{8,0},{10,2},{12,4},{14,6},{16,8},{18,10},{20,12},{22,14},{24,16},... | collective-permute-start | bytes 1966088 | tf_op jit(solution)/shard_map/cond/branch_1_fun/ppermute | solution.py:417
  72.2 5.1 %collective-permute-start.11 = (bf16[10,2,128,128]{3,2,1,0:T(8,128)(2,1)S(1)}, bf16[10,2,128,128]{3,2,1,0:T(8,128)(2,1)S(1)}, u32[]{:S(2)}, u32[]{:S(2)}) collective-permute-start(bf16[10,2,128,128]{3,2,1,0:T(8,128)(2,1)S(1)} %get-tuple-element.41), channel_id=1, source_target_pairs={{0,8},{2,10},{4,12},{6,14},{8,16},{10,18},{12,20},{14,22},{16,24},... | collective-permute-start | bytes 1966088 | tf_op jit(solution)/shard_map/cond/branch_1_fun/ppermute | solution.py:417
  77.3 6.9 %branch_1_fun.12 = (f32[8,1,128,256]{3,2,1,0:T(8,128)S(1)}, f32[8,1,2,512]{3,2,1,0:T(2,128)S(1)}) custom-call(s32[8,128]{1,0:T(8,128)S(1)} %get-tuple-element.27.plan_ref, bf16[10,2,128,128]{3,2,1,0:T(8,128)(2,1)S(1)} %collective-permute-done.8.refs_1_.down_ref, ...), custom_call_target="tpu_custom_call", output_to_operand_aliasing={{0}: (4, {}), {1}: (5, {})} | custom-call | flops 268435456 | bytes 2097152 | tf_op jit(solution)/shard_map/cond/branch_1_fun/pallas_call | solution.py:370
  84.2 3.9 %collective-permute-done.10.down_ref = bf16[10,2,128,128]{3,2,1,0:T(8,128)(2,1)S(1)} collective-permute-done((bf16[10,2,128,128]{3,2,1,0:T(8,128)(2,1)S(1)}, bf16[10,2,128,128]{3,2,1,0:T(8,128)(2,1)S(1)}, u32[]{:S(2)}, u32[]{:S(2)}) %collective-permute-start.10) | collective-permute-done | bytes 655392 | tf_op jit(solution)/shard_map/cond/branch_1_fun/ppermute | solution.py:417
  88.1 1.2 %collective-permute-done.11.up_ref = bf16[10,2,128,128]{3,2,1,0:T(8,128)(2,1)S(1)} collective-permute-done((bf16[10,2,128,128]{3,2,1,0:T(8,128)(2,1)S(1)}, bf16[10,2,128,128]{3,2,1,0:T(8,128)(2,1)S(1)}, u32[]{:S(2)}, u32[]{:S(2)}) %collective-permute-start.11) | collective-permute-done | bytes 655392 | tf_op jit(solution)/shard_map/cond/branch_1_fun/ppermute | solution.py:417
  89.3 4.9 %branch_1_fun.13 = (bf16[8,2,128,128]{3,2,1,0:T(8,128)(2,1)S(1)}, f32[8,1,128,256]{3,2,1,0:T(8,128)S(1)}, f32[8,1,2,512]{3,2,1,0:T(2,128)S(1)}) custom-call(s32[8,128]{1,0:T(8,128)S(1)} %get-tuple-element.27.plan_ref, bf16[10,2,128,128]{3,2,1,0:T(8,128)(2,1)S(1)} %collective-permute-done.10.down_ref, ...), custom_call_target="tpu_custom_call", output_to_operand_aliasing={{1}: (4, {}), {2}: (5, {})} | custom-call | flops 268435456 | bytes 2097152 | tf_op jit(solution)/shard_map/cond/branch_1_fun/pallas_call | solution.py:370
  94.2 11.5 %all_to_all.10 = bf16[8,2,128,128]{3,2,1,0:T(8,128)(2,1)S(1)} all-to-all(bf16[8,2,128,128]{3,2,1,0:T(8,128)(2,1)S(1)} %get-tuple-element.48), channel_id=1, replica_groups={{0,1,2,3,4,5,6,7},{8,9,10,11,12,13,14,15},{16,17,18,19,20,21,22,23},{24..., dimensions={0} | all-to-all | bytes 1048576 | tf_op jit(solution)/shard_map/all_to_all | solution.py:406
  (27 shorter events, 4.6 us)
Async XLA Ops:
  0.0 1.3 %copy-start.1 = (bf16[2,128,1024]{2,1,0:T(8,128)(2,1)S(1)}, bf16[2,128,1024]{2,1,0:T(8,128)(2,1)}, u32[]{:S(2)}) copy-start(bf16[2,128,1024]{2,1,0:T(8,128)(2,1)} %param.11) | copy-start | bytes 1572868
  1.2 1.0 copy-start.2
  3.8 5.3 %copy-start.3 = (s32[32,6]{0,1:T(8,128)S(1)}, s32[32,6]{0,1:T(8,128)}, u32[]{:S(2)}) copy-start(s32[32,6]{0,1:T(8,128)} %param.13) | copy-start | bytes 2308
  3.8 5.4 %copy-start.4 = (s32[32,6]{0,1:T(8,128)S(1)}, s32[32,6]{0,1:T(8,128)}, u32[]{:S(2)}) copy-start(s32[32,6]{0,1:T(8,128)} %param.14) | copy-start | bytes 2308
  3.8 5.5 %copy-start.5 = (s32[32,6]{0,1:T(8,128)S(1)}, s32[32,6]{0,1:T(8,128)}, u32[]{:S(2)}) copy-start(s32[32,6]{0,1:T(8,128)} %param.15) | copy-start | bytes 2308
  3.8 5.6 %copy-start.6 = (s32[32,6]{0,1:T(8,128)S(1)}, s32[32,6]{0,1:T(8,128)}, u32[]{:S(2)}) copy-start(s32[32,6]{0,1:T(8,128)} %param.16) | copy-start | bytes 2308
  3.8 5.7 %copy-start = (s32[4]{0:T(128)S(1)}, s32[4]{0:T(128)}, u32[]{:S(2)}) copy-start(s32[4]{0:T(128)} %ref_ref.1) | copy-start | bytes 52
  3.8 25.5 %all-to-all-start = ((bf16[8,2,3,128,128]{4,3,2,1,0:T(8,128)(2,1)}), bf16[8,2,3,128,128]{4,3,2,1,0:T(8,128)(2,1)S(1)}, u32[]{:S(2)}, u32[]{:S(2)}) async-start(bf16[8,2,3,128,128]{4,3,2,1,0:T(8,128)(2,1)} %maximum_bitcast_fusion), calls=%async_computation | async-start | bytes 3145728 | tf_op jit(solution)/shard_map/all_to_all | solution.py:406
  30.0 18.6 %collective-permute-start.6 = (bf16[10,2,128,128]{3,2,1,0:T(8,128)(2,1)S(1)}, bf16[10,2,128,128]{3,2,1,0:T(8,128)(2,1)S(1)}, u32[]{:S(2)}, u32[]{:S(2)}) collective-permute-start(bf16[10,2,128,128]{3,2,1,0:T(8,128)(2,1)S(1)} %get-tuple-element.31), channel_id=1, source_target_pairs={{8,0},{10,2},{12,4},{14,6},{16,8},{18,10},{20,12},{22,14},{24,16},... | collective-permute-start | bytes 1966088 | tf_op jit(solution)/shard_map/cond/branch_1_fun/ppermute | solution.py:417
  31.3 18.4 %collective-permute-start.7 = (bf16[10,2,128,128]{3,2,1,0:T(8,128)(2,1)S(1)}, bf16[10,2,128,128]{3,2,1,0:T(8,128)(2,1)S(1)}, u32[]{:S(2)}, u32[]{:S(2)}) collective-permute-start(bf16[10,2,128,128]{3,2,1,0:T(8,128)(2,1)S(1)} %get-tuple-element.32), channel_id=1, source_target_pairs={{0,8},{2,10},{4,12},{6,14},{8,16},{10,18},{12,20},{14,22},{16,24},... | collective-permute-start | bytes 1966088 | tf_op jit(solution)/shard_map/cond/branch_1_fun/ppermute | solution.py:417
  50.7 18.1 %collective-permute-start.8 = (bf16[10,2,128,128]{3,2,1,0:T(8,128)(2,1)S(1)}, bf16[10,2,128,128]{3,2,1,0:T(8,128)(2,1)S(1)}, u32[]{:S(2)}, u32[]{:S(2)}) collective-permute-start(bf16[10,2,128,128]{3,2,1,0:T(8,128)(2,1)S(1)} %get-tuple-element.38), channel_id=1, source_target_pairs={{8,0},{10,2},{12,4},{14,6},{16,8},{18,10},{20,12},{22,14},{24,16},... | collective-permute-start | bytes 1966088 | tf_op jit(solution)/shard_map/cond/branch_1_fun/ppermute | solution.py:417
  52.0 18.0 %collective-permute-start.9 = (bf16[10,2,128,128]{3,2,1,0:T(8,128)(2,1)S(1)}, bf16[10,2,128,128]{3,2,1,0:T(8,128)(2,1)S(1)}, u32[]{:S(2)}, u32[]{:S(2)}) collective-permute-start(bf16[10,2,128,128]{3,2,1,0:T(8,128)(2,1)S(1)} %get-tuple-element.39), channel_id=1, source_target_pairs={{0,8},{2,10},{4,12},{6,14},{8,16},{10,18},{12,20},{14,22},{16,24},... | collective-permute-start | bytes 1966088 | tf_op jit(solution)/shard_map/cond/branch_1_fun/ppermute | solution.py:417
  70.9 17.2 %collective-permute-start.10 = (bf16[10,2,128,128]{3,2,1,0:T(8,128)(2,1)S(1)}, bf16[10,2,128,128]{3,2,1,0:T(8,128)(2,1)S(1)}, u32[]{:S(2)}, u32[]{:S(2)}) collective-permute-start(bf16[10,2,128,128]{3,2,1,0:T(8,128)(2,1)S(1)} %get-tuple-element.40), channel_id=1, source_target_pairs={{8,0},{10,2},{12,4},{14,6},{16,8},{18,10},{20,12},{22,14},{24,16},... | collective-permute-start | bytes 1966088 | tf_op jit(solution)/shard_map/cond/branch_1_fun/ppermute | solution.py:417
  72.2 17.1 %collective-permute-start.11 = (bf16[10,2,128,128]{3,2,1,0:T(8,128)(2,1)S(1)}, bf16[10,2,128,128]{3,2,1,0:T(8,128)(2,1)S(1)}, u32[]{:S(2)}, u32[]{:S(2)}) collective-permute-start(bf16[10,2,128,128]{3,2,1,0:T(8,128)(2,1)S(1)} %get-tuple-element.41), channel_id=1, source_target_pairs={{0,8},{2,10},{4,12},{6,14},{8,16},{10,18},{12,20},{14,22},{16,24},... | collective-permute-start | bytes 1966088 | tf_op jit(solution)/shard_map/cond/branch_1_fun/ppermute | solution.py:417

commit v4 on v3

--- a/solution.py
+++ b/solution.py
@@ -18,7 +18,7 @@
 
 def plan_kernel(
     me_ref, ref_ref, dev_hbm, place_hbm, block_hbm, valid_hbm, out_ref, entries, sems,
-    *, inner, n_tok, rounds, room,
+    *, inner, n_tok, rounds, rooms,
 ):
     copies = [
         pltpu.make_async_copy(array, entries.at[index], sems.at[index])
@@ -71,10 +71,12 @@
     def count(mask, axis):
         return jnp.sum(jnp.where(mask, 1.0, 0.0), axis=axis, keepdims=True)
 
-    def one_way(start, reach, here):
+    def ranking(start, reach):
         start_col, reach_col = column(start), column(reach)
         ahead = (reach_col > reach) | ((reach_col == reach) & earlier)
-        rank = count((start_col == start) & (reach_col > 0) & ahead, 0)
+        return count((start_col == start) & (reach_col > 0) & ahead, 0)
+
+    def departure(start, reach, rank, room):
         depart = jnp.zeros_like(start)
         for plane in range(n_outer - 1, 0, -1):
             total = jnp.zeros((1, 1), f32)
@@ -93,7 +95,9 @@
                 turn = turn + jnp.where(total <= rank, 1.0, 0.0)
             depart = jnp.where((start == plane) & (reach > 0), turn, depart)
         last = jnp.max(jnp.where(reach > 0, depart + reach - 1.0, 0.0), axis=1, keepdims=True)
-
+        return depart, last
+
+    def one_way(start, reach, here, depart):
         def on_link(link):
             crosses = (reach > 0) & (start > link) & (start - reach <= link)
             step = jnp.where(crosses, depart + (start - 1.0 - link), -1.0)
@@ -103,11 +107,11 @@
         arrives, in_step, in_slot = on_link(here)
         leaves, out_step, out_slot = on_link(here - 1.0)
         source = jnp.where(start == here, unit.astype(f32), units + in_slot)
-        key = column(jnp.where(leaves, (out_step - 1.0) * room + out_slot, -1.0))
+        key = column(jnp.where(leaves, (out_step - 1.0) * units + out_slot, -1.0))
         sent = jnp.sum(
             jnp.where(key == square_lane.astype(f32), column(source), 0.0), axis=0, keepdims=True
         )
-        return arrives, in_step, in_slot, sent, last
+        return arrives, in_step, in_slot, sent
 
     lowest, highest = origin, origin
     for plane in range(n_outer):
@@ -115,15 +119,23 @@
         other = n_outer - 1 - plane
         lowest = jnp.where(need[other] & (origin > other), float(other), lowest)
     top = n_outer - 1.0
-    down = one_way(origin, origin - lowest, me)
-    up = one_way(top - origin, highest - origin, top - me)
+    ways = [(origin, origin - lowest), (top - origin, highest - origin)]
+    ranks = [ranking(*way) for way in ways]
+    chosen = jnp.full((1, 1), float(len(rooms)), f32)
+    departs = [jnp.zeros_like(origin)] * 2
+    for index in reversed(range(len(rooms))):
+        tried = [departure(*way, rank, rooms[index]) for way, rank in zip(ways, ranks)]
+        fits = jnp.maximum(tried[0][1], tried[1][1]) <= rounds
+        chosen = jnp.where(fits, float(index), chosen)
+        departs = [jnp.where(fits, new[0], old) for new, old in zip(tried, departs)]
+    down = one_way(*ways[0], me, departs[0])
+    up = one_way(*ways[1], top - me, departs[1])
     unit_f = unit.astype(f32)
     spots = unit_f
-    for way, (arrives, in_step, in_slot, _, _) in enumerate((down, up)):
+    for way, (arrives, in_step, in_slot, _) in enumerate((down, up)):
         spots = jnp.where(arrives, (in_step + way * rounds) * 1024 + in_slot, spots)
     distance = origin - me
     full = jnp.where(distance > 0, distance, jnp.where(distance < 0, n_outer - 1 - distance, 0))
-    last = jnp.maximum(down[4], up[4]) + jnp.zeros_like(origin)
     full = full * 1024 + unit_f
     first = me * plane_frames
     row_frame = lax.broadcasted_iota(jnp.int32, (n_frames, lanes), 0).astype(f32)
@@ -148,18 +160,17 @@
             refs = jnp.where(lane == block, found, refs)
         return [listed, refs]
 
-    last = jnp.maximum(down[4], up[4]) + jnp.zeros_like(origin)
-    rows = [down[3], up[3], last] + places(spots) + places(full)
+    rows = [down[3], up[3], chosen + jnp.zeros_like(origin)] + places(spots) + places(full)
     for index, row in enumerate(rows):
         out_ref[index : index + 1, :] = row.astype(jnp.int32)
 
 
-def make_plan(epi_dev, epi_frame, epi_block, valid, ref_local, my_outer, inner, n_tok, rounds, room):
+def make_plan(epi_dev, epi_frame, epi_block, valid, ref_local, my_outer, inner, n_tok, rounds, rooms):
     n_blocks = epi_dev.shape[0] * n_tok
     lanes = -(-n_blocks // 128) * 128
     smem, anywhere = pl.BlockSpec(memory_space=pltpu.SMEM), pl.BlockSpec(memory_space=pl.ANY)
     return pl.pallas_call(
-        functools.partial(plan_kernel, inner=inner, n_tok=n_tok, rounds=rounds, room=room),
+        functools.partial(plan_kernel, inner=inner, n_tok=n_tok, rounds=rounds, rooms=rooms),
         out_shape=jax.ShapeDtypeStruct((8, lanes), jnp.int32),
         in_specs=[smem, smem] + [anywhere] * 4,
         out_specs=pl.BlockSpec(memory_space=pltpu.VMEM),
@@ -176,7 +187,7 @@
     own = sources[0]
     for way, target in enumerate(targets):
         for slot in range(room):
-            code = plan_ref[way, (step - 1) * room + slot]
+            code = plan_ref[way, (step - 1) * units + slot]
             if step == 1:
                 target[slot] = own[code, 1:3]
             else:
@@ -267,12 +278,12 @@
             item(lax.div(index, n_refs), plan_ref[spot_row + 1, lax.rem(index, n_refs)])
 
 
-def near_kernel(plan_ref, own_ref, query_ref, acc_ref, stat_ref, block_set, *, n_tok, spot_row, ref_near):
+def near_kernel(plan_ref, own_ref, query_ref, acc_ref, stat_ref, *, n_tok, spot_row, ref_near):
     n_local, n_tiles, width, tile = acc_ref.shape
     heads = width // HEAD_DIM
     row_head = lax.broadcasted_iota(jnp.int32, (width, 1), 0) // HEAD_DIM
 
-    @pl.loop(0, n_local, unroll=2)
+    @pl.loop(0, n_local, unroll=math.gcd(4, n_local))
     def _(local):
         base = (local // FRAMES_DEV) * (n_tok * FRAMES_DEV) + local % FRAMES_DEV
         spots = [base + block * FRAMES_DEV for block in range(n_tok)]
@@ -294,11 +305,6 @@
             query_ref[local, index] = query
             fold(keys, values, query, acc_ref.at[local, index], stat_ref.at[local, index], True)
 
-    listed_items(
-        plan_ref, {0: (own_ref, 1)}, block_set, query_ref, acc_ref, stat_ref, spot_row,
-        0 if ref_near else n_tok,
-    )
-
 
 def near(plan, own, n_local, n_tok, spot_row, ref_near):
     width = own.shape[-1]
@@ -319,7 +325,6 @@
             grid=(),
             in_specs=[whole],
             out_specs=(whole, whole, whole),
-            scratch_shapes=[pltpu.VMEM((2, BLOCK, width), own.dtype)],
         ),
         compiler_params=pltpu.CompilerParams(vmem_limit_bytes=40 * 1024 * 1024),
         cost_estimate=pl.CostEstimate(
@@ -331,12 +336,12 @@
 
 
 def stage_kernel(
-    plan_ref, down_ref, up_ref, query_ref, acc_in, stat_in, acc_ref, *refs, numbers, spot_row, n_refs, final
+    plan_ref, query_ref, acc_in, stat_in, *refs, numbers, spot_row, n_refs, final
 ):
-    stat_ref, block_set = refs[-2:]
+    acc_ref, stat_ref, block_set = refs[-3:]
+    sources = {n: (ref, 0 if n else 1) for n, ref in zip(numbers, refs)}
     if final:
-        out_ref, acc_ref = acc_ref, refs[0]
-    sources = {numbers[0]: (down_ref, 0), numbers[1]: (up_ref, 0)}
+        out_ref = refs[-4]
     listed_items(plan_ref, sources, block_set, query_ref, acc_ref, stat_ref, spot_row, n_refs)
     if not final:
         return
@@ -344,7 +349,7 @@
     n_tok = n_tiles * tile // BLOCK
     row_head = lax.broadcasted_iota(jnp.int32, (width, 1), 0) // HEAD_DIM
 
-    @pl.loop(0, n_local, unroll=2)
+    @pl.loop(0, n_local, unroll=math.gcd(4, n_local))
     def _(local):
         for index in range(n_tiles):
             total = stat_ref[local, index][1:2]
@@ -352,7 +357,7 @@
             for head in range(1, width // HEAD_DIM):
                 other = 1.0 / total[:, head * tile : (head + 1) * tile]
                 share = jnp.where(row_head == head, other, share)
-            result = (acc_ref[local, index] * share).T.astype(out_ref.dtype)
+            result = (acc_ref[local, index] * share).astype(out_ref.dtype).T
             for block in range(tile // BLOCK):
                 rank = (local // FRAMES_DEV) * n_tok + index * (tile // BLOCK) + block
                 out_ref[rank, local % FRAMES_DEV] = result[block * BLOCK : (block + 1) * BLOCK]
@@ -375,18 +380,18 @@
         grid_spec=pltpu.PrefetchScalarGridSpec(
             num_scalar_prefetch=1,
             grid=(),
-            in_specs=[whole] * 5,
+            in_specs=[whole] * (3 + len(received)),
             out_specs=[whole] * len(out_shape),
             scratch_shapes=[pltpu.VMEM((2, BLOCK, width), query.dtype)],
         ),
-        input_output_aliases={4: len(out_shape) - 2, 5: len(out_shape) - 1},
+        input_output_aliases={2: len(out_shape) - 2, 3: len(out_shape) - 1},
         compiler_params=pltpu.CompilerParams(vmem_limit_bytes=40 * 1024 * 1024),
         cost_estimate=pl.CostEstimate(
             flops=4 * pairs * width,
             bytes_accessed=8 * acc.size,
             transcendentals=pairs * width // HEAD_DIM,
         ),
-    )(plan, *received, query, acc, stat)
+    )(plan, query, acc, stat, *received)
 
 
 def shards(queries, keys, values, epi_dev, epi_frame, epi_block, valid, ref_local, *, n_tm, n_tok):
@@ -395,7 +400,9 @@
     n_ranks = inner * n_tok
     units = n_ranks * FRAMES_DEV
     width = keys.shape[2] // n_ranks
-    rounds, room = n_outer - 1, -(-units * 5 // 8)
+    rounds = n_outer - 1
+    shares = (8, 9, 10, 12) if n_outer <= SPAN else (10,)
+    rooms = [-(-units * share // 16) for share in shares]
     ref_near = inner % SPAN == 0
     plane_groups = [
         [(o * inner + i) * n_tok + t for i in range(inner) for t in range(n_tok)]
@@ -418,7 +425,7 @@
 
     my_outer = (lax.axis_index("tm") // inner).astype(jnp.int32)
     plan = make_plan(
-        epi_dev, epi_frame, epi_block, valid, ref_local, my_outer, inner, n_tok, rounds, room
+        epi_dev, epi_frame, epi_block, valid, ref_local, my_outer, inner, n_tok, rounds, rooms
     )
     three = jnp.stack([queries, keys, values]).reshape(3, FRAMES_DEV, BLOCK, n_ranks, width)
     own = exchange(three.transpose(3, 1, 0, 2, 4)).reshape(units, 3, BLOCK, width)
@@ -433,6 +440,8 @@
                 query, acc, stat = near(plan, own, n_local, n_tok, spot_row, ref_near)
             else:
                 numbers = (step - 1, rounds + step - 1)
+                if step == 2:
+                    received, numbers = received + [own], numbers + (0,)
                 acc, stat = stage(
                     plan, received, query, acc, stat, numbers, n_ranks, spot_row, n_refs, False
                 )
@@ -441,13 +450,17 @@
         numbers = (rounds, 2 * rounds)
         return stage(plan, received, query, acc, stat, numbers, n_ranks, spot_row, n_refs, True)[0]
 
-    def listed(own):
-        return passed(own, 3, lambda own, got, step: pack(plan, own, got or [], step, room))
+    def listed(room):
+        return lambda own: passed(
+            own, 3, lambda own, got, step: pack(plan, own, got or [], step, room)
+        )
 
     def gathered(own):
         return passed(own, 5, lambda own, got, step: got or [own[:, 1:3]] * 2)
 
-    attended = exchange(lax.cond(plan[2, 0] <= rounds, listed, gathered, own))
+    attended = exchange(
+        lax.switch(plan[2, 0], [listed(room) for room in rooms] + [gathered], own)
+    )
     return attended.transpose(1, 2, 0, 3).reshape(queries.shape)
 
 

time: 109 us -> 110 us (level)
  the two profiles are of different devices: /device:TPU:0 before, /device:TPU:25 now
where the time goes in v4:
time: 110 us; the launch traced here: 111 us
  waiting for transfers between devices  42.6 us (39%)
  Pallas kernels  31.4 us (29%)
  blocking collectives  15.5 us (14%)
  starting transfers between devices  14.7 us (13%)
  local copies, waits for them, and re-layouts  4.14 us (4%)
  other arithmetic  1.34 us (1%)
    ppermute x6, waiting for transfers between devices, shift(): return lax.ppermute(x, 'tm', pairs)  26.3 us
    pallas_call x3, Pallas kernels, stage(): pl.pallas_call(functools.partial(stage_kernel, numbers=numbers, spot_row=...  21.8 us
    all_to_all x1, waiting for transfers between devices, exchange(): lax.all_to_all(x, ('tm', 'tok'), 0, 0, axis_index_groups=plane_groups, ti...  16.3 us
    all_to_all x1, blocking collectives, exchange(): lax.all_to_all(x, ('tm', 'tok'), 0, 0, axis_index_groups=plane_groups, ti...  15.5 us
    ppermute x6, starting transfers between devices, shift(): return lax.ppermute(x, 'tm', pairs)  10.1 us
    pallas_call x1, Pallas kernels, near(): pl.pallas_call(functools.partial(near_kernel, n_tok=n_tok, spot_row=spot_...  5.2 us
    all_to_all x1, starting transfers between devices, exchange(): lax.all_to_all(x, ('tm', 'tok'), 0, 0, axis_index_groups=plane_groups, ti...  4.54 us
    pallas_call x3, Pallas kernels, pack(): pl.pallas_call(functools.partial(pack_kernel, step=step, room=room, units...  2.52 us
  transfers between devices with their start and end apart: 7, of which 7 were waited for; matrix products, arithmetic and copies ran while one was open for 1% of the time, Pallas kernels for 18%

profile of v4, /device:TPU:25, one launch (start us, length us, event | category | flops | bytes accessed | tf_op | source)
XLA Modules:
  0.0 110.8 jit_solution(4786387654676190091)
XLA Ops:
  0.0 1.2 %copy.50 = bf16[32,8,8,128]{3,2,1,0:T(8,128)(2,1)S(1)} copy(bf16[32,8,8,128]{3,1,2,0:T(8,128)(2,1)} %bitcast.31) | data formatting | bytes 1048576
  2.5 1.3 %maximum_bitcast_fusion = bf16[8,2,3,128,128]{4,3,2,1,0:T(8,128)(2,1)} fusion(bf16[1,2,128,8,128]{4,2,0,1,3:T(8,128)(2,1)S(1)} %copy.45, bf16[1,2,128,8,128]{4,2,0,1,3:T(8,128)(2,1)S(1)} %copy.44, bf16[1,2,128,8,128]{4,2,0,1,3:T(8,128)(2,1)S(1)} %copy.43), kind=kLoop, calls=%fused_computation | loop fusion | flops 1572864 | bytes 3145728 | tf_op jit(solution)/shard_map/transpose | solution.py:431
  3.8 4.5 %all-to-all-start = ((bf16[8,2,3,128,128]{4,3,2,1,0:T(8,128)(2,1)}), bf16[8,2,3,128,128]{4,3,2,1,0:T(8,128)(2,1)S(1)}, u32[]{:S(2)}, u32[]{:S(2)}) async-start(bf16[8,2,3,128,128]{4,3,2,1,0:T(8,128)(2,1)} %maximum_bitcast_fusion), calls=%async_computation | async-start | bytes 3145728 | tf_op jit(solution)/shard_map/all_to_all | solution.py:413
  8.7 1.9 %shard_map.82 = s32[8,128]{1,0:T(8,128)S(1)} custom-call(s32[1]{0:T(128)} %bitcast.me_ref, s32[4]{0:T(128)S(1)} %copy-done, s32[32,6]{1,0:T(8,128)S(1)} %copy.39.dev_hbm, s32[32,6]{1,0:T(8,128)S(1)} %copy.40.place_hbm, s32[32,6]{1,0:T(8,128)S(1)} %copy.41.block_hbm, s32[32,6]{1,0:T(8,128)S(1)} %copy.42.valid_hbm), custom_call_target="tpu_custom_call" | custom-call | tf_op jit(solution)/shard_map/pallas_call | solution.py:172
  11.8 16.3 %all-to-all-done = bf16[8,2,3,128,128]{4,3,2,1,0:T(8,128)(2,1)S(1)} async-done(((bf16[8,2,3,128,128]{4,3,2,1,0:T(8,128)(2,1)}), bf16[8,2,3,128,128]{4,3,2,1,0:T(8,128)(2,1)S(1)}, u32[]{:S(2)}, u32[]{:S(2)}) %all-to-all-start) | async-done | bytes 1572896 | tf_op jit(solution)/shard_map/all_to_all | solution.py:413
  28.0 66.5 %conditional.1 = (bf16[8,2,128,128]{3,2,1,0:T(8,128)(2,1)S(1)}) conditional(s32[]{:T(128)} %bitcast.1, (s32[8,128]{1,0:T(8,128)S(1)}, bf16[16,3,128,128]{3,2,1,0:T(8,128)(2,1)S(1)}) %tuple.41, (s32[8,128]{1,0:T(8,128)S(1)}, bf16[16,3,128,128]{3,2,1,0:T(8,128)(2,1)S(1)}) %tuple.42, (s32[8,128]{1,0:T(8,128)S(1)}, ...), branch_computations={%region_0.1_spmd, %region_1.2_spmd, %region_2.3_spmd, %region_3.4_... | conditional | flops 1342177280 | bytes 38797560 | solution.py:462
  28.7 2.1 %collective-permute-start.12 = (bf16[10,2,128,128]{3,2,1,0:T(8,128)(2,1)S(1)}, bf16[10,2,128,128]{3,2,1,0:T(8,128)(2,1)S(1)}, u32[]{:S(2)}, u32[]{:S(2)}) collective-permute-start(bf16[10,2,128,128]{3,2,1,0:T(8,128)(2,1)S(1)} %get-tuple-element.80), channel_id=1, source_target_pairs={{8,0},{10,2},{12,4},{14,6},{16,8},{18,10},{20,12},{22,14},{24,16},... | collective-permute-start | bytes 1966088 | tf_op jit(solution)/shard_map/cond/branch_2_fun/ppermute | solution.py:424
  30.9 1.3 %collective-permute-start.13 = (bf16[10,2,128,128]{3,2,1,0:T(8,128)(2,1)S(1)}, bf16[10,2,128,128]{3,2,1,0:T(8,128)(2,1)S(1)}, u32[]{:S(2)}, u32[]{:S(2)}) collective-permute-start(bf16[10,2,128,128]{3,2,1,0:T(8,128)(2,1)S(1)} %get-tuple-element.81), channel_id=1, source_target_pairs={{0,8},{2,10},{4,12},{6,14},{8,16},{10,18},{12,20},{14,22},{16,24},... | collective-permute-start | bytes 1966088 | tf_op jit(solution)/shard_map/cond/branch_2_fun/ppermute | solution.py:424
  32.2 5.2 %branch_2_fun.7 = (bf16[8,1,128,512]{3,2,1,0:T(8,128)(2,1)S(1)}, f32[8,1,128,256]{3,2,1,0:T(8,128)S(1)}, f32[8,1,2,512]{3,2,1,0:T(2,128)S(1)}) custom-call(s32[8,128]{1,0:T(8,128)S(1)} %get-tuple-element.73.plan_ref, bf16[16,3,128,128]{3,2,1,0:T(8,128)(2,1)S(1)} %get-tuple-element.83.own_ref.refs_0_.refs_2_), custom_call_target="tpu_custom_call" | custom-call | flops 536870912 | bytes 4194304 | tf_op jit(solution)/shard_map/cond/branch_2_fun/pallas_call | solution.py:316
  37.4 7.0 %collective-permute-done.12.refs_0_.refs_1_ = bf16[10,2,128,128]{3,2,1,0:T(8,128)(2,1)S(1)} collective-permute-done((bf16[10,2,128,128]{3,2,1,0:T(8,128)(2,1)S(1)}, bf16[10,2,128,128]{3,2,1,0:T(8,128)(2,1)S(1)}, u32[]{:S(2)}, u32[]{:S(2)}) %collective-permute-start.12) | collective-permute-done | bytes 655392 | tf_op jit(solution)/shard_map/cond/branch_2_fun/ppermute | solution.py:424
  44.4 3.8 %collective-permute-done.13.refs_1_.refs_2_ = bf16[10,2,128,128]{3,2,1,0:T(8,128)(2,1)S(1)} collective-permute-done((bf16[10,2,128,128]{3,2,1,0:T(8,128)(2,1)S(1)}, bf16[10,2,128,128]{3,2,1,0:T(8,128)(2,1)S(1)}, u32[]{:S(2)}, u32[]{:S(2)}) %collective-permute-start.13) | collective-permute-done | bytes 655392 | tf_op jit(solution)/shard_map/cond/branch_2_fun/ppermute | solution.py:424
  48.2 0.9 branch_2_fun.10
  49.2 2.1 %collective-permute-start.14 = (bf16[10,2,128,128]{3,2,1,0:T(8,128)(2,1)S(1)}, bf16[10,2,128,128]{3,2,1,0:T(8,128)(2,1)S(1)}, u32[]{:S(2)}, u32[]{:S(2)}) collective-permute-start(bf16[10,2,128,128]{3,2,1,0:T(8,128)(2,1)S(1)} %get-tuple-element.86), channel_id=1, source_target_pairs={{8,0},{10,2},{12,4},{14,6},{16,8},{18,10},{20,12},{22,14},{24,16},... | collective-permute-start | bytes 1966088 | tf_op jit(solution)/shard_map/cond/branch_2_fun/ppermute | solution.py:424
  51.3 1.3 %collective-permute-start.15 = (bf16[10,2,128,128]{3,2,1,0:T(8,128)(2,1)S(1)}, bf16[10,2,128,128]{3,2,1,0:T(8,128)(2,1)S(1)}, u32[]{:S(2)}, u32[]{:S(2)}) collective-permute-start(bf16[10,2,128,128]{3,2,1,0:T(8,128)(2,1)S(1)} %get-tuple-element.87), channel_id=1, source_target_pairs={{0,8},{2,10},{4,12},{6,14},{8,16},{10,18},{12,20},{14,22},{16,24},... | collective-permute-start | bytes 1966088 | tf_op jit(solution)/shard_map/cond/branch_2_fun/ppermute | solution.py:424
  52.6 8.7 %branch_2_fun.9 = (f32[8,1,128,256]{3,2,1,0:T(8,128)S(1)}, f32[8,1,2,512]{3,2,1,0:T(2,128)S(1)}) custom-call(s32[8,128]{1,0:T(8,128)S(1)} %get-tuple-element.73.plan_ref, bf16[8,1,128,512]{3,2,1,0:T(8,128)(2,1)S(1)} %get-tuple-element.75.query_ref, f32[8,1,128,256]{3,2,1,0:T(8,128)S(1)} %get-tuple-element.78.acc_in, ...), custom_call_target="tpu_custom_call", output_to_operand_aliasing={{0}: (2, {}), {1}: (3, {})} | custom-call | flops 268435456 | bytes 2097152 | tf_op jit(solution)/shard_map/cond/branch_2_fun/pallas_call | solution.py:375
  61.3 2.3 %collective-permute-done.14.refs_0_.refs_1_ = bf16[10,2,128,128]{3,2,1,0:T(8,128)(2,1)S(1)} collective-permute-done((bf16[10,2,128,128]{3,2,1,0:T(8,128)(2,1)S(1)}, bf16[10,2,128,128]{3,2,1,0:T(8,128)(2,1)S(1)}, u32[]{:S(2)}, u32[]{:S(2)}) %collective-permute-start.14) | collective-permute-done | bytes 655392 | tf_op jit(solution)/shard_map/cond/branch_2_fun/ppermute | solution.py:424
  63.6 3.9 %collective-permute-done.15.refs_1_.refs_2_ = bf16[10,2,128,128]{3,2,1,0:T(8,128)(2,1)S(1)} collective-permute-done((bf16[10,2,128,128]{3,2,1,0:T(8,128)(2,1)S(1)}, bf16[10,2,128,128]{3,2,1,0:T(8,128)(2,1)S(1)}, u32[]{:S(2)}, u32[]{:S(2)}) %collective-permute-start.15) | collective-permute-done | bytes 655392 | tf_op jit(solution)/shard_map/cond/branch_2_fun/ppermute | solution.py:424
  68.4 2.1 %collective-permute-start.16 = (bf16[10,2,128,128]{3,2,1,0:T(8,128)(2,1)S(1)}, bf16[10,2,128,128]{3,2,1,0:T(8,128)(2,1)S(1)}, u32[]{:S(2)}, u32[]{:S(2)}) collective-permute-start(bf16[10,2,128,128]{3,2,1,0:T(8,128)(2,1)S(1)} %get-tuple-element.91), channel_id=1, source_target_pairs={{8,0},{10,2},{12,4},{14,6},{16,8},{18,10},{20,12},{22,14},{24,16},... | collective-permute-start | bytes 1966088 | tf_op jit(solution)/shard_map/cond/branch_2_fun/ppermute | solution.py:424
  70.5 1.3 %collective-permute-start.17 = (bf16[10,2,128,128]{3,2,1,0:T(8,128)(2,1)S(1)}, bf16[10,2,128,128]{3,2,1,0:T(8,128)(2,1)S(1)}, u32[]{:S(2)}, u32[]{:S(2)}) collective-permute-start(bf16[10,2,128,128]{3,2,1,0:T(8,128)(2,1)S(1)} %get-tuple-element.92), channel_id=1, source_target_pairs={{0,8},{2,10},{4,12},{6,14},{8,16},{10,18},{12,20},{14,22},{16,24},... | collective-permute-start | bytes 1966088 | tf_op jit(solution)/shard_map/cond/branch_2_fun/ppermute | solution.py:424
  71.8 4.4 %branch_2_fun.11 = (f32[8,1,128,256]{3,2,1,0:T(8,128)S(1)}, f32[8,1,2,512]{3,2,1,0:T(2,128)S(1)}) custom-call(s32[8,128]{1,0:T(8,128)S(1)} %get-tuple-element.73.plan_ref, bf16[8,1,128,512]{3,2,1,0:T(8,128)(2,1)S(1)} %get-tuple-element.75.query_ref, f32[8,1,128,256]{3,2,1,0:T(8,128)S(1)} %get-tuple-element.84.acc_in, ...), custom_call_target="tpu_custom_call", output_to_operand_aliasing={{0}: (2, {}), {1}: (3, {})} | custom-call | flops 268435456 | bytes 2097152 | tf_op jit(solution)/shard_map/cond/branch_2_fun/pallas_call | solution.py:375
  76.2 5.4 %collective-permute-done.16.refs_0_ = bf16[10,2,128,128]{3,2,1,0:T(8,128)(2,1)S(1)} collective-permute-done((bf16[10,2,128,128]{3,2,1,0:T(8,128)(2,1)S(1)}, bf16[10,2,128,128]{3,2,1,0:T(8,128)(2,1)S(1)}, u32[]{:S(2)}, u32[]{:S(2)}) %collective-permute-start.16) | collective-permute-done | bytes 655392 | tf_op jit(solution)/shard_map/cond/branch_2_fun/ppermute | solution.py:424
  81.6 3.9 %collective-permute-done.17.refs_1_ = bf16[10,2,128,128]{3,2,1,0:T(8,128)(2,1)S(1)} collective-permute-done((bf16[10,2,128,128]{3,2,1,0:T(8,128)(2,1)S(1)}, bf16[10,2,128,128]{3,2,1,0:T(8,128)(2,1)S(1)}, u32[]{:S(2)}, u32[]{:S(2)}) %collective-permute-start.17) | collective-permute-done | bytes 655392 | tf_op jit(solution)/shard_map/cond/branch_2_fun/ppermute | solution.py:424
  85.4 8.6 %branch_2_fun.13 = (bf16[8,2,128,128]{3,2,1,0:T(8,128)(2,1)S(1)}, f32[8,1,128,256]{3,2,1,0:T(8,128)S(1)}, f32[8,1,2,512]{3,2,1,0:T(2,128)S(1)}) custom-call(s32[8,128]{1,0:T(8,128)S(1)} %get-tuple-element.73.plan_ref, bf16[8,1,128,512]{3,2,1,0:T(8,128)(2,1)S(1)} %get-tuple-element.75.query_ref, ...), custom_call_target="tpu_custom_call", output_to_operand_aliasing={{1}: (2, {}), {2}: (3, {})} | custom-call | flops 268435456 | bytes 2097152 | tf_op jit(solution)/shard_map/cond/branch_2_fun/pallas_call | solution.py:375
  94.5 15.5 %all_to_all.10 = bf16[8,2,128,128]{3,2,1,0:T(8,128)(2,1)S(1)} all-to-all(bf16[8,2,128,128]{3,2,1,0:T(8,128)(2,1)S(1)} %get-tuple-element.128), channel_id=1, replica_groups={{0,1,2,3,4,5,6,7},{8,9,10,11,12,13,14,15},{16,17,18,19,20,21,22,23},{24..., dimensions={0} | all-to-all | bytes 1048576 | tf_op jit(solution)/shard_map/all_to_all | solution.py:413
  (27 shorter events, 4.6 us)
Async XLA Ops:
  0.0 1.3 %copy-start.1 = (bf16[2,128,1024]{2,1,0:T(8,128)(2,1)S(1)}, bf16[2,128,1024]{2,1,0:T(8,128)(2,1)}, u32[]{:S(2)}) copy-start(bf16[2,128,1024]{2,1,0:T(8,128)(2,1)} %param.14) | copy-start | bytes 1572868
  1.2 1.0 copy-start.2
  3.8 4.6 %copy-start.3 = (s32[32,6]{0,1:T(8,128)S(1)}, s32[32,6]{0,1:T(8,128)}, u32[]{:S(2)}) copy-start(s32[32,6]{0,1:T(8,128)} %param.16) | copy-start | bytes 2308
  3.8 4.7 %copy-start.4 = (s32[32,6]{0,1:T(8,128)S(1)}, s32[32,6]{0,1:T(8,128)}, u32[]{:S(2)}) copy-start(s32[32,6]{0,1:T(8,128)} %param.17) | copy-start | bytes 2308
  3.8 4.7 %copy-start.5 = (s32[32,6]{0,1:T(8,128)S(1)}, s32[32,6]{0,1:T(8,128)}, u32[]{:S(2)}) copy-start(s32[32,6]{0,1:T(8,128)} %param.18) | copy-start | bytes 2308
  3.8 4.8 %copy-start.6 = (s32[32,6]{0,1:T(8,128)S(1)}, s32[32,6]{0,1:T(8,128)}, u32[]{:S(2)}) copy-start(s32[32,6]{0,1:T(8,128)} %param.19) | copy-start | bytes 2308
  3.8 4.9 %copy-start = (s32[4]{0:T(128)S(1)}, s32[4]{0:T(128)}, u32[]{:S(2)}) copy-start(s32[4]{0:T(128)} %ref_ref.1) | copy-start | bytes 52
  3.8 24.2 %all-to-all-start = ((bf16[8,2,3,128,128]{4,3,2,1,0:T(8,128)(2,1)}), bf16[8,2,3,128,128]{4,3,2,1,0:T(8,128)(2,1)S(1)}, u32[]{:S(2)}, u32[]{:S(2)}) async-start(bf16[8,2,3,128,128]{4,3,2,1,0:T(8,128)(2,1)} %maximum_bitcast_fusion), calls=%async_computation | async-start | bytes 3145728 | tf_op jit(solution)/shard_map/all_to_all | solution.py:413
  28.7 15.7 %collective-permute-start.12 = (bf16[10,2,128,128]{3,2,1,0:T(8,128)(2,1)S(1)}, bf16[10,2,128,128]{3,2,1,0:T(8,128)(2,1)S(1)}, u32[]{:S(2)}, u32[]{:S(2)}) collective-permute-start(bf16[10,2,128,128]{3,2,1,0:T(8,128)(2,1)S(1)} %get-tuple-element.80), channel_id=1, source_target_pairs={{8,0},{10,2},{12,4},{14,6},{16,8},{18,10},{20,12},{22,14},{24,16},... | collective-permute-start | bytes 1966088 | tf_op jit(solution)/shard_map/cond/branch_2_fun/ppermute | solution.py:424
  30.9 17.4 %collective-permute-start.13 = (bf16[10,2,128,128]{3,2,1,0:T(8,128)(2,1)S(1)}, bf16[10,2,128,128]{3,2,1,0:T(8,128)(2,1)S(1)}, u32[]{:S(2)}, u32[]{:S(2)}) collective-permute-start(bf16[10,2,128,128]{3,2,1,0:T(8,128)(2,1)S(1)} %get-tuple-element.81), channel_id=1, source_target_pairs={{0,8},{2,10},{4,12},{6,14},{8,16},{10,18},{12,20},{14,22},{16,24},... | collective-permute-start | bytes 1966088 | tf_op jit(solution)/shard_map/cond/branch_2_fun/ppermute | solution.py:424
  49.2 14.4 %collective-permute-start.14 = (bf16[10,2,128,128]{3,2,1,0:T(8,128)(2,1)S(1)}, bf16[10,2,128,128]{3,2,1,0:T(8,128)(2,1)S(1)}, u32[]{:S(2)}, u32[]{:S(2)}) collective-permute-start(bf16[10,2,128,128]{3,2,1,0:T(8,128)(2,1)S(1)} %get-tuple-element.86), channel_id=1, source_target_pairs={{8,0},{10,2},{12,4},{14,6},{16,8},{18,10},{20,12},{22,14},{24,16},... | collective-permute-start | bytes 1966088 | tf_op jit(solution)/shard_map/cond/branch_2_fun/ppermute | solution.py:424
  51.3 16.2 %collective-permute-start.15 = (bf16[10,2,128,128]{3,2,1,0:T(8,128)(2,1)S(1)}, bf16[10,2,128,128]{3,2,1,0:T(8,128)(2,1)S(1)}, u32[]{:S(2)}, u32[]{:S(2)}) collective-permute-start(bf16[10,2,128,128]{3,2,1,0:T(8,128)(2,1)S(1)} %get-tuple-element.87), channel_id=1, source_target_pairs={{0,8},{2,10},{4,12},{6,14},{8,16},{10,18},{12,20},{14,22},{16,24},... | collective-permute-start | bytes 1966088 | tf_op jit(solution)/shard_map/cond/branch_2_fun/ppermute | solution.py:424
  68.4 13.2 %collective-permute-start.16 = (bf16[10,2,128,128]{3,2,1,0:T(8,128)(2,1)S(1)}, bf16[10,2,128,128]{3,2,1,0:T(8,128)(2,1)S(1)}, u32[]{:S(2)}, u32[]{:S(2)}) collective-permute-start(bf16[10,2,128,128]{3,2,1,0:T(8,128)(2,1)S(1)} %get-tuple-element.91), channel_id=1, source_target_pairs={{8,0},{10,2},{12,4},{14,6},{16,8},{18,10},{20,12},{22,14},{24,16},... | collective-permute-start | bytes 1966088 | tf_op jit(solution)/shard_map/cond/branch_2_fun/ppermute | solution.py:424
  70.5 15.0 %collective-permute-start.17 = (bf16[10,2,128,128]{3,2,1,0:T(8,128)(2,1)S(1)}, bf16[10,2,128,128]{3,2,1,0:T(8,128)(2,1)S(1)}, u32[]{:S(2)}, u32[]{:S(2)}) collective-permute-start(bf16[10,2,128,128]{3,2,1,0:T(8,128)(2,1)S(1)} %get-tuple-element.92), channel_id=1, source_target_pairs={{0,8},{2,10},{4,12},{6,14},{8,16},{10,18},{12,20},{14,22},{16,24},... | collective-permute-start | bytes 1966088 | tf_op jit(solution)/shard_map/cond/branch_2_fun/ppermute | solution.py:424

commit v5 on v0

v5 whole, which is shorter than its diff:
```python
import functools
import math

import jax
import jax.numpy as jnp
from jax import lax
from jax.experimental import pallas as pl
from jax.experimental.pallas import tpu as pltpu
from jax.sharding import PartitionSpec as P

HEADS = 16
HEAD_DIM = 64
BLOCK = 128
FRAMES_DEV = 2
ENTRIES = 6
SPAN = 4
FAR = 1024
DEAD = 65536
BATCH = 4

STRIDE = FRAMES_DEV + 1
WHOLE = pl.BlockSpec(memory_space=pltpu.VMEM)


def split_kernel(q_hbm, k_hbm, v_hbm, out_ref, q_ref, k_ref, v_ref, sems):
    copies = [
        pltpu.make_async_copy(source, target, sems.at[index])
        for index, (source, target) in enumerate(
            ((q_hbm, q_ref), (k_hbm, k_ref), (v_hbm, v_ref))
        )
    ]
    for copy in copies:
        copy.start()
    for copy in copies:
        copy.wait()
    for rank in range(out_ref.shape[0]):
        lanes = slice(rank * HEAD_DIM, (rank + 1) * HEAD_DIM)
        for frame in range(FRAMES_DEV):
            out_ref[rank, frame] = jnp.concatenate(
                [k_ref[frame, :, lanes], v_ref[frame, :, lanes]], 1
            )
        out_ref[rank, FRAMES_DEV] = jnp.concatenate(
            [q_ref[frame, :, lanes] for frame in range(FRAMES_DEV)], 1
        )


def merge_kernel(x_ref, out_ref):
    for frame in range(FRAMES_DEV):
        part = slice(frame * HEAD_DIM, (frame + 1) * HEAD_DIM)
        for rank in range(0, x_ref.shape[0], 2):
            out_ref[frame, :, rank * HEAD_DIM : (rank + 2) * HEAD_DIM] = jnp.concatenate(
                [x_ref[rank, :, part], x_ref[rank + 1, :, part]], 1
            )


def plan_kernel(
    me_ref, ref_ref, dev_hbm, place_hbm, block_hbm, valid_hbm, out_ref, entries, sems,
    *, inner, n_tok, rooms,
):
    copies = [
        pltpu.make_async_copy(array, entries.at[index], sems.at[index])
        for index, array in enumerate((dev_hbm, place_hbm, block_hbm, valid_hbm))
    ]
    for copy in copies:
        copy.start()
    for copy in copies:
        copy.wait()
    n_frames = dev_hbm.shape[0]
    units = inner * n_tok * STRIDE
    group_frames = inner * FRAMES_DEV
    n_outer = n_frames // group_frames
    lanes = out_ref.shape[1]
    f32 = jnp.float32
    me = me_ref[0].astype(f32)
    dev = entries[0]
    ids = (dev // inner) * units + ((dev % inner) * n_tok + entries[2]) * STRIDE + entries[1]
    used = entries[3] > 0
    frame_lane = lax.broadcasted_iota(jnp.int32, (n_frames, lanes), 1)
    hit = jnp.zeros((n_frames, lanes), f32)
    for entry in range(ENTRIES):
        here = (ids[:, entry : entry + 1] == frame_lane) & used[:, entry : entry + 1]
        hit = jnp.where(here, 1.0, hit)
    lane = lax.broadcasted_iota(jnp.int32, (1, lanes), 1)
    unit = (lane % units).astype(f32)
    origin = (lane // units).astype(f32)
    crosses = jnp.zeros((1, lanes), f32)
    for group in range(n_outer):
        rows = lax.slice_in_dim(hit, group * group_frames, (group + 1) * group_frames)
        wanted = jnp.max(rows, axis=0, keepdims=True)
        crosses = jnp.where(origin != group, jnp.maximum(wanted, crosses), crosses)

    def count(mask, axis):
        return jnp.sum(jnp.where(mask, 1.0, 0.0), axis=axis, keepdims=True)

    steps = jnp.where(origin > me, me - origin + n_outer, me - origin)
    everything = jnp.where(origin == me, unit, FAR + (steps - 1.0) * units + unit)
    sent, spots, chosen = jnp.zeros_like(origin), everything, jnp.full((1, 1), float(len(rooms)), f32)
    if rooms:
        square_row = lax.broadcasted_iota(jnp.int32, (lanes, lanes), 0)
        square_lane = lax.broadcasted_iota(jnp.int32, (lanes, lanes), 1)

        def column(row):
            return jnp.sum(jnp.where(square_row == square_lane, row, 0.0), axis=1, keepdims=True)

        key = jnp.where(crosses > 0, origin, -1.0)
        slot = count((column(key) == key) & (square_row < square_lane), 0)
        most = jnp.max(jnp.where(crosses > 0, slot + 1.0, 0.0), axis=1, keepdims=True)
        for index in reversed(range(len(rooms))):
            chosen = jnp.where(most <= rooms[index], float(index), chosen)
        mine = column(jnp.where((crosses > 0) & (origin == me), slot, -1.0))
        sent = jnp.sum(
            jnp.where(mine == square_lane.astype(f32), column(unit), 0.0), axis=0, keepdims=True
        )
        spots = jnp.where(origin == me, unit, FAR + slot)

    row_frame = lax.broadcasted_iota(jnp.int32, (n_frames, lanes), 0).astype(f32)
    wide_lane = frame_lane.astype(f32)

    def places(table):
        listed = jnp.zeros((1, lanes), f32)
        for entry in range(ENTRIES):
            mine, live = ids[:, entry : entry + 1], used[:, entry : entry + 1]
            found = jnp.sum(jnp.where(mine == frame_lane, table, 0.0), axis=1, keepdims=True)
            found = jnp.where(live, found, float(DEAD))
            target = (row_frame - me * group_frames) * 8 + entry
            listed += jnp.sum(jnp.where(target == wide_lane, found, 0.0), axis=0, keepdims=True)
        listed = jnp.where(lane % 8 < ENTRIES, listed, float(DEAD))
        refs = jnp.zeros((1, lanes), f32)
        for local in range(max(1, inner // SPAN)):
            scene = me_ref[0] * inner // SPAN + local
            ref_frame = scene * (SPAN * FRAMES_DEV) + ref_ref[scene]
            ref_dev = ref_frame // FRAMES_DEV
            base = (ref_dev // inner) * units + (ref_dev % inner) * n_tok * STRIDE
            for block in range(n_tok):
                which = base + block * STRIDE + ref_frame % FRAMES_DEV
                found = jnp.sum(jnp.where(lane == which, table, 0.0), axis=1, keepdims=True)
                refs = jnp.where(lane == local * n_tok + block, found, refs)
        return [listed, refs]

    rows = [sent, chosen + jnp.zeros_like(origin)] + places(spots) + places(everything)
    for index, row in enumerate(rows):
        out_ref[index : index + 1, :] = row.astype(jnp.int32)


def make_plan(epi_dev, epi_frame, epi_block, valid, ref_local, my_outer, inner, n_tok, rooms):
    n_outer = epi_dev.shape[0] // (inner * FRAMES_DEV)
    n_units = n_outer * inner * n_tok * STRIDE
    lanes = -(-n_units // 128) * 128
    smem, anywhere = pl.BlockSpec(memory_space=pltpu.SMEM), pl.BlockSpec(memory_space=pl.ANY)
    return pl.pallas_call(
        functools.partial(plan_kernel, inner=inner, n_tok=n_tok, rooms=rooms),
        out_shape=jax.ShapeDtypeStruct((8, lanes), jnp.int32),
        in_specs=[smem, smem] + [anywhere] * 4,
        out_specs=WHOLE,
        scratch_shapes=[
            pltpu.VMEM((4,) + epi_dev.shape, jnp.int32),
            pltpu.SemaphoreType.DMA((4,)),
        ],
        compiler_params=pltpu.CompilerParams(vmem_limit_bytes=32 * 1024 * 1024),
    )(my_outer.reshape(1), ref_local, epi_dev, epi_frame, epi_block, valid)


def pack_kernel(plan_ref, own_ref, *targets):
    first = 0
    for target in targets:
        for slot in range(target.shape[0]):
            target[slot] = own_ref[plan_ref[0, first + slot]]
        first += target.shape[0]


def pack(plan, own, sizes):
    return pl.pallas_call(
        pack_kernel,
        out_shape=[jax.ShapeDtypeStruct((size,) + own.shape[1:], own.dtype) for size in sizes],
        grid_spec=pltpu.PrefetchScalarGridSpec(
            num_scalar_prefetch=1,
            grid=(),
            in_specs=[WHOLE],
            out_specs=[WHOLE] * len(sizes),
        ),
        compiler_params=pltpu.CompilerParams(vmem_limit_bytes=24 * 1024 * 1024),
        cost_estimate=pl.CostEstimate(
            flops=0, bytes_accessed=4 * sum(sizes) * own[0].size, transcendentals=0
        ),
    )(plan, own)


def part_of(pairs, query):
    scores = jnp.dot(pairs, query, preferred_element_type=jnp.float32)
    top = jnp.max(scores, axis=0, keepdims=True)
    weights = jnp.exp(scores - top)
    total = jnp.sum(weights, axis=0, keepdims=True)
    attended = jnp.dot(
        pairs.T[HEAD_DIM:], weights.astype(jnp.bfloat16), preferred_element_type=jnp.float32
    )
    return attended, top, total


def near_kernel(plan_ref, own_ref, query_ref, acc_ref, stat_ref, *, n_tok, spot_row, ref_near):
    n_local, n_tiles, _, tile = acc_ref.shape
    inner = n_local // FRAMES_DEV

    @pl.loop(0, inner, unroll=math.gcd(2, inner))
    def _(chip):
        spots = [(chip * n_tok + block) * STRIDE for block in range(n_tok)]
        refs = []
        if ref_near:
            scene = chip // SPAN * n_tok
            refs = [own_ref[plan_ref[spot_row + 1, scene + block]] for block in range(n_tok)]
        turned = [own_ref[spot + FRAMES_DEV].T for spot in spots]
        for frame in range(FRAMES_DEV):
            pairs = jnp.concatenate([own_ref[spot + frame] for spot in spots] + refs, 0)
            local = chip * FRAMES_DEV + frame
            for index in range(n_tiles):
                first = index * tile // BLOCK
                query = jnp.concatenate(
                    [
                        block[frame * HEAD_DIM : (frame + 1) * HEAD_DIM]
                        for block in turned[first : first + tile // BLOCK]
                    ],
                    1,
                ) * jnp.asarray(HEAD_DIM**-0.5, own_ref.dtype)
                query = jnp.concatenate([query, jnp.zeros_like(query)], 0)
                query_ref[local, index] = query
                attended, top, total = part_of(pairs, query)
                acc_ref[local, index] = attended
                stat_ref[local, index, 0:1] = top
                stat_ref[local, index, 1:2] = total


def near(plan, own, inner, n_tok, spot_row, ref_near):
    rows = n_tok * BLOCK
    tile = math.gcd(rows, 256)
    n_local = inner * FRAMES_DEV
    pairs = n_local * rows * (1 + ref_near) * rows
    lead = (n_local, rows // tile)
    return pl.pallas_call(
        functools.partial(near_kernel, n_tok=n_tok, spot_row=spot_row, ref_near=ref_near),
        out_shape=(
            jax.ShapeDtypeStruct(lead + (2 * HEAD_DIM, tile), own.dtype),
            jax.ShapeDtypeStruct(lead + (HEAD_DIM, tile), jnp.float32),
            jax.ShapeDtypeStruct(lead + (2, tile), jnp.float32),
        ),
        grid_spec=pltpu.PrefetchScalarGridSpec(
            num_scalar_prefetch=1,
            grid=(),
            in_specs=[WHOLE],
            out_specs=(WHOLE, WHOLE, WHOLE),
        ),
        compiler_params=pltpu.CompilerParams(vmem_limit_bytes=40 * 1024 * 1024),
        cost_estimate=pl.CostEstimate(
            flops=8 * pairs * HEAD_DIM,
            bytes_accessed=16 * n_local * rows * HEAD_DIM,
            transcendentals=pairs,
        ),
    )(plan, own)


def stage_kernel(
    plan_ref, query_ref, acc_in, stat_in, source_ref, *refs, low, high, spot_row, n_refs, final
):
    acc_ref, stat_ref, items = refs[-3:]
    n_local, n_tiles, _, tile = acc_ref.shape

    def list_up(row, per_frame):
        def one(index, found):
            code = plan_ref[row, lax.rem(index, per_frame) if row > spot_row else index]
            items[found] = lax.div(index, per_frame) * DEAD + (code - low)
            return found + ((code >= low) & (code < high)).astype(jnp.int32)

        return one

    found = lax.fori_loop(0, n_local * 8, list_up(spot_row, 8), jnp.int32(0), unroll=8)
    if n_refs:
        found = lax.fori_loop(0, n_local * n_refs, list_up(spot_row + 1, n_refs), found)

    @pl.loop(0, lax.div(found + (BATCH - 1), jnp.int32(BATCH)))
    def _(step):
        for index in range(n_tiles):
            parts = []
            for turn in range(BATCH):
                here = step * BATCH + turn < found
                word = items[jnp.where(here, step * BATCH + turn, 0)]
                local = word >> 16
                parts.append((here, local, part_of(source_ref[word & (DEAD - 1)], query_ref[local, index])))
            for here, local, (attended, top, total) in parts:
                old_top = stat_ref[local, index, 0:1]
                new_top = jnp.where(here, jnp.maximum(old_top, top), old_top)
                keep = jnp.exp(old_top - new_top)
                add = jnp.where(here, jnp.exp(jnp.minimum(top - new_top, 0.0)), 0.0)
                acc_ref[local, index] = acc_ref[local, index] * keep + attended * add
                stat_ref[local, index, 1:2] = stat_ref[local, index, 1:2] * keep + total * add
                stat_ref[local, index, 0:1] = new_top

    if not final:
        return
    out_ref = refs[0]
    n_tok = n_tiles * tile // BLOCK
    inner = n_local // FRAMES_DEV

    @pl.loop(0, inner, unroll=math.gcd(4, inner))
    def _(chip):
        for index in range(n_tiles):
            parts = []
            for frame in range(FRAMES_DEV):
                local = chip * FRAMES_DEV + frame
                parts.append(acc_ref[local, index] * (1.0 / stat_ref[local, index][1:2]))
            result = jnp.concatenate(parts, 0).astype(out_ref.dtype).T
            for block in range(tile // BLOCK):
                out_ref[chip * n_tok + index * (tile // BLOCK) + block] = result[
                    block * BLOCK : (block + 1) * BLOCK
                ]


def stage(plan, source, query, acc, stat, low, n_ranks, spot_row, n_refs, final):
    out_shape = [jax.ShapeDtypeStruct(x.shape, x.dtype) for x in (acc, stat)]
    if final:
        result = jax.ShapeDtypeStruct((n_ranks, BLOCK, FRAMES_DEV * HEAD_DIM), query.dtype)
        out_shape = [result] + out_shape
    pairs = 2 * acc.size // HEAD_DIM * BLOCK
    return pl.pallas_call(
        functools.partial(
            stage_kernel, low=low, high=low + source.shape[0], spot_row=spot_row,
            n_refs=n_refs, final=final,
        ),
        out_shape=out_shape,
        grid_spec=pltpu.PrefetchScalarGridSpec(
            num_scalar_prefetch=1,
            grid=(),
            in_specs=[WHOLE] * 4,
            out_specs=[WHOLE] * len(out_shape),
            scratch_shapes=[pltpu.SMEM((acc.shape[0] * (8 + n_refs) + 1,), jnp.int32)],
        ),
        input_output_aliases={2: len(out_shape) - 2, 3: len(out_shape) - 1},
        compiler_params=pltpu.CompilerParams(vmem_limit_bytes=40 * 1024 * 1024),
        cost_estimate=pl.CostEstimate(
            flops=8 * pairs * HEAD_DIM, bytes_accessed=8 * acc.size, transcendentals=pairs
        ),
    )(plan, query, acc, stat, source)


def shards(queries, keys, values, epi_dev, epi_frame, epi_block, valid, ref_local, *, n_tm, n_tok):
    inner = HEADS // n_tok
    n_outer = n_tm // inner
    n_ranks = inner * n_tok
    units = n_ranks * STRIDE
    ref_near = inner % SPAN == 0
    n_refs = 0 if ref_near else n_tok
    blocks = n_ranks * FRAMES_DEV
    rooms = [-(-blocks * share // 16) for share in (10, 11, 12, 13, 14)] if n_outer == 2 else []
    groups = [
        [(o * inner + i) * n_tok + t for i in range(inner) for t in range(n_tok)]
        for o in range(n_outer)
    ]

    def exchange(x):
        return lax.all_to_all(x, ("tm", "tok"), 0, 0, axis_index_groups=groups, tiled=True)

    def turn(x):
        return lax.ppermute(x, "tm", [(d, (d + inner) % n_tm) for d in range(n_tm)])

    my_outer = (lax.axis_index("tm") // inner).astype(jnp.int32)
    plan = make_plan(
        epi_dev, epi_frame, epi_block, valid, ref_local, my_outer, inner, n_tok, rooms
    )
    small = pltpu.CompilerParams(vmem_limit_bytes=24 * 1024 * 1024)
    own = pl.pallas_call(
        split_kernel,
        out_shape=jax.ShapeDtypeStruct((n_ranks, STRIDE, BLOCK, 2 * HEAD_DIM), keys.dtype),
        in_specs=[pl.BlockSpec(memory_space=pltpu.HBM)] * 3,
        out_specs=WHOLE,
        scratch_shapes=[pltpu.VMEM(keys.shape, keys.dtype)] * 3 + [pltpu.SemaphoreType.DMA((3,))],
        compiler_params=small,
    )(queries, keys, values)
    own = exchange(own).reshape(units, BLOCK, 2 * HEAD_DIM)

    def attend(own, arrivals, spot_row, waiting=None):
        query, acc, stat = near(plan, own, inner, n_tok, spot_row, ref_near)
        acc, stat = stage(plan, own, query, acc, stat, 0, n_ranks, spot_row, n_refs, False)
        if waiting is not None:
            waiting, acc = lax.optimization_barrier((waiting, acc))
            arrivals = arrivals + [turn(waiting)]
        low = FAR
        for index, arrived in enumerate(arrivals):
            final = index == len(arrivals) - 1
            *result, acc, stat = stage(
                plan, arrived, query, acc, stat, low, n_ranks, spot_row, n_refs, final
            )
            low += arrived.shape[0]
        return result[0]

    def listed(room):
        first = -(-room * 2 // 3)

        def run(own):
            early, late = pack(plan, own, (first, room - first))
            return attend(own, [turn(early)], 2, late)

        return run

    def gathered(own):
        arrivals = [turn(own)]
        for _ in range(n_outer - 2):
            arrivals.append(turn(arrivals[-1]))
        return attend(own, arrivals, 4)

    options = [listed(room) for room in rooms] + [gathered]
    attended = exchange(lax.switch(plan[1, 0], options, own))
    return pl.pallas_call(
        merge_kernel,
        out_shape=jax.ShapeDtypeStruct(queries.shape, queries.dtype),
        in_specs=[WHOLE],
        out_specs=WHOLE,
        compiler_params=small,
    )(attended)


def solution(mesh):
    return jax.shard_map(
        functools.partial(shards, n_tm=mesh.shape["tm"], n_tok=mesh.shape["tok"]),
        mesh=mesh,
        in_specs=(P("tm", "tok", None),) * 3 + (P(),) * 5,
        out_specs=P("tm", "tok", None),
        check_vma=False,
    )
```

time: 262 us -> 96.3 us (0.37)
  waiting for transfers between devices: 111 us -> 30.6 us
  local copies, waits for them, and re-layouts: 71 us -> 4.02 us
  Pallas kernels: 0 us -> 36.6 us
  matrix products: 23 us -> 0 us
  blocking collectives: 32.7 us -> 13.3 us
  between operations: 14.2 us -> 0.75 us
  starting transfers between devices: 3.53 us -> 9.16 us
  other arithmetic: 5.45 us -> 0 us
    all_gather x2 -> x0, waiting for transfers between devices: 106 us -> none  [the longest x1 54.9 us: shards(): lax.all_gather(head_v, 'tm', axis=0, tiled=True)]
    pallas_call x0 -> x8, Pallas kernels: none -> 36.6 us  [the longest x3 23.8 us: stage(): pl.pallas_call(functools.partial(stage_kernel, low=low, high=low + source...]
    all_gather x2 -> x0, local copies, waits for them, and re-layouts: 22.9 us -> none  [the longest x1 11.5 us: shards(): lax.all_gather(head_v, 'tm', axis=0, tiled=True)]
    all_to_all x3 -> x1, blocking collectives: 32.7 us -> 13.3 us  [exchange(): lax.all_to_all(x, ('tm', 'tok'), 0, 0, axis_index_groups=groups, tiled=True)]
    gather x4 -> x0, local copies, waits for them, and re-layouts: 16 us -> none  [the longest x2 8 us: pick_block(): lax.dynamic_slice(piece_values, corner, (1, BLOCK, slab_width))[0]]
    dynamic_slice x15 -> x0, local copies, waits for them, and re-layouts: 15.5 us -> none  [the longest x14 14.9 us: shards(): lax.map(one_frame, (head_q, head_k, head_v, epi_keys, epi_values, live_epi))]
    all_to_all x1, waiting for transfers between devices: 4.69 us -> 19.1 us  [exchange(): lax.all_to_all(x, ('tm', 'tok'), 0, 0, axis_index_groups=groups, tiled=True)]
    sub x2 -> x0, matrix products: 14.2 us -> none  [per_block(): weights = jnp.exp(scores - row_max) * live_mask]
  transfers between devices with their start and end apart: 3 -> 3, of which waited for: 3 -> 2; matrix products, arithmetic and copies ran while one was open for 9% -> 1% of each run, Pallas kernels for 0% -> 32%
where the time goes in v5:
time: 96.3 us; the launch traced here: 95 us
  Pallas kernels  36.6 us (38%)
  waiting for transfers between devices  30.6 us (32%)
  blocking collectives  13.3 us (14%)
  starting transfers between devices  9.16 us (10%)
  local copies, waits for them, and re-layouts  4.02 us (4%)
    pallas_call x3, Pallas kernels, stage(): pl.pallas_call(functools.partial(stage_kernel, low=low, high=low + source...  23.8 us
    all_to_all x1, waiting for transfers between devices, exchange(): lax.all_to_all(x, ('tm', 'tok'), 0, 0, axis_index_groups=groups, tiled=True)  19.1 us
    all_to_all x1, blocking collectives, exchange(): lax.all_to_all(x, ('tm', 'tok'), 0, 0, axis_index_groups=groups, tiled=True)  13.3 us
    ppermute x2, waiting for transfers between devices, turn(): return lax.ppermute(x, 'tm', [(d, (d + inner) % n_tm) for d in range(n_tm)])  11.6 us
    pallas_call x1, Pallas kernels, near(): pl.pallas_call(functools.partial(near_kernel, n_tok=n_tok, spot_row=spot_...  7.75 us
    all_to_all x1, starting transfers between devices, exchange(): lax.all_to_all(x, ('tm', 'tok'), 0, 0, axis_index_groups=groups, tiled=True)  6.43 us
    unnamed x20, local copies, waits for them, and re-layouts  3.5 us
    ppermute x2, starting transfers between devices, turn(): return lax.ppermute(x, 'tm', [(d, (d + inner) % n_tm) for d in range(n_tm)])  2.73 us
  transfers between devices with their start and end apart: 3, of which 2 were waited for; matrix products, arithmetic and copies ran while one was open for 1% of the time, Pallas kernels for 32%

profile of v5, /device:TPU:0, one launch (start us, length us, event | category | flops | bytes accessed | tf_op | source)
XLA Modules:
  0.0 95.0 jit_solution(6756500438604198877)
XLA Ops:
  0.0 1.0 %copy-done = bf16[2,128,1024]{2,1,0:T(8,128)(2,1)S(1)} copy-done((bf16[2,128,1024]{2,1,0:T(8,128)(2,1)S(1)}, bf16[2,128,1024]{2,1,0:T(8,128)(2,1)}, u32[]{:S(2)}) %copy-start) | copy-done | bytes 524312
  1.0 1.0 %copy-done.1 = bf16[2,128,1024]{2,1,0:T(8,128)(2,1)S(1)} copy-done((bf16[2,128,1024]{2,1,0:T(8,128)(2,1)S(1)}, bf16[2,128,1024]{2,1,0:T(8,128)(2,1)}, u32[]{:S(2)}) %copy-start.1) | copy-done | bytes 524312
  2.1 1.0 %copy-done.2 = bf16[2,128,1024]{2,1,0:T(8,128)(2,1)S(1)} copy-done((bf16[2,128,1024]{2,1,0:T(8,128)(2,1)S(1)}, bf16[2,128,1024]{2,1,0:T(8,128)(2,1)}, u32[]{:S(2)}) %copy-start.2) | copy-done | bytes 524312
  3.1 1.8 %shard_map.83 = bf16[16,3,128,128]{3,2,1,0:T(8,128)(2,1)} custom-call(bf16[2,128,1024]{2,1,0:T(8,128)(2,1)S(1)} %copy-done, bf16[2,128,1024]{2,1,0:T(8,128)(2,1)S(1)} %copy-done.1, bf16[2,128,1024]{2,1,0:T(8,128)(2,1)S(1)} %copy-done.2), custom_call_target="tpu_custom_call" | custom-call | tf_op jit(solution)/shard_map/pallas_call | solution.py:367
  4.9 0.0 copy-start.5
  5.0 6.4 %all-to-all-start = ((bf16[16,3,128,128]{3,2,1,0:T(8,128)(2,1)}), bf16[16,3,128,128]{3,2,1,0:T(8,128)(2,1)S(1)}, u32[]{:S(2)}, u32[]{:S(2)}) async-start(bf16[16,3,128,128]{3,2,1,0:T(8,128)(2,1)} %shard_map.83), calls=%async_computation | async-start | bytes 3145728 | tf_op jit(solution)/shard_map/all_to_all | solution.py:357
  11.4 0.1 copy.43.dev_hbm
  11.5 0.1 copy.44.place_hbm
  11.6 0.1 copy.45.block_hbm
  11.7 0.1 copy.46.valid_hbm
  11.8 1.6 %shard_map.82 = s32[8,128]{1,0:T(8,128)S(1)} custom-call(s32[1]{0:T(128)} %bitcast.me_ref, s32[4]{0:T(128)S(1)} %copy-done.3, s32[32,6]{1,0:T(8,128)S(1)} %copy.43.dev_hbm, s32[32,6]{1,0:T(8,128)S(1)} %copy.44.place_hbm, s32[32,6]{1,0:T(8,128)S(1)} %copy.45.block_hbm, s32[32,6]{1,0:T(8,128)S(1)} %copy.46.valid_hbm), custom_call_target="tpu_custom_call" | custom-call | tf_op jit(solution)/shard_map/pallas_call | solution.py:150
  13.4 0.5 slice.3
  14.5 19.1 %all-to-all-done = bf16[16,3,128,128]{3,2,1,0:T(8,128)(2,1)S(1)} async-done(((bf16[16,3,128,128]{3,2,1,0:T(8,128)(2,1)}), bf16[16,3,128,128]{3,2,1,0:T(8,128)(2,1)S(1)}, u32[]{:S(2)}, u32[]{:S(2)}) %all-to-all-start) | async-done | bytes 1572896 | tf_op jit(solution)/shard_map/all_to_all | solution.py:357
  33.6 47.1 %conditional.1 = (bf16[16,128,128]{2,1,0:T(8,128)(2,1)S(1)}) conditional(s32[]{:T(128)} %bitcast.1, (s32[8,128]{1,0:T(8,128)S(1)}, bf16[48,128,128]{2,1,0:T(8,128)(2,1)S(1)}) %tuple.35, (s32[8,128]{1,0:T(8,128)S(1)}, bf16[48,128,128]{2,1,0:T(8,128)(2,1)S(1)}) %tuple.36, (s32[8,128]{1,0:T(8,128)S(1)}, ...), branch_computations={%region_0.1_spmd, %region_1.2_spmd, %region_2.3_spmd, %region_3.4_... | conditional | flops 2684354560 | bytes 15990872 | solution.py:408
  33.6 0.7 branch_3_fun.6
  34.3 2.7 %collective-permute-start.6 = (bf16[18,128,128]{2,1,0:T(8,128)(2,1)S(1)}, bf16[18,128,128]{2,1,0:T(8,128)(2,1)S(1)}, u32[]{:S(2)}, u32[]{:S(2)}) collective-permute-start(bf16[18,128,128]{2,1,0:T(8,128)(2,1)S(1)} %get-tuple-element.87), channel_id=1, source_target_pairs={{0,16},{2,18},{4,20},{6,22},{8,24},{10,26},{12,28},{14,30},{16,0},... | collective-permute-start | bytes 1769480 | tf_op jit(solution)/shard_map/cond/branch_3_fun/ppermute | solution.py:360
  36.9 7.7 %branch_3_fun.5 = (bf16[16,1,128,256]{3,2,1,0:T(8,128)(2,1)S(1)}, f32[16,1,64,256]{3,2,1,0:T(8,128)S(1)}, f32[16,1,2,256]{3,2,1,0:T(2,128)S(1)}) custom-call(s32[8,128]{1,0:T(8,128)S(1)} %get-tuple-element.78.plan_ref, bf16[48,128,128]{2,1,0:T(8,128)(2,1)S(1)} %get-tuple-element.79.own_ref.source_ref), custom_call_target="tpu_custom_call" | custom-call | flops 1073741824 | bytes 4194304 | tf_op jit(solution)/shard_map/cond/branch_3_fun/pallas_call | solution.py:237
  44.7 13.0 %branch_3_fun.7 = (f32[16,1,64,256]{3,2,1,0:T(8,128)S(1)}, f32[16,1,2,256]{3,2,1,0:T(2,128)S(1)}) custom-call(s32[8,128]{1,0:T(8,128)S(1)} %get-tuple-element.78.plan_ref, bf16[16,1,128,256]{3,2,1,0:T(8,128)(2,1)S(1)} %get-tuple-element.80.query_ref, f32[16,1,64,256]{3,2,1,0:T(8,128)S(1)} %get-tuple-element.82.acc_in, ...), custom_call_target="tpu_custom_call", output_to_operand_aliasing={{0}: (2, {}), {1}: (3, {})} | custom-call | flops 536870912 | bytes 2097152 | tf_op jit(solution)/shard_map/cond/branch_3_fun/pallas_call | solution.py:321
  57.6 0.1 collective-permute-start.7
  57.7 11.6 %collective-permute-done.6.source_ref = bf16[18,128,128]{2,1,0:T(8,128)(2,1)S(1)} collective-permute-done((bf16[18,128,128]{2,1,0:T(8,128)(2,1)S(1)}, bf16[18,128,128]{2,1,0:T(8,128)(2,1)S(1)}, u32[]{:S(2)}, u32[]{:S(2)}) %collective-permute-start.6) | collective-permute-done | bytes 589856 | tf_op jit(solution)/shard_map/cond/branch_3_fun/ppermute | solution.py:360
  69.3 8.2 %branch_3_fun.8 = (f32[16,1,64,256]{3,2,1,0:T(8,128)S(1)}, f32[16,1,2,256]{3,2,1,0:T(2,128)S(1)}) custom-call(s32[8,128]{1,0:T(8,128)S(1)} %get-tuple-element.78.plan_ref, bf16[16,1,128,256]{3,2,1,0:T(8,128)(2,1)S(1)} %get-tuple-element.80.query_ref, f32[16,1,64,256]{3,2,1,0:T(8,128)S(1)} %get-tuple-element.85.acc_in, ...), custom_call_target="tpu_custom_call", output_to_operand_aliasing={{0}: (2, {}), {1}: (3, {})} | custom-call | flops 536870912 | bytes 2097152 | tf_op jit(solution)/shard_map/cond/branch_3_fun/pallas_call | solution.py:321
  77.5 2.7 %branch_3_fun.9 = (bf16[16,128,128]{2,1,0:T(8,128)(2,1)S(1)}, f32[16,1,64,256]{3,2,1,0:T(8,128)S(1)}, f32[16,1,2,256]{3,2,1,0:T(2,128)S(1)}) custom-call(s32[8,128]{1,0:T(8,128)S(1)} %get-tuple-element.78.plan_ref, bf16[16,1,128,256]{3,2,1,0:T(8,128)(2,1)S(1)} %get-tuple-element.80.query_ref, ...), custom_call_target="tpu_custom_call", output_to_operand_aliasing={{1}: (2, {}), {2}: (3, {})} | custom-call | flops 536870912 | bytes 2097152 | tf_op jit(solution)/shard_map/cond/branch_3_fun/pallas_call | solution.py:321
  80.7 13.3 %all_to_all.10.x_ref = bf16[16,128,128]{2,1,0:T(8,128)(2,1)S(1)} all-to-all(bf16[16,128,128]{2,1,0:T(8,128)(2,1)S(1)} %get-tuple-element.114), channel_id=1, replica_groups={{0,1,2,3,4,5,6,7,8,9,10,11,12,13,14,15},{16,17,18,19,20,21,22,23,24,25,..., dimensions={0} | all-to-all | bytes 1048576 | tf_op jit(solution)/shard_map/all_to_all | solution.py:357
  94.0 1.0 %shard_map.84 = bf16[2,128,1024]{2,1,0:T(8,128)(2,1)} custom-call(bf16[16,128,128]{2,1,0:T(8,128)(2,1)S(1)} %all_to_all.10.x_ref), custom_call_target="tpu_custom_call" | custom-call | tf_op jit(solution)/shard_map/pallas_call | solution.py:409
  (13 shorter events, 0.0 us)
Async XLA Ops:
  0.0 1.0 %copy-start = (bf16[2,128,1024]{2,1,0:T(8,128)(2,1)S(1)}, bf16[2,128,1024]{2,1,0:T(8,128)(2,1)}, u32[]{:S(2)}) copy-start(bf16[2,128,1024]{2,1,0:T(8,128)(2,1)} %q_hbm.1) | copy-start | bytes 1572868
  1.0 1.0 %copy-start.1 = (bf16[2,128,1024]{2,1,0:T(8,128)(2,1)S(1)}, bf16[2,128,1024]{2,1,0:T(8,128)(2,1)}, u32[]{:S(2)}) copy-start(bf16[2,128,1024]{2,1,0:T(8,128)(2,1)} %k_hbm.1) | copy-start | bytes 1572868
  2.1 1.0 %copy-start.2 = (bf16[2,128,1024]{2,1,0:T(8,128)(2,1)S(1)}, bf16[2,128,1024]{2,1,0:T(8,128)(2,1)}, u32[]{:S(2)}) copy-start(bf16[2,128,1024]{2,1,0:T(8,128)(2,1)} %v_hbm.1) | copy-start | bytes 1572868
  4.9 6.5 %copy-start.4 = (s32[32,6]{0,1:T(8,128)S(1)}, s32[32,6]{0,1:T(8,128)}, u32[]{:S(2)}) copy-start(s32[32,6]{0,1:T(8,128)} %param.17) | copy-start | bytes 2308
  4.9 6.6 %copy-start.5 = (s32[32,6]{0,1:T(8,128)S(1)}, s32[32,6]{0,1:T(8,128)}, u32[]{:S(2)}) copy-start(s32[32,6]{0,1:T(8,128)} %param.18) | copy-start | bytes 2308
  4.9 6.7 %copy-start.6 = (s32[32,6]{0,1:T(8,128)S(1)}, s32[32,6]{0,1:T(8,128)}, u32[]{:S(2)}) copy-start(s32[32,6]{0,1:T(8,128)} %param.19) | copy-start | bytes 2308
  5.0 6.8 %copy-start.7 = (s32[32,6]{0,1:T(8,128)S(1)}, s32[32,6]{0,1:T(8,128)}, u32[]{:S(2)}) copy-start(s32[32,6]{0,1:T(8,128)} %param.20) | copy-start | bytes 2308
  5.0 6.8 %copy-start.3 = (s32[4]{0:T(128)S(1)}, s32[4]{0:T(128)}, u32[]{:S(2)}) copy-start(s32[4]{0:T(128)} %ref_ref.1) | copy-start | bytes 52
  5.0 28.6 %all-to-all-start = ((bf16[16,3,128,128]{3,2,1,0:T(8,128)(2,1)}), bf16[16,3,128,128]{3,2,1,0:T(8,128)(2,1)S(1)}, u32[]{:S(2)}, u32[]{:S(2)}) async-start(bf16[16,3,128,128]{3,2,1,0:T(8,128)(2,1)} %shard_map.83), calls=%async_computation | async-start | bytes 3145728 | tf_op jit(solution)/shard_map/all_to_all | solution.py:357
  34.3 35.0 %collective-permute-start.6 = (bf16[18,128,128]{2,1,0:T(8,128)(2,1)S(1)}, bf16[18,128,128]{2,1,0:T(8,128)(2,1)S(1)}, u32[]{:S(2)}, u32[]{:S(2)}) collective-permute-start(bf16[18,128,128]{2,1,0:T(8,128)(2,1)S(1)} %get-tuple-element.87), channel_id=1, source_target_pairs={{0,16},{2,18},{4,20},{6,22},{8,24},{10,26},{12,28},{14,30},{16,0},... | collective-permute-start | bytes 1769480 | tf_op jit(solution)/shard_map/cond/branch_3_fun/ppermute | solution.py:360
  57.6 19.8 %collective-permute-start.7 = (bf16[8,128,128]{2,1,0:T(8,128)(2,1)S(1)}, bf16[8,128,128]{2,1,0:T(8,128)(2,1)S(1)}, u32[]{:S(2)}, u32[]{:S(2)}) collective-permute-start(bf16[8,128,128]{2,1,0:T(8,128)(2,1)S(1)} %get-tuple-element.90), channel_id=1, source_target_pairs={{0,16},{2,18},{4,20},{6,22},{8,24},{10,26},{12,28},{14,30},{16,0},... | collective-permute-start | bytes 786440 | tf_op jit(solution)/shard_map/cond/branch_3_fun/ppermute | solution.py:360

commit v6 on v5

--- a/solution.py
+++ b/solution.py
@@ -16,7 +16,8 @@
 SPAN = 4
 FAR = 1024
 DEAD = 65536
-BATCH = 4
+BATCH_BITS = 2
+BATCH = 1 << BATCH_BITS
 
 STRIDE = FRAMES_DEV + 1
 WHOLE = pl.BlockSpec(memory_space=pltpu.VMEM)
@@ -55,7 +56,7 @@
 
 def plan_kernel(
     me_ref, ref_ref, dev_hbm, place_hbm, block_hbm, valid_hbm, out_ref, entries, sems,
-    *, inner, n_tok, rooms,
+    *, inner, n_tok, flip, rooms,
 ):
     copies = [
         pltpu.make_async_copy(array, entries.at[index], sems.at[index])
@@ -73,7 +74,8 @@
     f32 = jnp.float32
     me = me_ref[0].astype(f32)
     dev = entries[0]
-    ids = (dev // inner) * units + ((dev % inner) * n_tok + entries[2]) * STRIDE + entries[1]
+    spot = (dev % inner + flip * (dev // inner)) % inner
+    ids = (dev // inner) * units + (spot * n_tok + entries[2]) * STRIDE + entries[1]
     used = entries[3] > 0
     frame_lane = lax.broadcasted_iota(jnp.int32, (n_frames, lanes), 1)
     hit = jnp.zeros((n_frames, lanes), f32)
@@ -115,6 +117,10 @@
 
     row_frame = lax.broadcasted_iota(jnp.int32, (n_frames, lanes), 0).astype(f32)
     wide_lane = frame_lane.astype(f32)
+    local_row = row_frame - me * group_frames
+    turned = local_row + me * (flip * FRAMES_DEV)
+    turned = jnp.where(turned >= group_frames, turned - group_frames, turned) * 8
+    turned = jnp.where((local_row >= 0) & (local_row < group_frames), turned, -8.0)
 
     def places(table):
         listed = jnp.zeros((1, lanes), f32)
@@ -122,15 +128,16 @@
             mine, live = ids[:, entry : entry + 1], used[:, entry : entry + 1]
             found = jnp.sum(jnp.where(mine == frame_lane, table, 0.0), axis=1, keepdims=True)
             found = jnp.where(live, found, float(DEAD))
-            target = (row_frame - me * group_frames) * 8 + entry
+            target = turned + entry
             listed += jnp.sum(jnp.where(target == wide_lane, found, 0.0), axis=0, keepdims=True)
         listed = jnp.where(lane % 8 < ENTRIES, listed, float(DEAD))
         refs = jnp.zeros((1, lanes), f32)
         for local in range(max(1, inner // SPAN)):
-            scene = me_ref[0] * inner // SPAN + local
+            scene = me_ref[0] * inner // SPAN + (local * SPAN + flip * me_ref[0]) % inner // SPAN
             ref_frame = scene * (SPAN * FRAMES_DEV) + ref_ref[scene]
             ref_dev = ref_frame // FRAMES_DEV
-            base = (ref_dev // inner) * units + (ref_dev % inner) * n_tok * STRIDE
+            ref_spot = (ref_dev % inner + flip * (ref_dev // inner)) % inner
+            base = (ref_dev // inner) * units + ref_spot * n_tok * STRIDE
             for block in range(n_tok):
                 which = base + block * STRIDE + ref_frame % FRAMES_DEV
                 found = jnp.sum(jnp.where(lane == which, table, 0.0), axis=1, keepdims=True)
@@ -142,13 +149,13 @@
         out_ref[index : index + 1, :] = row.astype(jnp.int32)
 
 
-def make_plan(epi_dev, epi_frame, epi_block, valid, ref_local, my_outer, inner, n_tok, rooms):
+def make_plan(epi_dev, epi_frame, epi_block, valid, ref_local, my_outer, inner, n_tok, flip, rooms):
     n_outer = epi_dev.shape[0] // (inner * FRAMES_DEV)
     n_units = n_outer * inner * n_tok * STRIDE
     lanes = -(-n_units // 128) * 128
     smem, anywhere = pl.BlockSpec(memory_space=pltpu.SMEM), pl.BlockSpec(memory_space=pl.ANY)
     return pl.pallas_call(
-        functools.partial(plan_kernel, inner=inner, n_tok=n_tok, rooms=rooms),
+        functools.partial(plan_kernel, inner=inner, n_tok=n_tok, flip=flip, rooms=rooms),
         out_shape=jax.ShapeDtypeStruct((8, lanes), jnp.int32),
         in_specs=[smem, smem] + [anywhere] * 4,
         out_specs=WHOLE,
@@ -262,19 +269,20 @@
     acc_ref, stat_ref, items = refs[-3:]
     n_local, n_tiles, _, tile = acc_ref.shape
 
-    def list_up(row, per_frame):
-        def one(index, found):
-            code = plan_ref[row, lax.rem(index, per_frame) if row > spot_row else index]
-            items[found] = lax.div(index, per_frame) * DEAD + (code - low)
-            return found + ((code >= low) & (code < high)).astype(jnp.int32)
-
-        return one
-
-    found = lax.fori_loop(0, n_local * 8, list_up(spot_row, 8), jnp.int32(0), unroll=8)
-    if n_refs:
-        found = lax.fori_loop(0, n_local * n_refs, list_up(spot_row + 1, n_refs), found)
-
-    @pl.loop(0, lax.div(found + (BATCH - 1), jnp.int32(BATCH)))
+    def add(found, local, code):
+        items[found] = (local << 16) + (code - low)
+        return found + ((code >= low) & (code < high)).astype(jnp.int32)
+
+    def listed(local, found):
+        for entry in range(ENTRIES):
+            found = add(found, local, plan_ref[spot_row, local * 8 + entry])
+        for block in range(n_refs):
+            found = add(found, local, plan_ref[spot_row + 1, block])
+        return found
+
+    found = lax.fori_loop(0, n_local, listed, jnp.int32(0), unroll=math.gcd(2, n_local))
+
+    @pl.loop(0, (found + (BATCH - 1)) >> BATCH_BITS)
     def _(step):
         for index in range(n_tiles):
             parts = []
@@ -348,8 +356,13 @@
     n_refs = 0 if ref_near else n_tok
     blocks = n_ranks * FRAMES_DEV
     rooms = [-(-blocks * share // 16) for share in (10, 11, 12, 13, 14)] if n_outer == 2 else []
+    flip = inner // 2 if n_outer == 2 and inner % (2 * SPAN) == 0 else 0
+
+    def device(o, spot):
+        return o * inner + (spot + flip * o) % inner
+
     groups = [
-        [(o * inner + i) * n_tok + t for i in range(inner) for t in range(n_tok)]
+        [device(o, i) * n_tok + t for i in range(inner) for t in range(n_tok)]
         for o in range(n_outer)
     ]
 
@@ -357,11 +370,14 @@
         return lax.all_to_all(x, ("tm", "tok"), 0, 0, axis_index_groups=groups, tiled=True)
 
     def turn(x):
-        return lax.ppermute(x, "tm", [(d, (d + inner) % n_tm) for d in range(n_tm)])
+        pairs = [
+            (device(o, i), device((o + 1) % n_outer, i)) for o in range(n_outer) for i in range(inner)
+        ]
+        return lax.ppermute(x, "tm", pairs)
 
     my_outer = (lax.axis_index("tm") // inner).astype(jnp.int32)
     plan = make_plan(
-        epi_dev, epi_frame, epi_block, valid, ref_local, my_outer, inner, n_tok, rooms
+        epi_dev, epi_frame, epi_block, valid, ref_local, my_outer, inner, n_tok, flip, rooms
     )
     small = pltpu.CompilerParams(vmem_limit_bytes=24 * 1024 * 1024)
     own = pl.pallas_call(
@@ -371,30 +387,31 @@
         out_specs=WHOLE,
         scratch_shapes=[pltpu.VMEM(keys.shape, keys.dtype)] * 3 + [pltpu.SemaphoreType.DMA((3,))],
         compiler_params=small,
-    )(queries, keys, values)
+    )(*[pltpu.with_memory_space_constraint(x, pltpu.HBM) for x in (queries, keys, values)])
     own = exchange(own).reshape(units, BLOCK, 2 * HEAD_DIM)
 
-    def attend(own, arrivals, spot_row, waiting=None):
+    def attend(own, arrivals, spot_row, waiting=()):
         query, acc, stat = near(plan, own, inner, n_tok, spot_row, ref_near)
         acc, stat = stage(plan, own, query, acc, stat, 0, n_ranks, spot_row, n_refs, False)
-        if waiting is not None:
-            waiting, acc = lax.optimization_barrier((waiting, acc))
-            arrivals = arrivals + [turn(waiting)]
+        arrivals, waiting = list(arrivals), list(waiting)
         low = FAR
-        for index, arrived in enumerate(arrivals):
-            final = index == len(arrivals) - 1
+        while arrivals:
+            if waiting:
+                held, acc = lax.optimization_barrier((waiting.pop(0), acc))
+                arrivals.append(turn(held))
+            arrived = arrivals.pop(0)
             *result, acc, stat = stage(
-                plan, arrived, query, acc, stat, low, n_ranks, spot_row, n_refs, final
+                plan, arrived, query, acc, stat, low, n_ranks, spot_row, n_refs, not arrivals
             )
             low += arrived.shape[0]
         return result[0]
 
     def listed(room):
-        first = -(-room * 2 // 3)
+        sizes = (room - room // 2, room // 2 - room // 5, room // 5)
 
         def run(own):
-            early, late = pack(plan, own, (first, room - first))
-            return attend(own, [turn(early)], 2, late)
+            first, *later = pack(plan, own, sizes)
+            return attend(own, [turn(first)], 2, later)
 
         return run
 

time: 96.3 us -> 92.3 us (0.958)
  waiting for transfers between devices: 30.6 us -> 21.7 us
  blocking collectives: 13.3 us -> 17.1 us
  local copies, waits for them, and re-layouts: 4.02 us -> 0.89 us
  starting transfers between devices: 9.16 us -> 12.1 us
  Pallas kernels: 36.6 us -> 37.7 us
    ppermute x2 -> x3, waiting for transfers between devices: 11.6 us -> 2.61 us  [turn(): return lax.ppermute(x, 'tm', pairs)]
    all_to_all x1, blocking collectives: 13.3 us -> 17.1 us  [exchange(): lax.all_to_all(x, ('tm', 'tok'), 0, 0, axis_index_groups=groups, tiled=True)]
    unnamed x20 -> x14, local copies, waits for them, and re-layouts: 3.5 us -> 0.38 us
    ppermute x2 -> x3, starting transfers between devices: 2.73 us -> 5.65 us  [turn(): return lax.ppermute(x, 'tm', pairs)]
    pallas_call x1, Pallas kernels: 1.78 us -> 3.04 us  [shards(): pl.pallas_call(split_kernel, out_shape=jax.ShapeDtypeStruct((n_ranks, STR...]
    pallas_call x3 -> x4, Pallas kernels: 23.8 us -> 23.7 us  [stage(): pl.pallas_call(functools.partial(stage_kernel, low=low, high=low + source...]
  transfers between devices with their start and end apart: 3 -> 4, of which waited for: 2 -> 3; matrix products, arithmetic and copies ran while one was open for 1% -> 1% of each run, Pallas kernels for 32% -> 33%
where the time goes in v6:
time: 92.3 us; the launch traced here: 90.5 us
  Pallas kernels  37.7 us (41%)
  waiting for transfers between devices  21.7 us (24%)
  blocking collectives  17.1 us (19%)
  starting transfers between devices  12.1 us (13%)
    pallas_call x4, Pallas kernels, stage(): pl.pallas_call(functools.partial(stage_kernel, low=low, high=low + source...  23.7 us
    all_to_all x1, waiting for transfers between devices, exchange(): lax.all_to_all(x, ('tm', 'tok'), 0, 0, axis_index_groups=groups, tiled=True)  19.1 us
    all_to_all x1, blocking collectives, exchange(): lax.all_to_all(x, ('tm', 'tok'), 0, 0, axis_index_groups=groups, tiled=True)  17.1 us
    pallas_call x1, Pallas kernels, near(): pl.pallas_call(functools.partial(near_kernel, n_tok=n_tok, spot_row=spot_...  7.75 us
    all_to_all x1, starting transfers between devices, exchange(): lax.all_to_all(x, ('tm', 'tok'), 0, 0, axis_index_groups=groups, tiled=True)  6.43 us
    ppermute x3, starting transfers between devices, turn(): return lax.ppermute(x, 'tm', pairs)  5.65 us
    pallas_call x1, Pallas kernels, shards(): pl.pallas_call(split_kernel, out_shape=jax.ShapeDtypeStruct((n_ranks, STR...  3.04 us
    ppermute x3, waiting for transfers between devices, turn(): return lax.ppermute(x, 'tm', pairs)  2.61 us
  transfers between devices with their start and end apart: 4, of which 3 were waited for; matrix products, arithmetic and copies ran while one was open for 1% of the time, Pallas kernels for 33%

profile of v6, /device:TPU:0, one launch (start us, length us, event | category | flops | bytes accessed | tf_op | source)
XLA Modules:
  0.0 90.5 jit_solution(16855258948908177527)
XLA Ops:
  0.0 3.0 %shard_map.83 = bf16[16,3,128,128]{3,2,1,0:T(8,128)(2,1)} custom-call(bf16[2,128,1024]{2,1,0:T(8,128)(2,1)} %q_hbm.1, bf16[2,128,1024]{2,1,0:T(8,128)(2,1)} %k_hbm.1, bf16[2,128,1024]{2,1,0:T(8,128)(2,1)} %v_hbm.1), custom_call_target="tpu_custom_call" | custom-call | tf_op jit(solution)/shard_map/pallas_call | solution.py:383
  3.1 0.0 copy-start.2
  3.1 6.4 %all-to-all-start = ((bf16[16,3,128,128]{3,2,1,0:T(8,128)(2,1)}), bf16[16,3,128,128]{3,2,1,0:T(8,128)(2,1)S(1)}, u32[]{:S(2)}, u32[]{:S(2)}) async-start(bf16[16,3,128,128]{3,2,1,0:T(8,128)(2,1)} %shard_map.83), calls=%async_computation | async-start | bytes 3145728 | tf_op jit(solution)/shard_map/all_to_all | solution.py:370
  9.6 0.1 copy.53.dev_hbm
  9.7 0.1 copy.54.place_hbm
  9.8 0.1 copy.55.block_hbm
  9.8 0.1 copy.56.valid_hbm
  9.9 1.5 %shard_map.82 = s32[8,128]{1,0:T(8,128)S(1)} custom-call(s32[1]{0:T(128)} %bitcast.me_ref, s32[4]{0:T(128)S(1)} %copy-done, s32[32,6]{1,0:T(8,128)S(1)} %copy.53.dev_hbm, s32[32,6]{1,0:T(8,128)S(1)} %copy.54.place_hbm, s32[32,6]{1,0:T(8,128)S(1)} %copy.55.block_hbm, s32[32,6]{1,0:T(8,128)S(1)} %copy.56.valid_hbm), custom_call_target="tpu_custom_call" | custom-call | tf_op jit(solution)/shard_map/pallas_call | solution.py:157
  11.5 0.5 slice.3
  12.6 19.1 %all-to-all-done = bf16[16,3,128,128]{3,2,1,0:T(8,128)(2,1)S(1)} async-done(((bf16[16,3,128,128]{3,2,1,0:T(8,128)(2,1)}), bf16[16,3,128,128]{3,2,1,0:T(8,128)(2,1)S(1)}, u32[]{:S(2)}, u32[]{:S(2)}) %all-to-all-start) | async-done | bytes 1572896 | tf_op jit(solution)/shard_map/all_to_all | solution.py:370
  31.7 40.6 %conditional.1 = (bf16[16,128,128]{2,1,0:T(8,128)(2,1)S(1)}) conditional(s32[]{:T(128)} %bitcast.1, (s32[8,128]{1,0:T(8,128)S(1)}, bf16[48,128,128]{2,1,0:T(8,128)(2,1)S(1)}) %tuple.40, (s32[8,128]{1,0:T(8,128)S(1)}, bf16[48,128,128]{2,1,0:T(8,128)(2,1)S(1)}) %tuple.41, (s32[8,128]{1,0:T(8,128)S(1)}, ...), branch_computations={%region_0.1_spmd, %region_1.2_spmd, %region_2.3_spmd, %region_3.4_... | conditional | flops 3221225472 | bytes 18088064 | solution.py:425
  31.7 0.6 branch_1_fun.7
  32.4 2.7 %collective-permute-start.3 = (bf16[11,128,128]{2,1,0:T(8,128)(2,1)S(1)}, bf16[11,128,128]{2,1,0:T(8,128)(2,1)S(1)}, u32[]{:S(2)}, u32[]{:S(2)}) collective-permute-start(bf16[11,128,128]{2,1,0:T(8,128)(2,1)S(1)} %get-tuple-element.65), channel_id=1, source_target_pairs={{0,24},{2,26},{4,28},{6,30},{8,16},{10,18},{12,20},{14,22},{24,0},... | collective-permute-start | bytes 1081352 | tf_op jit(solution)/shard_map/cond/branch_1_fun/ppermute | solution.py:376
  35.0 7.7 %branch_1_fun.6 = (bf16[16,1,128,256]{3,2,1,0:T(8,128)(2,1)S(1)}, f32[16,1,64,256]{3,2,1,0:T(8,128)S(1)}, f32[16,1,2,256]{3,2,1,0:T(2,128)S(1)}) custom-call(s32[8,128]{1,0:T(8,128)S(1)} %get-tuple-element.55.plan_ref, bf16[48,128,128]{2,1,0:T(8,128)(2,1)S(1)} %get-tuple-element.56.own_ref.source_ref), custom_call_target="tpu_custom_call" | custom-call | flops 1073741824 | bytes 4194304 | tf_op jit(solution)/shard_map/cond/branch_1_fun/pallas_call | solution.py:244
  42.8 9.7 %branch_1_fun.8 = (f32[16,1,64,256]{3,2,1,0:T(8,128)S(1)}, f32[16,1,2,256]{3,2,1,0:T(2,128)S(1)}) custom-call(s32[8,128]{1,0:T(8,128)S(1)} %get-tuple-element.55.plan_ref, bf16[16,1,128,256]{3,2,1,0:T(8,128)(2,1)S(1)} %get-tuple-element.57.query_ref, f32[16,1,64,256]{3,2,1,0:T(8,128)S(1)} %get-tuple-element.60.acc_in, ...), custom_call_target="tpu_custom_call", output_to_operand_aliasing={{0}: (2, {}), {1}: (3, {})} | custom-call | flops 536870912 | bytes 2097152 | tf_op jit(solution)/shard_map/cond/branch_1_fun/pallas_call | solution.py:329
  52.5 2.3 %collective-permute-start.4 = (bf16[7,128,128]{2,1,0:T(8,128)(2,1)S(1)}, bf16[7,128,128]{2,1,0:T(8,128)(2,1)S(1)}, u32[]{:S(2)}, u32[]{:S(2)}) collective-permute-start(bf16[7,128,128]{2,1,0:T(8,128)(2,1)S(1)} %get-tuple-element.69), channel_id=1, source_target_pairs={{0,24},{2,26},{4,28},{6,30},{8,16},{10,18},{12,20},{14,22},{24,0},... | collective-permute-start | bytes 688136 | tf_op jit(solution)/shard_map/cond/branch_1_fun/ppermute | solution.py:376
  54.8 5.9 %branch_1_fun.9 = (f32[16,1,64,256]{3,2,1,0:T(8,128)S(1)}, f32[16,1,2,256]{3,2,1,0:T(2,128)S(1)}) custom-call(s32[8,128]{1,0:T(8,128)S(1)} %get-tuple-element.55.plan_ref, bf16[16,1,128,256]{3,2,1,0:T(8,128)(2,1)S(1)} %get-tuple-element.57.query_ref, f32[16,1,64,256]{3,2,1,0:T(8,128)S(1)} %get-tuple-element.63.acc_in, ...), custom_call_target="tpu_custom_call", output_to_operand_aliasing={{0}: (2, {}), {1}: (3, {})} | custom-call | flops 536870912 | bytes 2097152 | tf_op jit(solution)/shard_map/cond/branch_1_fun/pallas_call | solution.py:329
  60.6 0.7 collective-permute-start.5
  61.4 1.4 %collective-permute-done.4.source_ref = bf16[7,128,128]{2,1,0:T(8,128)(2,1)S(1)} collective-permute-done((bf16[7,128,128]{2,1,0:T(8,128)(2,1)S(1)}, bf16[7,128,128]{2,1,0:T(8,128)(2,1)S(1)}, u32[]{:S(2)}, u32[]{:S(2)}) %collective-permute-start.4) | collective-permute-done | bytes 229408 | tf_op jit(solution)/shard_map/cond/branch_1_fun/ppermute | solution.py:376
  62.7 4.9 %branch_1_fun.10 = (f32[16,1,64,256]{3,2,1,0:T(8,128)S(1)}, f32[16,1,2,256]{3,2,1,0:T(2,128)S(1)}) custom-call(s32[8,128]{1,0:T(8,128)S(1)} %get-tuple-element.55.plan_ref, bf16[16,1,128,256]{3,2,1,0:T(8,128)(2,1)S(1)} %get-tuple-element.57.query_ref, f32[16,1,64,256]{3,2,1,0:T(8,128)S(1)} %get-tuple-element.67.acc_in, ...), custom_call_target="tpu_custom_call", output_to_operand_aliasing={{0}: (2, {}), {1}: (3, {})} | custom-call | flops 536870912 | bytes 2097152 | tf_op jit(solution)/shard_map/cond/branch_1_fun/pallas_call | solution.py:329
  67.7 1.3 %collective-permute-done.5.source_ref = bf16[4,128,128]{2,1,0:T(8,128)(2,1)S(1)} collective-permute-done((bf16[4,128,128]{2,1,0:T(8,128)(2,1)S(1)}, bf16[4,128,128]{2,1,0:T(8,128)(2,1)S(1)}, u32[]{:S(2)}, u32[]{:S(2)}) %collective-permute-start.5) | collective-permute-done | bytes 131104 | tf_op jit(solution)/shard_map/cond/branch_1_fun/ppermute | solution.py:376
  68.9 3.3 %branch_1_fun.11 = (bf16[16,128,128]{2,1,0:T(8,128)(2,1)S(1)}, f32[16,1,64,256]{3,2,1,0:T(8,128)S(1)}, f32[16,1,2,256]{3,2,1,0:T(2,128)S(1)}) custom-call(s32[8,128]{1,0:T(8,128)S(1)} %get-tuple-element.55.plan_ref, bf16[16,1,128,256]{3,2,1,0:T(8,128)(2,1)S(1)} %get-tuple-element.57.query_ref, ...), custom_call_target="tpu_custom_call", output_to_operand_aliasing={{1}: (2, {}), {2}: (3, {})} | custom-call | flops 536870912 | bytes 2097152 | tf_op jit(solution)/shard_map/cond/branch_1_fun/pallas_call | solution.py:329
  72.4 17.1 %all_to_all.10.x_ref = bf16[16,128,128]{2,1,0:T(8,128)(2,1)S(1)} all-to-all(bf16[16,128,128]{2,1,0:T(8,128)(2,1)S(1)} %get-tuple-element.139), channel_id=1, replica_groups={{0,1,2,3,4,5,6,7,8,9,10,11,12,13,14,15},{24,25,26,27,28,29,30,31,16,17,..., dimensions={0} | all-to-all | bytes 1048576 | tf_op jit(solution)/shard_map/all_to_all | solution.py:370
  89.4 1.0 %shard_map.84 = bf16[2,128,1024]{2,1,0:T(8,128)(2,1)} custom-call(bf16[16,128,128]{2,1,0:T(8,128)(2,1)S(1)} %all_to_all.10.x_ref), custom_call_target="tpu_custom_call" | custom-call | tf_op jit(solution)/shard_map/pallas_call | solution.py:426
  (10 shorter events, 0.0 us)
Async XLA Ops:
  3.0 6.5 %copy-start.1 = (s32[32,6]{0,1:T(8,128)S(1)}, s32[32,6]{0,1:T(8,128)}, u32[]{:S(2)}) copy-start(s32[32,6]{0,1:T(8,128)} %param.17) | copy-start | bytes 2308
  3.1 6.6 %copy-start.2 = (s32[32,6]{0,1:T(8,128)S(1)}, s32[32,6]{0,1:T(8,128)}, u32[]{:S(2)}) copy-start(s32[32,6]{0,1:T(8,128)} %param.18) | copy-start | bytes 2308
  3.1 6.7 %copy-start.3 = (s32[32,6]{0,1:T(8,128)S(1)}, s32[32,6]{0,1:T(8,128)}, u32[]{:S(2)}) copy-start(s32[32,6]{0,1:T(8,128)} %param.19) | copy-start | bytes 2308
  3.1 6.8 %copy-start.4 = (s32[32,6]{0,1:T(8,128)S(1)}, s32[32,6]{0,1:T(8,128)}, u32[]{:S(2)}) copy-start(s32[32,6]{0,1:T(8,128)} %param.20) | copy-start | bytes 2308
  3.1 6.8 %copy-start = (s32[4]{0:T(128)S(1)}, s32[4]{0:T(128)}, u32[]{:S(2)}) copy-start(s32[4]{0:T(128)} %ref_ref.1) | copy-start | bytes 52
  3.1 28.6 %all-to-all-start = ((bf16[16,3,128,128]{3,2,1,0:T(8,128)(2,1)}), bf16[16,3,128,128]{3,2,1,0:T(8,128)(2,1)S(1)}, u32[]{:S(2)}, u32[]{:S(2)}) async-start(bf16[16,3,128,128]{3,2,1,0:T(8,128)(2,1)} %shard_map.83), calls=%async_computation | async-start | bytes 3145728 | tf_op jit(solution)/shard_map/all_to_all | solution.py:370
  32.4 22.4 %collective-permute-start.3 = (bf16[11,128,128]{2,1,0:T(8,128)(2,1)S(1)}, bf16[11,128,128]{2,1,0:T(8,128)(2,1)S(1)}, u32[]{:S(2)}, u32[]{:S(2)}) collective-permute-start(bf16[11,128,128]{2,1,0:T(8,128)(2,1)S(1)} %get-tuple-element.65), channel_id=1, source_target_pairs={{0,24},{2,26},{4,28},{6,30},{8,16},{10,18},{12,20},{14,22},{24,0},... | collective-permute-start | bytes 1081352 | tf_op jit(solution)/shard_map/cond/branch_1_fun/ppermute | solution.py:376
  52.5 10.2 %collective-permute-start.4 = (bf16[7,128,128]{2,1,0:T(8,128)(2,1)S(1)}, bf16[7,128,128]{2,1,0:T(8,128)(2,1)S(1)}, u32[]{:S(2)}, u32[]{:S(2)}) collective-permute-start(bf16[7,128,128]{2,1,0:T(8,128)(2,1)S(1)} %get-tuple-element.69), channel_id=1, source_target_pairs={{0,24},{2,26},{4,28},{6,30},{8,16},{10,18},{12,20},{14,22},{24,0},... | collective-permute-start | bytes 688136 | tf_op jit(solution)/shard_map/cond/branch_1_fun/ppermute | solution.py:376
  60.6 8.3 %collective-permute-start.5 = (bf16[4,128,128]{2,1,0:T(8,128)(2,1)S(1)}, bf16[4,128,128]{2,1,0:T(8,128)(2,1)S(1)}, u32[]{:S(2)}, u32[]{:S(2)}) collective-permute-start(bf16[4,128,128]{2,1,0:T(8,128)(2,1)S(1)} %get-tuple-element.72), channel_id=1, source_target_pairs={{0,24},{2,26},{4,28},{6,30},{8,16},{10,18},{12,20},{14,22},{24,0},... | collective-permute-start | bytes 393224 | tf_op jit(solution)/shard_map/cond/branch_1_fun/ppermute | solution.py:376

commit v7 on v6

--- a/solution.py
+++ b/solution.py
@@ -32,17 +32,19 @@
     ]
     for copy in copies:
         copy.start()
-    for copy in copies:
+    copies[0].wait()
+    lanes_of = [slice(rank * HEAD_DIM, (rank + 1) * HEAD_DIM) for rank in range(out_ref.shape[0])]
+    for rank, lanes in enumerate(lanes_of):
+        out_ref[rank, FRAMES_DEV] = jnp.concatenate(
+            [q_ref[frame, :, lanes] for frame in range(FRAMES_DEV)], 1
+        )
+    for copy in copies[1:]:
         copy.wait()
-    for rank in range(out_ref.shape[0]):
-        lanes = slice(rank * HEAD_DIM, (rank + 1) * HEAD_DIM)
+    for rank, lanes in enumerate(lanes_of):
         for frame in range(FRAMES_DEV):
             out_ref[rank, frame] = jnp.concatenate(
                 [k_ref[frame, :, lanes], v_ref[frame, :, lanes]], 1
             )
-        out_ref[rank, FRAMES_DEV] = jnp.concatenate(
-            [q_ref[frame, :, lanes] for frame in range(FRAMES_DEV)], 1
-        )
 
 
 def merge_kernel(x_ref, out_ref):
@@ -355,7 +357,7 @@
     ref_near = inner % SPAN == 0
     n_refs = 0 if ref_near else n_tok
     blocks = n_ranks * FRAMES_DEV
-    rooms = [-(-blocks * share // 16) for share in (10, 11, 12, 13, 14)] if n_outer == 2 else []
+    rooms = [-(-blocks * share // 32) for share in (*range(19, 27), 28)] if n_outer == 2 else []
     flip = inner // 2 if n_outer == 2 and inner % (2 * SPAN) == 0 else 0
 
     def device(o, spot):
@@ -407,7 +409,7 @@
         return result[0]
 
     def listed(room):
-        sizes = (room - room // 2, room // 2 - room // 5, room // 5)
+        sizes = (room - room * 2 // 5, room * 2 // 5)
 
         def run(own):
             first, *later = pack(plan, own, sizes)

time: 92.3 us -> 89.6 us (0.971)
  waiting for transfers between devices: 21.7 us -> 24.5 us
  starting transfers between devices: 12.1 us -> 9.42 us
  Pallas kernels: 37.7 us -> 35.5 us
    ppermute x3 -> x2, waiting for transfers between devices: 2.61 us -> 5.42 us  [turn(): return lax.ppermute(x, 'tm', pairs)]
    ppermute x3 -> x2, starting transfers between devices: 5.65 us -> 2.99 us  [turn(): return lax.ppermute(x, 'tm', pairs)]
    pallas_call x4 -> x3, Pallas kernels: 23.7 us -> 21.7 us  [stage(): pl.pallas_call(functools.partial(stage_kernel, low=low, high=low + source...]
  transfers between devices with their start and end apart: 4 -> 3, of which waited for: 3 -> 2; matrix products, arithmetic and copies ran while one was open for 1% -> 1% of each run, Pallas kernels for 33% -> 28%
where the time goes in v7:
time: 89.6 us; the launch traced here: 88.1 us
  Pallas kernels  35.5 us (40%)
  waiting for transfers between devices  24.5 us (27%)
  blocking collectives  16.7 us (19%)
  starting transfers between devices  9.42 us (11%)
    pallas_call x3, Pallas kernels, stage(): pl.pallas_call(functools.partial(stage_kernel, low=low, high=low + source...  21.7 us
    all_to_all x1, waiting for transfers between devices, exchange(): lax.all_to_all(x, ('tm', 'tok'), 0, 0, axis_index_groups=groups, tiled=True)  19.1 us
    all_to_all x1, blocking collectives, exchange(): lax.all_to_all(x, ('tm', 'tok'), 0, 0, axis_index_groups=groups, tiled=True)  16.7 us
    pallas_call x1, Pallas kernels, near(): pl.pallas_call(functools.partial(near_kernel, n_tok=n_tok, spot_row=spot_...  7.75 us
    all_to_all x1, starting transfers between devices, exchange(): lax.all_to_all(x, ('tm', 'tok'), 0, 0, axis_index_groups=groups, tiled=True)  6.43 us
    ppermute x2, waiting for transfers between devices, turn(): return lax.ppermute(x, 'tm', pairs)  5.42 us
    ppermute x2, starting transfers between devices, turn(): return lax.ppermute(x, 'tm', pairs)  2.99 us
    pallas_call x1, Pallas kernels, shards(): pl.pallas_call(split_kernel, out_shape=jax.ShapeDtypeStruct((n_ranks, STR...  2.86 us
  transfers between devices with their start and end apart: 3, of which 2 were waited for; matrix products, arithmetic and copies ran while one was open for 1% of the time, Pallas kernels for 28%

profile of v7, /device:TPU:0, one launch (start us, length us, event | category | flops | bytes accessed | tf_op | source)
XLA Modules:
  0.0 88.1 jit_solution(5560985657775518119)
XLA Ops:
  0.0 2.9 %shard_map.83 = bf16[16,3,128,128]{3,2,1,0:T(8,128)(2,1)} custom-call(bf16[2,128,1024]{2,1,0:T(8,128)(2,1)} %q_hbm.1, bf16[2,128,1024]{2,1,0:T(8,128)(2,1)} %k_hbm.1, bf16[2,128,1024]{2,1,0:T(8,128)(2,1)} %v_hbm.1), custom_call_target="tpu_custom_call" | custom-call | tf_op jit(solution)/shard_map/pallas_call | solution.py:385
  2.9 0.0 copy-start.1
  2.9 0.0 copy-start.2
  2.9 0.0 copy-start.4
  2.9 0.0 copy-start
  2.9 6.4 %all-to-all-start = ((bf16[16,3,128,128]{3,2,1,0:T(8,128)(2,1)}), bf16[16,3,128,128]{3,2,1,0:T(8,128)(2,1)S(1)}, u32[]{:S(2)}, u32[]{:S(2)}) async-start(bf16[16,3,128,128]{3,2,1,0:T(8,128)(2,1)} %shard_map.83), calls=%async_computation | async-start | bytes 3145728 | tf_op jit(solution)/shard_map/all_to_all | solution.py:372
  9.4 0.1 copy.67.dev_hbm
  9.5 0.1 copy.68.place_hbm
  9.6 0.1 copy.69.block_hbm
  9.7 0.1 copy.70.valid_hbm
  9.8 1.5 %shard_map.82 = s32[8,128]{1,0:T(8,128)S(1)} custom-call(s32[1]{0:T(128)} %bitcast.me_ref, s32[4]{0:T(128)S(1)} %copy-done, s32[32,6]{1,0:T(8,128)S(1)} %copy.67.dev_hbm, s32[32,6]{1,0:T(8,128)S(1)} %copy.68.place_hbm, s32[32,6]{1,0:T(8,128)S(1)} %copy.69.block_hbm, s32[32,6]{1,0:T(8,128)S(1)} %copy.70.valid_hbm), custom_call_target="tpu_custom_call" | custom-call | tf_op jit(solution)/shard_map/pallas_call | solution.py:159
  11.3 0.5 slice.3
  12.5 19.1 %all-to-all-done = bf16[16,3,128,128]{3,2,1,0:T(8,128)(2,1)S(1)} async-done(((bf16[16,3,128,128]{3,2,1,0:T(8,128)(2,1)}), bf16[16,3,128,128]{3,2,1,0:T(8,128)(2,1)S(1)}, u32[]{:S(2)}, u32[]{:S(2)}) %all-to-all-start) | async-done | bytes 1572896 | tf_op jit(solution)/shard_map/all_to_all | solution.py:372
  31.5 38.8 %conditional.1 = (bf16[16,128,128]{2,1,0:T(8,128)(2,1)S(1)}) conditional(s32[]{:T(128)} %bitcast.1, (s32[8,128]{1,0:T(8,128)S(1)}, bf16[48,128,128]{2,1,0:T(8,128)(2,1)S(1)}) %tuple.55, (s32[8,128]{1,0:T(8,128)S(1)}, bf16[48,128,128]{2,1,0:T(8,128)(2,1)S(1)}) %tuple.56, (s32[8,128]{1,0:T(8,128)S(1)}, ...), branch_computations={%region_0.1_spmd, %region_1.2_spmd, %region_2.3_spmd, %region_3.4_... | conditional | flops 2684354560 | bytes 15990872 | solution.py:427
  31.6 0.7 branch_4_fun.6
  32.2 2.7 %collective-permute-start.8 = (bf16[14,128,128]{2,1,0:T(8,128)(2,1)S(1)}, bf16[14,128,128]{2,1,0:T(8,128)(2,1)S(1)}, u32[]{:S(2)}, u32[]{:S(2)}) collective-permute-start(bf16[14,128,128]{2,1,0:T(8,128)(2,1)S(1)} %get-tuple-element.121), channel_id=1, source_target_pairs={{0,24},{2,26},{4,28},{6,30},{8,16},{10,18},{12,20},{14,22},{24,0},... | collective-permute-start | bytes 1376264 | tf_op jit(solution)/shard_map/cond/branch_4_fun/ppermute | solution.py:378
  34.9 7.8 %branch_4_fun.5 = (bf16[16,1,128,256]{3,2,1,0:T(8,128)(2,1)S(1)}, f32[16,1,64,256]{3,2,1,0:T(8,128)S(1)}, f32[16,1,2,256]{3,2,1,0:T(2,128)S(1)}) custom-call(s32[8,128]{1,0:T(8,128)S(1)} %get-tuple-element.112.plan_ref, bf16[48,128,128]{2,1,0:T(8,128)(2,1)S(1)} %get-tuple-element.113.own_ref.source_ref), custom_call_target="tpu_custom_call" | custom-call | flops 1073741824 | bytes 4194304 | tf_op jit(solution)/shard_map/cond/branch_4_fun/pallas_call | solution.py:246
  42.6 9.7 %branch_4_fun.7 = (f32[16,1,64,256]{3,2,1,0:T(8,128)S(1)}, f32[16,1,2,256]{3,2,1,0:T(2,128)S(1)}) custom-call(s32[8,128]{1,0:T(8,128)S(1)} %get-tuple-element.112.plan_ref, bf16[16,1,128,256]{3,2,1,0:T(8,128)(2,1)S(1)} %get-tuple-element.114.query_ref, ...), custom_call_target="tpu_custom_call", output_to_operand_aliasing={{0}: (2, {}), {1}: (3, {})} | custom-call | flops 536870912 | bytes 2097152 | tf_op jit(solution)/shard_map/cond/branch_4_fun/pallas_call | solution.py:331
  52.3 0.3 collective-permute-start.9
  52.7 5.9 %branch_4_fun.8 = (f32[16,1,64,256]{3,2,1,0:T(8,128)S(1)}, f32[16,1,2,256]{3,2,1,0:T(2,128)S(1)}) custom-call(s32[8,128]{1,0:T(8,128)S(1)} %get-tuple-element.112.plan_ref, bf16[16,1,128,256]{3,2,1,0:T(8,128)(2,1)S(1)} %get-tuple-element.114.query_ref, ...), custom_call_target="tpu_custom_call", output_to_operand_aliasing={{0}: (2, {}), {1}: (3, {})} | custom-call | flops 536870912 | bytes 2097152 | tf_op jit(solution)/shard_map/cond/branch_4_fun/pallas_call | solution.py:331
  58.5 5.4 %collective-permute-done.9.source_ref = bf16[9,128,128]{2,1,0:T(8,128)(2,1)S(1)} collective-permute-done((bf16[9,128,128]{2,1,0:T(8,128)(2,1)S(1)}, bf16[9,128,128]{2,1,0:T(8,128)(2,1)S(1)}, u32[]{:S(2)}, u32[]{:S(2)}) %collective-permute-start.9) | collective-permute-done | bytes 294944 | tf_op jit(solution)/shard_map/cond/branch_4_fun/ppermute | solution.py:378
  64.0 6.1 %branch_4_fun.9 = (bf16[16,128,128]{2,1,0:T(8,128)(2,1)S(1)}, f32[16,1,64,256]{3,2,1,0:T(8,128)S(1)}, f32[16,1,2,256]{3,2,1,0:T(2,128)S(1)}) custom-call(s32[8,128]{1,0:T(8,128)S(1)} %get-tuple-element.112.plan_ref, bf16[16,1,128,256]{3,2,1,0:T(8,128)(2,1)S(1)} %get-tuple-element.114.query_ref, ...), custom_call_target="tpu_custom_call", output_to_operand_aliasing={{1}: (2, {}), {2}: (3, {})} | custom-call | flops 536870912 | bytes 2097152 | tf_op jit(solution)/shard_map/cond/branch_4_fun/pallas_call | solution.py:331
  70.3 16.7 %all_to_all.10.x_ref = bf16[16,128,128]{2,1,0:T(8,128)(2,1)S(1)} all-to-all(bf16[16,128,128]{2,1,0:T(8,128)(2,1)S(1)} %get-tuple-element.190), channel_id=1, replica_groups={{0,1,2,3,4,5,6,7,8,9,10,11,12,13,14,15},{24,25,26,27,28,29,30,31,16,17,..., dimensions={0} | all-to-all | bytes 1048576 | tf_op jit(solution)/shard_map/all_to_all | solution.py:372
  87.1 1.0 %shard_map.84 = bf16[2,128,1024]{2,1,0:T(8,128)(2,1)} custom-call(bf16[16,128,128]{2,1,0:T(8,128)(2,1)S(1)} %all_to_all.10.x_ref), custom_call_target="tpu_custom_call" | custom-call | tf_op jit(solution)/shard_map/pallas_call | solution.py:428
  (7 shorter events, 0.0 us)
Async XLA Ops:
  2.9 6.5 %copy-start.1 = (s32[32,6]{0,1:T(8,128)S(1)}, s32[32,6]{0,1:T(8,128)}, u32[]{:S(2)}) copy-start(s32[32,6]{0,1:T(8,128)} %param.21) | copy-start | bytes 2308
  2.9 6.6 %copy-start.2 = (s32[32,6]{0,1:T(8,128)S(1)}, s32[32,6]{0,1:T(8,128)}, u32[]{:S(2)}) copy-start(s32[32,6]{0,1:T(8,128)} %param.22) | copy-start | bytes 2308
  2.9 6.7 %copy-start.3 = (s32[32,6]{0,1:T(8,128)S(1)}, s32[32,6]{0,1:T(8,128)}, u32[]{:S(2)}) copy-start(s32[32,6]{0,1:T(8,128)} %param.23) | copy-start | bytes 2308
  2.9 6.8 %copy-start.4 = (s32[32,6]{0,1:T(8,128)S(1)}, s32[32,6]{0,1:T(8,128)}, u32[]{:S(2)}) copy-start(s32[32,6]{0,1:T(8,128)} %param.24) | copy-start | bytes 2308
  2.9 6.8 %copy-start = (s32[4]{0:T(128)S(1)}, s32[4]{0:T(128)}, u32[]{:S(2)}) copy-start(s32[4]{0:T(128)} %ref_ref.1) | copy-start | bytes 52
  2.9 28.6 %all-to-all-start = ((bf16[16,3,128,128]{3,2,1,0:T(8,128)(2,1)}), bf16[16,3,128,128]{3,2,1,0:T(8,128)(2,1)S(1)}, u32[]{:S(2)}, u32[]{:S(2)}) async-start(bf16[16,3,128,128]{3,2,1,0:T(8,128)(2,1)} %shard_map.83), calls=%async_computation | async-start | bytes 3145728 | tf_op jit(solution)/shard_map/all_to_all | solution.py:372
  32.2 20.5 %collective-permute-start.8 = (bf16[14,128,128]{2,1,0:T(8,128)(2,1)S(1)}, bf16[14,128,128]{2,1,0:T(8,128)(2,1)S(1)}, u32[]{:S(2)}, u32[]{:S(2)}) collective-permute-start(bf16[14,128,128]{2,1,0:T(8,128)(2,1)S(1)} %get-tuple-element.121), channel_id=1, source_target_pairs={{0,24},{2,26},{4,28},{6,30},{8,16},{10,18},{12,20},{14,22},{24,0},... | collective-permute-start | bytes 1376264 | tf_op jit(solution)/shard_map/cond/branch_4_fun/ppermute | solution.py:378
  52.3 11.6 %collective-permute-start.9 = (bf16[9,128,128]{2,1,0:T(8,128)(2,1)S(1)}, bf16[9,128,128]{2,1,0:T(8,128)(2,1)S(1)}, u32[]{:S(2)}, u32[]{:S(2)}) collective-permute-start(bf16[9,128,128]{2,1,0:T(8,128)(2,1)S(1)} %get-tuple-element.124), channel_id=1, source_target_pairs={{0,24},{2,26},{4,28},{6,30},{8,16},{10,18},{12,20},{14,22},{24,0},... | collective-permute-start | bytes 884744 | tf_op jit(solution)/shard_map/cond/branch_4_fun/ppermute | solution.py:378
